TPU v7x, 32 devices: a whole 2x2x4 slice. The times are simulated.
32 devices in a mesh: shots: 2 (over y), gx: 4 (over z), gy: 2 (over x), gz: 2 (over core).
Axes of the slice: x: 2, y: 2, z: 4, core: 2. Of those that a mesh axis runs over, the one named last changes fastest.
Arguments:
- forward_prev: float32 [64, 128, 256], P(('shots', 'gx'), 'gy', 'gz'), parts along dimension 0, may hold values from -1.8 to 1.8
- forward_now: float32 [64, 128, 256], P(('shots', 'gx'), 'gy', 'gz'), parts along dimension 0, may hold values from -1.8 to 1.8
- adjoint_prev: float32 [64, 128, 256], P(('shots', 'gx'), 'gy', 'gz'), parts along dimension 0, may hold values from -1.8 to 1.8
- adjoint_now: float32 [64, 128, 256], P(('shots', 'gx'), 'gy', 'gz'), parts along dimension 0, may hold values from -1.8 to 1.8
- model_table: float32 [2, 8192, 2, 128], P('gz', ('gx', 'gy')), may hold values from 0 to 0.3, as said below
- tile_owner: int32 [4, 4, 2, 512, 1], P(('shots', 'gz'), 'gx', 'gy'), parts along dimension 0, may hold values from 0 to 7; in each aligned block of 512 rows (0 to 511, 512 to 1023, ..., all dimensions but the last counted through in order) at most 128 rows name the same one
- tile_slot: int32 [4, 4, 2, 512], P(('shots', 'gz'), 'gx', 'gy'), parts along dimension 0, may hold values from 0 to 1023
- source_index: int32 [6], P('shots'), parts along dimension 0, may hold values from 0 to 31
- wavelet: float32 [32], P('shots'), parts along dimension 0, may hold values from -6 to 6
- receiver_depth: int32 [64, 128], P(('shots', 'gx'), 'gy'), parts along dimension 0, may hold values from 0 to 127
- traces: float32 [16, 64, 128], P(None, ('shots', 'gx'), 'gy'), parts along dimension 1, may hold values from -6 to 6
Outputs:
- forward_final: float32 [64, 128, 256], P(('shots', 'gx'), 'gy', 'gz'), parts along dimension 0
- adjoint_final: float32 [64, 128, 256], P(('shots', 'gx'), 'gy', 'gz'), parts along dimension 0
- model_gradient: float32 [2, 16384, 2, 128], P('gz', ('shots', 'gx', 'gy')), parts along dimension 1
There are 2 independent parts, one for each index of `shots`. A program takes and returns all parts, laid end to end along the dimension named above; an argument that names none is the same for every part. Nothing has to cross between parts.
Inputs may be any that keep to these rules, and one draw needn't show every extreme that they name: `tile_owner`: among the 512 columns of one device's block, no owner is named more than 128 times, and in every draw some owner is named exactly 128 times by some block. `model_table`: component 0 lies in 0.04 to 0.14, component 1 in 0 to 0.3.
All inputs are finite; a program needn't handle non-finite values.
Results may differ from a plain program's by a relative error of at most 0.0003.
Values sent between devices are 32-bit elements; how exact they have to be, the bound alone decides.
No kernel may reach another device: no remote copies, remote signals or barrier semaphores. Data moves between devices by JAX's collectives and lax.ppermute only.
A program may use at most 64 MiB of HBM per device.

v0:
```python
import jax
import jax.numpy as jnp
from jax import lax
from jax.sharding import PartitionSpec as P

STENCIL = (-205.0 / 72.0, 8.0 / 5.0, -1.0 / 5.0, 8.0 / 315.0, -1.0 / 560.0)


def with_halo(block, sides, width):
    for axis, dim in sides:
        count = lax.axis_size(axis)
        forward = [(i, i + 1) for i in range(count - 1)]
        backward = [(target, source) for source, target in forward]
        low = lax.ppermute(
            lax.slice_in_dim(block, block.shape[dim] - width, None, axis=dim), axis, forward
        )
        high = lax.ppermute(lax.slice_in_dim(block, 0, width, axis=dim), axis, backward)
        block = jnp.concatenate([low, block, high], axis=dim)
    return block


def derivatives(padded, shape):
    size_x, size_y, size_z = shape

    def window(off_x, off_y, off_z):
        return padded[
            4 + off_x : 4 + off_x + size_x,
            4 + off_y : 4 + off_y + size_y,
            4 + off_z : 4 + off_z + size_z,
        ]

    center = window(0, 0, 0)
    along_x = STENCIL[0] * center
    along_y = STENCIL[0] * center
    along_z = STENCIL[0] * center
    for offset in range(1, 5):
        along_x = along_x + STENCIL[offset] * (window(offset, 0, 0) + window(-offset, 0, 0))
        along_y = along_y + STENCIL[offset] * (window(0, offset, 0) + window(0, -offset, 0))
        along_z = along_z + STENCIL[offset] * (window(0, 0, offset) + window(0, 0, -offset))
    return (along_x + along_y, along_z)


def propagate(previous, current, slow_coef, aniso_coef, padded):
    horizontal, vertical = derivatives(padded, current.shape)
    laplacian = (1.0 + 2.0 * aniso_coef) * horizontal + vertical
    following = 2.0 * current - previous + slow_coef * laplacian
    return (following, laplacian, horizontal)


def body(
    forward_prev,
    forward_now,
    adjoint_prev,
    adjoint_now,
    model_table,
    tile_owner,
    tile_slot,
    source_index,
    wavelet,
    receiver_depth,
    traces,
):
    block_x, block_y, block_z = forward_now.shape
    columns = block_x * block_y
    owners_count = lax.axis_size(("gx", "gy"))
    capacity = max(2, 2 * columns // owners_count)
    column_owner = tile_owner.reshape(columns)
    column_slot = tile_slot.reshape(columns)
    local_table = model_table[0]
    held_count = local_table.shape[0]
    one_hot = (column_owner[:, None] == jnp.arange(owners_count, dtype=jnp.int32)[None, :]).astype(
        jnp.float32
    )
    earlier = (
        jnp.arange(columns, dtype=jnp.int32)[:, None]
        > jnp.arange(columns, dtype=jnp.int32)[None, :]
    ).astype(jnp.float32)
    counted_before = jnp.dot(earlier, one_hot, precision=lax.Precision.HIGHEST)
    slot_rank = jnp.sum(counted_before * one_hot, axis=1).astype(jnp.int32)
    requests = (
        jnp.full((owners_count, capacity), -1, jnp.int32)
        .at[column_owner, slot_rank]
        .set(column_slot)
    )
    received = lax.all_to_all(requests, ("gx", "gy"), split_axis=0, concat_axis=0, tiled=True)
    clipped = jnp.clip(received, 0, held_count - 1)
    fetched = lax.all_to_all(
        local_table[clipped], ("gx", "gy"), split_axis=0, concat_axis=0, tiled=True
    )
    cell_params = (
        fetched[column_owner, slot_rank].reshape(block_x, block_y, 2, block_z).transpose(2, 0, 1, 3)
    )
    slow_coef = cell_params[0]
    aniso_coef = cell_params[1]
    grid_x = lax.axis_index("gx") * block_x + jnp.arange(block_x, dtype=jnp.int32)[:, None, None]
    grid_y = lax.axis_index("gy") * block_y + jnp.arange(block_y, dtype=jnp.int32)[None, :, None]
    grid_z = lax.axis_index("gz") * block_z + jnp.arange(block_z, dtype=jnp.int32)[None, None, :]
    source_mask = (
        (grid_x == source_index[0]) & (grid_y == source_index[1]) & (grid_z == source_index[2])
    ).astype(jnp.float32)
    receiver_mask = (grid_z == receiver_depth[:, :, None]).astype(jnp.float32)

    def forward(carried, weight):
        previous, current = carried
        padded = with_halo(current, (("gx", 0), ("gy", 1), ("gz", 2)), 4)
        following, laplacian, horizontal = propagate(
            previous, current, slow_coef, aniso_coef, padded
        )
        following = following + weight * source_mask
        return ((current, following), (laplacian, horizontal))

    (_, forward_final), (laplacians, horizontals) = lax.scan(
        forward, (forward_prev, forward_now), wavelet
    )

    def backward(carried, inputs):
        previous, current, grad_slow, grad_aniso = carried
        trace_row, laplacian, horizontal = inputs
        padded = with_halo(current, (("gx", 0), ("gy", 1), ("gz", 2)), 4)
        following, _, _ = propagate(previous, current, slow_coef, aniso_coef, padded)
        following = following + trace_row[:, :, None] * receiver_mask
        grad_slow = grad_slow + following * laplacian
        grad_aniso = grad_aniso + following * (2.0 * slow_coef * horizontal)
        return ((current, following, grad_slow, grad_aniso), None)

    zero_field = jnp.zeros((block_x, block_y, block_z), jnp.float32)
    (_, adjoint_final, grad_slow, grad_aniso), _ = lax.scan(
        backward,
        (adjoint_prev, adjoint_now, zero_field, zero_field),
        (traces[::-1], laplacians[::-1], horizontals[::-1]),
    )
    grad_cells = (
        jnp.stack([grad_slow, grad_aniso]).transpose(1, 2, 0, 3).reshape(columns, 2, block_z)
    )
    outgoing = (
        jnp.zeros((owners_count, capacity, 2, block_z), jnp.float32)
        .at[column_owner, slot_rank]
        .set(grad_cells)
    )
    returned = lax.all_to_all(outgoing, ("gx", "gy"), split_axis=0, concat_axis=0, tiled=True)
    target = jnp.where(received < 0, held_count, received).reshape(owners_count * capacity)
    model_gradient = (
        jnp.zeros((held_count, 2, block_z), jnp.float32)
        .at[target]
        .add(returned.reshape(owners_count * capacity, 2, block_z), mode="drop")
    )
    return (forward_final, adjoint_final, model_gradient[None])


def solution(mesh):
    in_specs = (
        P(("shots", "gx"), "gy", "gz"),
        P(("shots", "gx"), "gy", "gz"),
        P(("shots", "gx"), "gy", "gz"),
        P(("shots", "gx"), "gy", "gz"),
        P("gz", ("gx", "gy"), None, None),
        P(("shots", "gz"), "gx", "gy", None, None),
        P(("shots", "gz"), "gx", "gy", None),
        P("shots"),
        P("shots"),
        P(("shots", "gx"), "gy"),
        P(None, ("shots", "gx"), "gy"),
    )
    out_specs = (
        P(("shots", "gx"), "gy", "gz"),
        P(("shots", "gx"), "gy", "gz"),
        P("gz", ("shots", "gx", "gy"), None, None),
    )
    return jax.shard_map(body, mesh=mesh, in_specs=in_specs, out_specs=out_specs, check_vma=False)
```

profile of v0, /device:TPU:1, one launch (start us, length us, event | category | flops | bytes accessed | tf_op | source)
XLA Modules:
  0.0 1330.6 jit_solution(18363129317404440637)
XLA Ops:
  2.5 42.4 %scatter_fusion = s32[8,128]{1,0:T(8,128)S(1)} fusion(s32[8,128]{1,0:T(8,128)S(1)} %broadcast_in_dim.18, s32[512]{0:T(512)S(1)} %bitcast.76, s32[512]{0:T(512)} %bitcast.87), kind=kCustom, calls=%fused_computation.2 | custom fusion | bytes 10240 | tf_op jit(solution)/shard_map/scatter | solution.py:83
  44.9 11.6 all_to_all.22
  56.6 7.5 gather_fusion
  76.2 15.2 %all-to-all-done.1 = f32[8,128,2,128]{3,2,1,0:T(2,128)S(1)} async-done(((f32[8,128,2,128]{3,2,1,0:T(2,128)}), f32[8,128,2,128]{3,2,1,0:T(2,128)S(1)}, u32[]{:S(2)}, u32[]{:S(2)}) %all-to-all-start.1) | async-done | bytes 1048608 | tf_op jit(solution)/shard_map/all_to_all | solution.py:87
  95.0 498.9 %while.34 = (s32[]{:T(128)}, f32[8,64,128]{2,0,1:T(8,128)}, f32[8,64,128]{2,0,1:T(8,128)S(1)}, f32[16,8,64,128]{3,1,2,0:T(8,128)}, f32[16,8,64,128]{3,1,2,0:T(8,...) while((s32[]{:T(128)}, f32[8,64,128]{2,0,1:T(8,128)}, ...), condition=%wide.region_3.4_spmd.clone, body=%wide.region_2.3_spmd.clone.sunk | while | flops 7618562 | bytes 16921708 | solution.py:112
  112.2 7.5 collective-permute-start.5
  130.5 4.7 collective-permute-start.1
  161.7 4.4 collective-permute-start.1
  192.7 4.6 collective-permute-start.1
  593.9 4.6 rev.10
  598.5 4.6 rev.11
  603.1 535.8 %while.35 = (s32[]{:T(128)}, f32[8,64,128]{2,0,1:T(8,128)}, f32[8,64,128]{2,0,1:T(8,128)S(1)}, f32[8,64,128]{2,0,1:T(8,128)}, f32[8,64,128]{2,0,1:T(8,128)}, /*i...) while((s32[]{:T(128)}, f32[8,64,128]{2,0,1:T(8,128)}, ...), condition=%wide.region_5.6_spmd.clone, body=%wide.region_4.5_spmd.clone.sunk | while | flops 8077315 | bytes 16536580 | solution.py:127
  628.5 5.6 fusion.102
  661.9 5.7 fusion.102
  695.4 5.6 fusion.102
  728.9 5.7 fusion.102
  762.4 5.7 fusion.102
  795.9 5.7 fusion.102
  829.4 5.7 fusion.102
  862.9 5.7 fusion.102
  896.4 5.6 fusion.102
  929.9 5.7 fusion.102
  963.4 5.6 fusion.102
  996.9 5.7 fusion.102
  1030.4 5.6 fusion.102
  1063.8 5.7 fusion.102
  1097.3 5.6 fusion.102
  1130.8 5.6 fusion.102
  1141.8 50.4 %scatter_fusion.1 = f32[8,128,2,128]{3,2,1,0:T(2,128)} fusion(f32[8,128,2,128]{3,2,1,0:T(2,128)} %broadcast_in_dim.22, s32[512]{0:T(512)S(1)} %bitcast.77, f32[512,2,128]{2,1,0:T(2,128)S(1)} %copy.100), kind=kCustom, calls=%fused_computation.3 | custom fusion | bytes 1576960 | tf_op jit(solution)/shard_map/scatter | solution.py:138
  1192.2 8.3 all-to-all-start.2
  1202.1 24.5 %all-to-all-done.2 = f32[8,128,2,128]{3,2,1,0:T(2,128)S(1)} async-done(((f32[8,128,2,128]{3,2,1,0:T(2,128)}), f32[8,128,2,128]{3,2,1,0:T(2,128)S(1)}, u32[]{:S(2)}, u32[]{:S(2)}) %all-to-all-start.2) | async-done | bytes 1048608 | tf_op jit(solution)/shard_map/all_to_all | solution.py:140
  1227.8 102.8 %scatter_fusion.2 = f32[1024,2,128]{2,1,0:T(2,128)} fusion(f32[1024,2,128]{2,1,0:T(2,128)} %broadcast_in_dim.21, s32[1024]{0:T(1024)S(1)} %bitcast.84, f32[1024,2,128]{2,1,0:T(2,128)S(1)} %bitcast.79), kind=kCustom, calls=%fused_computation.4 | custom fusion | flops 262144 | bytes 3149824 | tf_op jit(solution)/shard_map/scatter-add | solution.py:145
  (1199 shorter events, 941.1 us)
Async XLA Ops:
  64.1 27.3 %all-to-all-start.1 = ((f32[8,128,2,128]{3,2,1,0:T(2,128)}), f32[8,128,2,128]{3,2,1,0:T(2,128)S(1)}, u32[]{:S(2)}, u32[]{:S(2)}) async-start(f32[8,128,2,128]{3,2,1,0:T(2,128)} %bitcast.10), calls=%async_computation.1 | async-start | bytes 2097152 | tf_op jit(solution)/shard_map/all_to_all | solution.py:87
  110.4 11.4 collective-permute-start.4
  112.2 10.1 collective-permute-start.5
  129.2 7.3 collective-permute-start
  130.5 7.3 collective-permute-start.1
  145.6 7.5 collective-permute-start.4
  176.6 7.5 collective-permute-start.4
  191.4 7.2 collective-permute-start
  207.6 7.5 collective-permute-start.4
  238.6 7.5 collective-permute-start.4
  269.5 7.5 collective-permute-start.4
  300.5 7.5 collective-permute-start.4
  331.4 7.5 collective-permute-start.4
  362.4 7.5 collective-permute-start.4
  393.3 7.5 collective-permute-start.4
  424.3 7.5 collective-permute-start.4
  455.3 7.5 collective-permute-start.4
  486.2 7.5 collective-permute-start.4
  517.1 7.5 collective-permute-start.4
  548.1 7.5 collective-permute-start.4
  579.1 7.5 collective-permute-start.4
  603.2 7.2 collective-permute-start.6
  636.6 7.2 collective-permute-start.6
  670.1 7.2 collective-permute-start.6
  703.6 7.2 collective-permute-start.6
  737.1 7.2 collective-permute-start.6
  770.6 7.2 collective-permute-start.6
  804.1 7.2 collective-permute-start.6
  837.6 7.2 collective-permute-start.6
  904.6 7.2 collective-permute-start.6
  971.6 7.2 collective-permute-start.6
  1192.2 34.3 %all-to-all-start.2 = ((f32[8,128,2,128]{3,2,1,0:T(2,128)}), f32[8,128,2,128]{3,2,1,0:T(2,128)S(1)}, u32[]{:S(2)}, u32[]{:S(2)}) async-start(f32[8,128,2,128]{3,2,1,0:T(2,128)} %scatter_fusion.1), calls=%async_computation.2 | async-start | bytes 2097152 | tf_op jit(solution)/shard_map/all_to_all | solution.py:140
  (298 other events, 1725.2 us)
where the time goes:
time: 1350 us; the launch traced here: 1330 us
  starting transfers between devices  527 us (39%)
  other arithmetic  348 us (26%)
  local copies, waits for them, and re-layouts  330 us (24%)
  waiting for transfers between devices  108 us (8%)
    ppermute x96, starting transfers between devices, with_halo(): lax.ppermute(lax.slice_in_dim(block, block.shape[dim] - width, None, axis...  313 us
    ppermute x96, starting transfers between devices, with_halo(): lax.ppermute(lax.slice_in_dim(block, 0, width, axis=dim), axis, backward)  202 us
    scatter-add x1, other arithmetic, body(): model_gradient = jnp.zeros((held_count, 2, block_z), jnp.float32).at[targ...  103 us
    add x16, other arithmetic, backward(): grad_aniso = grad_aniso + following * (2.0 * slow_coef * horizontal)  90.5 us
    dynamic_update_slice x32, other arithmetic, body(): lax.scan(forward, (forward_prev, forward_now), wavelet)  73.4 us
    ppermute x96, waiting for transfers between devices, with_halo(): lax.ppermute(lax.slice_in_dim(block, block.shape[dim] - width, None, axis...  67.8 us
    scatter x1, local copies, waits for them, and re-layouts, body(): outgoing = jnp.zeros((owners_count, capacity, 2, block_z), jnp.float32).a...  50.4 us
    ppermute x32, local copies, waits for them, and re-layouts, with_halo(): lax.ppermute(lax.slice_in_dim(block, 0, width, axis=dim), axis, backward)  48.2 us
  transfers between devices with their start and end apart: 194, of which 66 were waited for; matrix products, arithmetic and copies ran while one was open for 10% of the time, Pallas kernels for 0%

commit v1 on v0

--- a/solution.py
+++ b/solution.py
@@ -1,6 +1,11 @@
+import functools
+
 import jax
 import jax.numpy as jnp
+import numpy as np
 from jax import lax
+from jax.experimental import pallas as pl
+from jax.experimental.pallas import tpu as pltpu
 from jax.sharding import PartitionSpec as P
 
 STENCIL = (-205.0 / 72.0, 8.0 / 5.0, -1.0 / 5.0, 8.0 / 315.0, -1.0 / 560.0)
@@ -47,7 +52,7 @@
     return (following, laplacian, horizontal)
 
 
-def body(
+def block_body(
     forward_prev,
     forward_now,
     adjoint_prev,
@@ -147,6 +152,658 @@
     return (forward_final, adjoint_final, model_gradient[None])
 
 
+BX, BY, BZ = 8, 64, 128
+GX, GY = 4, 2
+NXA, NYA = BX * GX, BY * GY
+ZS = 16
+ZE = 32
+HALO = 8
+OWN = slice(HALO, HALO + ZS)
+SCALE = 5040.0
+PADX = 4
+STEPS = 16
+ROUNDS = STEPS // 2
+MIB = 1 << 20
+F32 = jnp.float32
+BF16 = jnp.bfloat16
+H, IX, IY, SHOT, LINE, SX, SY, SZ = range(8)
+
+
+def slabs_fit(mesh):
+    names = ("shots", "gx", "gy", "gz")
+    return tuple(mesh.shape[n] for n in names) == (2, GX, GY, 2)
+
+
+def line_device(place):
+    chip, core = divmod(place, 2)
+    ix, iy = (chip, 0) if chip < GX else (2 * GX - 1 - chip, 1)
+    return (ix * GY + iy) * 2 + core
+
+
+def off_chip_pairs():
+    count = 2 * GX * GY
+    pairs = []
+    for low in range(1, count, 2):
+        a, b = line_device(low), line_device((low + 1) % count)
+        pairs += [(a, b), (b, a)]
+    return pairs
+
+
+OFF_PAIRS = off_chip_pairs()
+SWAP = [(0, 1), (1, 0)]
+
+
+def to_sibling(x):
+    return lax.ppermute(x, "gz", SWAP)
+
+
+def to_off_chip(x):
+    return lax.ppermute(x, ("gx", "gy", "gz"), OFF_PAIRS)
+
+
+def band(size):
+    out = np.zeros((size, size), np.float32)
+    for offset in range(1, 5):
+        value = round(STENCIL[offset] * SCALE)
+        for i in range(size - offset):
+            out[i, i + offset] = value
+            out[i + offset, i] = value
+    return out
+
+
+def matrices():
+    along_y = band(NYA)
+    along_y = np.concatenate([along_y, along_y], 0)
+    along_z = band(ZE)
+    full = np.kron(np.eye(8, dtype=np.float32), along_z)
+    own = np.kron(np.eye(8, dtype=np.float32), along_z[OWN])
+    return [jnp.asarray(m, BF16) for m in (along_y, full, own)]
+
+
+def vmem(count):
+    return [pl.BlockSpec(memory_space=pltpu.VMEM)] * count
+
+
+SMEM = pl.BlockSpec(memory_space=pltpu.SMEM)
+
+
+def call(kernel, outs, specs, scratch=(), limit=24, flops=0, moved=0, aliases=None):
+    return pl.pallas_call(
+        kernel,
+        out_shape=[jax.ShapeDtypeStruct(s, d) for s, d in outs],
+        in_specs=specs,
+        out_specs=vmem(len(outs)),
+        scratch_shapes=list(scratch),
+        input_output_aliases=aliases or {},
+        compiler_params=pltpu.CompilerParams(vmem_limit_bytes=limit * MIB),
+        cost_estimate=pl.CostEstimate(flops=flops, bytes_accessed=moved, transcendentals=0),
+    )
+
+
+def half_lanes(shape):
+    return lax.broadcasted_iota(jnp.int32, shape, len(shape) - 1) < BY
+
+
+def roll_half(x):
+    return pltpu.roll(x, BY, x.ndim - 1)
+
+
+def place(scal, chunk):
+    chip, core = divmod(chunk, 2)
+    mine = core == scal[H]
+    return mine, jnp.where(scal[H] == 0, chip, GX - 1 - chip)
+
+
+def pack_table(scal, table, keep, give):
+    first = scal[SHOT] * 1024
+    for q in range(4):
+        for comp in range(2):
+            rows = table[pl.ds(first + q * 256 + comp, 128, stride=2), :]
+            turned = rows.T
+            for chunk in range(8):
+                mine, g = place(scal, chunk)
+                piece = turned[chunk * ZS : (chunk + 1) * ZS][None]
+
+                @pl.when(mine)
+                def _():
+                    keep[pl.ds(g, 1), q, comp * ZS : (comp + 1) * ZS, :] = piece
+
+                @pl.when(jnp.logical_not(mine))
+                def _():
+                    give[pl.ds(g, 1), q, comp * ZS : (comp + 1) * ZS, :] = piece
+
+
+def pack_fields(scal, *refs):
+    fields, (keep, give) = refs[:4], refs[4:]
+    for f in range(4):
+        for i in range(4):
+            pair = fields[f][2 * i : 2 * i + 2].reshape(128, 128)
+            turned = pair.T
+            for chunk in range(8):
+                mine, g = place(scal, chunk)
+                piece = turned[chunk * ZS : (chunk + 1) * ZS][None]
+
+                @pl.when(mine)
+                def _():
+                    keep[pl.ds(g, 1), f, i] = piece
+
+                @pl.when(jnp.logical_not(mine))
+                def _():
+                    give[pl.ds(g, 1), f, i] = piece
+
+
+def unpack_small(scal, mine, other, ids_slab, ids_owner, depth, traces):
+    low = half_lanes((8, 128))
+    h = scal[H]
+    for ix in range(GX):
+        rows = slice(ix * BX, (ix + 1) * BX)
+        for ref, is_mine in ((mine, True), (other, False)):
+            a, b = ref[ix * GY], ref[ix * GY + 1]
+            core = h if is_mine else 1 - h
+            for tt in range(4):
+                even = jnp.where(low, a[tt], roll_half(b[tt]))
+                odd = jnp.where(low, roll_half(a[tt]), b[tt])
+                traces[pl.ds(core * 8 + 2 * tt, 1), rows, :] = even[None]
+                traces[pl.ds(core * 8 + 2 * tt + 1, 1), rows, :] = odd[None]
+            ids = jnp.where(low, a[4], roll_half(b[4])).astype(jnp.int32)
+            if is_mine:
+                ids_owner[rows, :] = ids
+                depth[rows, :] = jnp.where(low, roll_half(a[4]), b[4]).astype(jnp.int32)
+
+            @pl.when(core == scal[IY])
+            def _():
+                ids_slab[rows, :] = ids
+
+
+def gather_half(second, scal, table, ids, *refs):
+    if second:
+        before, out, sib, off = refs
+    else:
+        (out,) = refs
+    half = 1 - scal[SHOT] if second else scal[SHOT]
+
+    def column(x, carry):
+        row = ids[pl.ds(x, 1), :]
+        chunk = row >> 7
+        local = jnp.where(((chunk >> 2) & 1) == half, ((chunk >> 3) << 2) | (chunk & 3), -1)
+        lane = jnp.broadcast_to(row & 127, (8, 128))
+        local = jnp.broadcast_to(local, (8, 128))
+        if second:
+            totals = [before[x, 8 * t : 8 * t + 8, :] for t in range(4)]
+        else:
+            totals = [jnp.zeros((8, 128), F32) for t in range(4)]
+        for j in range(32):
+            hit = local == j
+            for t in range(4):
+                value = jnp.take_along_axis(
+                    table[j // 4, j % 4, 8 * t : 8 * t + 8, :], lane, axis=1, mode="promise_in_bounds"
+                )
+                totals[t] = jnp.where(hit, value, totals[t])
+        for t in range(4):
+            out[x, 8 * t : 8 * t + 8, :] = totals[t]
+        return carry
+
+    lax.fori_loop(0, NXA, column, 0)
+    if second:
+        h = scal[H]
+        for comp in range(2):
+            rows = slice(comp * HALO, (comp + 1) * HALO)
+            sib[:, rows, :] = out[:, pl.ds(comp * ZS + HALO * (1 - h), HALO), :]
+            off[:, rows, :] = out[:, pl.ds(comp * ZS + HALO * h, HALO), :]
+
+
+def is_edge(scal):
+    return (scal[LINE] == 0) | (scal[LINE] == 2 * GX * GY - 1)
+
+
+def extend_coefs(scal, coefs, sib, off, slow, aniso):
+    sib_at = (ZE - HALO) * (1 - scal[H])
+    off_at = (ZE - HALO) * scal[H]
+    inside = jnp.where(is_edge(scal), 0.0, 1.0)
+    slow[:, OWN, :] = coefs[:, 0:ZS, :]
+    slow[:, pl.ds(sib_at, HALO), :] = sib[:, 0:HALO, :]
+    slow[:, pl.ds(off_at, HALO), :] = off[:, 0:HALO, :] * inside
+    aniso[:, OWN, :] = 1.0 + 2.0 * coefs[:, ZS:, :]
+    aniso[:, pl.ds(sib_at, HALO), :] = 1.0 + 2.0 * sib[:, HALO:, :]
+    aniso[:, pl.ds(off_at, HALO), :] = 1.0 + 2.0 * off[:, HALO:, :]
+
+
+def unpack_fields(scal, got, *outs):
+    low = half_lanes((ZS, 128))
+    h = scal[H]
+    for kind in range(2):
+        prev, now, sib, off = outs[4 * kind : 4 * kind + 4]
+        for step, own in ((0, prev), (1, now)):
+            f = 2 * kind + step
+            for ix in range(GX):
+                for i in range(4):
+                    a, b = got[ix * GY, f, i], got[ix * GY + 1, f, i]
+                    x = ix * BX + 2 * i
+                    own[x] = jnp.where(low, a, roll_half(b))
+                    own[x + 1] = jnp.where(low, roll_half(a), b)
+            sib[step] = own[:, pl.ds(HALO * (1 - h), HALO), :]
+            off[step] = own[:, pl.ds(HALO * h, HALO), :]
+
+
+def ranks_of(owner, owners):
+    masks = jnp.concatenate(
+        [(owner[ix * BX : (ix + 1) * BX] == o).astype(F32) for ix in range(GX) for o in owners], axis=0
+    )
+    rows = masks.shape[0]
+    first = lax.broadcasted_iota(jnp.int32, (128, 128), 0)
+    second = lax.broadcasted_iota(jnp.int32, (128, 128), 1)
+    before = (first < second).astype(F32).astype(BF16)
+    bits = masks.astype(BF16)
+    along = jnp.dot(bits, before, preferred_element_type=F32)
+    sums = jnp.dot(bits, jnp.ones((128, 128), BF16), preferred_element_type=F32)
+    r0 = lax.broadcasted_iota(jnp.int32, (rows, rows), 0)
+    r1 = lax.broadcasted_iota(jnp.int32, (rows, rows), 1)
+    earlier = (((r0 >> 3) == (r1 >> 3)) & (r1 < r0)).astype(F32).astype(BF16)
+    above = jnp.dot(earlier, sums.astype(BF16), preferred_element_type=F32)
+    return jnp.where(masks > 0.0, along + above, -1.0).astype(jnp.int32)
+
+
+def index_kernel(scal, ids_slab, ids_owner, out, ranks, acc):
+    me = scal[IX] * GY + scal[IY]
+    ranks[0:256] = ranks_of(ids_slab[...] >> 10, list(range(8)))
+    ranks[256:288] = ranks_of(ids_owner[...] >> 10, [me])
+    acc[...] = jnp.full((256, 128), -1, jnp.int32)
+    lanes = lax.broadcasted_iota(jnp.int32, (256, 128), 1)
+    places = lax.broadcasted_iota(jnp.int32, (256, 128), 0)
+
+    def combo(n, carry):
+        is_slab = n < 32
+        ix = jnp.where(is_slab, n >> 3, n - 32)
+        found = jnp.full((256, 128), -1, jnp.int32)
+        for x in range(BX):
+            row = jnp.broadcast_to(ranks[pl.ds(n * BX + x, 1), :], (256, 128))
+            slots = ids_owner[pl.ds(ix * BX + x, 1), :] & 1023
+            column = x * 128 + lax.broadcasted_iota(jnp.int32, (1, 128), 1)
+            value = jnp.broadcast_to(jnp.where(is_slab, column, slots), (256, 128))
+            found = jnp.where(row == places, value, found)
+        best = jnp.max(found, axis=1, keepdims=True)
+        acc[...] = jnp.where(lanes == n, jnp.broadcast_to(best, (256, 128)), acc[...])
+        return carry
+
+    lax.fori_loop(0, 36, combo, 0)
+    turned = acc[...].astype(F32).T[0:40].astype(jnp.int32)
+    out[0] = turned[:, 0:128]
+    out[1] = turned[:, 128:256]
+
+
+def stencil(field, g, along_y, along_z, own):
+    rows = slice(PADX + 8 * g, PADX + 8 * g + 8)
+    zs = OWN if own else slice(0, ZE)
+    depth = ZS if own else ZE
+    whole = field[rows].reshape(8 * ZE, 128)
+    high = whole.astype(BF16)
+    rest = (whole - high.astype(F32)).astype(BF16)
+    both = jnp.concatenate([high, rest], axis=1)
+    my = jnp.dot(both, along_y[...], preferred_element_type=F32).reshape(8, ZE, 128)[:, zs]
+    mz = jnp.dot(along_z[...], both, preferred_element_type=F32)
+    mz = (mz[:, :128] + mz[:, 128:]).reshape(8, depth, 128)
+    center = field[rows, zs, :]
+    hor = my * (1.0 / SCALE) + (2.0 * STENCIL[0]) * center
+    for i in range(1, 5):
+        up = field[PADX + 8 * g + i : PADX + 8 * g + 8 + i, zs, :]
+        down = field[PADX + 8 * g - i : PADX + 8 * g + 8 - i, zs, :]
+        hor = hor + STENCIL[i] * (up + down)
+    ver = mz * (1.0 / SCALE) + STENCIL[0] * center
+    return center, hor, ver
+
+
+def round_kernel(kind, r, scal, *refs):
+    refs = list(refs)
+    take = lambda n: [refs.pop(0) for _ in range(n)]
+    first, later, last = r == 0, r >= ROUNDS // 2, r == ROUNDS - 1
+    if kind == "u":
+        (weights,) = take(1)
+    else:
+        traces, depth = take(2)
+    own, sib, off = take(3)
+    (prev,) = take(1)
+    slow, aniso, along_y, along_z, along_z_own = take(5)
+    if later:
+        if kind == "u":
+            partner_mid, partner_end = take(2)
+        else:
+            (partner,) = take(1)
+        if r > ROUNDS // 2:
+            (total_in,) = take(1)
+    out_own, out_mid = take(2)
+    if not last:
+        out_sib, out_off = take(2)
+    if later:
+        (total,) = take(1)
+    elif kind == "u":
+        (history,) = take(1)
+    e0, e1 = take(2)
+
+    h = scal[H]
+    sib_at = (ZE - HALO) * (1 - h)
+    off_at = (ZE - HALO) * h
+    edge = is_edge(scal)
+    zero = jnp.zeros((PADX, ZE, 128), F32)
+    for e in (e0, e1):
+        e[0:PADX] = zero
+        e[PADX + NXA :] = zero
+    inner = slice(PADX, PADX + NXA)
+    now = 1 if first else 0
+    e0[inner, OWN, :] = own[...]
+    e0[inner, pl.ds(sib_at, HALO), :] = sib[now]
+    e0[inner, pl.ds(off_at, HALO), :] = jnp.where(edge, 0.0, off[now])
+    if first:
+        out_mid[:, OWN, :] = prev[...]
+        out_mid[:, pl.ds(sib_at, HALO), :] = sib[0]
+        out_mid[:, pl.ds(off_at, HALO), :] = jnp.where(edge, 0.0, off[0])
+        prev = out_mid
+    top = scal[LINE] * ZS - HALO
+
+    def source(weight, depth_rows, start):
+        shape = (1, depth_rows, 128)
+        z = lax.broadcasted_iota(jnp.int32, shape, 1) + start
+        y = lax.broadcasted_iota(jnp.int32, shape, 2)
+        return jnp.where((z == scal[SZ]) & (y == scal[SY]), weight, 0.0)
+
+    def receivers(t, g, depth_rows, start):
+        z = lax.broadcasted_iota(jnp.int32, (depth_rows, 128), 0) + start
+        out = []
+        for x in range(8 * g, 8 * g + 8):
+            at = jnp.broadcast_to(depth[x : x + 1, :], (depth_rows, 128))
+            value = jnp.broadcast_to(traces[t, x : x + 1, :], (depth_rows, 128))
+            out.append(jnp.where(z == at, value, 0.0)[None])
+        return jnp.concatenate(out, axis=0)
+
+    for step in range(2):
+        t = 2 * r + step
+        field = e1 if step else e0
+        depth_rows = ZS if step else ZE
+        start = top + HALO if step else top
+        for g in range(4):
+            xs = slice(8 * g, 8 * g + 8)
+            zs = OWN if step else slice(0, ZE)
+            center, hor, ver = stencil(field, g, along_y, along_z_own if step else along_z, step)
+            before = e0[PADX + 8 * g : PADX + 8 * g + 8, OWN, :] if step else prev[xs]
+            lap = aniso[xs, zs, :] * hor + ver
+            following = 2.0 * center - before + slow[xs, zs, :] * lap
+            if kind == "a":
+                following = following + receivers(STEPS - 1 - t, g, depth_rows, start)
+            if step:
+                out_own[xs] = following
+            else:
+                e1[PADX + 8 * g : PADX + 8 * g + 8] = following
+            if step == 0:
+                hor, ver = hor[:, OWN], ver[:, OWN]
+            if kind == "u" and not later:
+                history[2 * step, xs] = hor
+                history[2 * step + 1, xs] = ver
+            if later:
+                if kind == "u":
+                    other = partner_mid[xs, OWN, :] if step else partner_end[xs]
+                    hor_part, ver_part = hor, ver
+                else:
+                    other = following if step else following[:, OWN]
+                    hor_part = partner[2 * (1 - step), xs]
+                    ver_part = partner[2 * (1 - step) + 1, xs]
+                sum_h, sum_v = other * hor_part, other * ver_part
+                if step:
+                    sum_h, sum_v = total[0, xs] + sum_h, total[1, xs] + sum_v
+                elif r > ROUNDS // 2:
+                    sum_h, sum_v = total_in[0, xs] + sum_h, total_in[1, xs] + sum_v
+                total[0, xs] = sum_h
+                total[1, xs] = sum_v
+        if kind == "u":
+            if step:
+                row = out_own[pl.ds(scal[SX], 1)]
+                out_own[pl.ds(scal[SX], 1)] = row + source(weights[t], ZS, start)
+            else:
+                row = e1[pl.ds(PADX + scal[SX], 1)]
+                e1[pl.ds(PADX + scal[SX], 1)] = row + source(weights[t], ZE, start)
+    out_mid[...] = e1[inner]
+    if not last:
+        out_sib[0] = out_own[:, pl.ds(HALO * (1 - h), HALO), :]
+        out_off[0] = out_own[:, pl.ds(HALO * h, HALO), :]
+
+
+def pack_out(scal, u, a, total_u, total_a, coefs, index, out, grads):
+    for x in range(NXA):
+        gh = total_u[0, x] + total_a[0, x]
+        gv = total_u[1, x] + total_a[1, x]
+        slow, aniso = coefs[x, 0:ZS, :], coefs[x, ZS:, :]
+        grads[x, 0:ZS, :] = (1.0 + 2.0 * aniso) * gh + gv
+        grads[x, ZS:, :] = (2.0 * slow) * gh
+    low = half_lanes((ZS, 128))
+    for f, field in enumerate((u, a)):
+        for ix in range(GX):
+            for i in range(4):
+                x0, x1 = field[ix * BX + 2 * i], field[ix * BX + 2 * i + 1]
+                at = 256 + (f * 4 + i) * ZS
+                out[ix * GY, at : at + ZS, :] = jnp.where(low, x0, roll_half(x1))
+                out[ix * GY + 1, at : at + ZS, :] = jnp.where(low, roll_half(x0), x1)
+
+    def combo(n, carry):
+        ix, o = n >> 3, n & 7
+        for part in range(2):
+            row = index[part, pl.ds(n, 1), :]
+            lane = jnp.broadcast_to(row & 127, (8, 128))
+            which = jnp.broadcast_to(row >> 7, (8, 128))
+            totals = [jnp.zeros((8, 128), F32) for t in range(4)]
+            for x in range(BX):
+                hit = which == x
+                for t in range(4):
+                    value = jnp.take_along_axis(
+                        grads[ix * BX + x, 8 * t : 8 * t + 8, :], lane, axis=1, mode="promise_in_bounds"
+                    )
+                    totals[t] = jnp.where(hit, value, totals[t])
+            for t in range(4):
+                at = pl.multiple_of((ix * 2 + part) * 32 + 8 * t, 8)
+                out[o, pl.ds(at, 8), :] = totals[t]
+        return carry
+
+    lax.fori_loop(0, 32, combo, 0)
+
+
+def finish(scal, got, other, index, u_out, a_out, model, turned, columns):
+    h = scal[H]
+    sources = []
+    for ix in range(GX):
+        chip = jnp.where(h == 0, ix, GX - 1 - ix)
+        base = chip * 2 * ZS
+        sources.append((got, ix, True, base + h * ZS))
+        sources.append((other, ix, False, base + (1 - h) * ZS))
+
+    def piece(ref, ix, mine, start, count):
+        if mine:
+            return ref[ix, pl.ds(h, 1), start : start + count, :].reshape(count, 128)
+        return ref[ix, start : start + count, :]
+
+    for f, out in enumerate((u_out, a_out)):
+        for i in range(4):
+            for ref, ix, mine, z0 in sources:
+                turned[pl.ds(pl.multiple_of(z0, ZS), ZS), :] = piece(ref, ix, mine, 256 + (f * 4 + i) * ZS, ZS)
+            out[2 * i : 2 * i + 2] = turned[...].T.reshape(2, BY, 128)
+    for n in range(8):
+        for comp in range(2):
+            for ref, ix, mine, z0 in sources:
+                rows = pl.ds(pl.multiple_of(comp * 128 + z0, ZS), ZS)
+                columns[rows, n * 128 : (n + 1) * 128] = piece(ref, ix, mine, n * 32 + comp * ZS, ZS)
+    values = columns[...]
+    high = values.astype(BF16)
+    rest = (values - high.astype(F32)).astype(BF16)
+    named = jnp.concatenate(
+        [index[n % 2, 32 + n // 2 : 33 + n // 2, :] for n in range(8)], axis=1
+    )
+    for block in range(4):
+        slot = lax.broadcasted_iota(jnp.int32, (256, 1024), 0) + block * 256
+        pick = (slot == jnp.broadcast_to(named, (256, 1024))).astype(F32).astype(BF16)
+        dims = (((1,), (1,)), ((), ()))
+        sums = lax.dot_general(pick, high, dims, preferred_element_type=F32)
+        sums = sums + lax.dot_general(pick, rest, dims, preferred_element_type=F32)
+        for comp in range(2):
+            model[pl.ds(block * 512 + comp, 256, stride=2), :] = sums[:, comp * 128 : (comp + 1) * 128]
+
+
+def by_half(h, mine, other):
+    first = jnp.where(h == 0, mine, other)
+    second = jnp.where(h == 0, other, mine)
+    both = jnp.stack([first, second], axis=1)
+    return both.reshape((GX * GY,) + mine.shape[1:])
+
+
+def exchange(x):
+    return lax.all_to_all(x, ("gx", "gy"), split_axis=0, concat_axis=0, tiled=True)
+
+
+def slab_body(
+    forward_prev,
+    forward_now,
+    adjoint_prev,
+    adjoint_now,
+    model_table,
+    tile_owner,
+    tile_slot,
+    source_index,
+    wavelet,
+    receiver_depth,
+    traces,
+):
+    h = lax.axis_index("gz")
+    ix, iy = lax.axis_index("gx"), lax.axis_index("gy")
+    chip = jnp.where(iy == 0, ix, 2 * GX - 1 - ix)
+    line = 2 * chip + h
+    scal = jnp.stack(
+        [h, ix, iy, lax.axis_index("shots"), line, source_index[0], source_index[1], source_index[2]]
+    ).astype(jnp.int32)
+
+    table = model_table.reshape(2048, 128)
+    keep, give = call(
+        pack_table, [((4, 4, 32, 128), F32)] * 2, [SMEM] + vmem(1), moved=2 * MIB, flops=1 << 20
+    )(scal, table)
+    table_chunks = by_half(h, keep, to_sibling(give))
+    ids = (tile_owner.reshape(BX, BY) * 1024 + tile_slot.reshape(BX, BY)).astype(F32)
+    small = jnp.concatenate([ids, receiver_depth.astype(F32)], axis=1)[None]
+    trace_half = lax.dynamic_slice_in_dim(traces, h * 8, 8, axis=0).reshape(4, 2, BX, BY)
+    trace_half = trace_half.transpose(0, 2, 1, 3).reshape(4, BX, 128)
+    small = jnp.concatenate([trace_half, small], axis=0).reshape(1, 40, 128)
+    small = jnp.broadcast_to(small, (8, 40, 128))
+    sent = jnp.concatenate([table_chunks.reshape(8, 128, 128), small], axis=1)
+    arrived = exchange(sent)
+    table_mine = arrived[:, :128].reshape(8, 4, 32, 128)
+    small_mine = arrived[:, 128:].reshape(8, 5, 8, 128)
+    table_other = lax.ppermute(table_mine, "shots", SWAP)
+    small_other = to_sibling(small_mine)
+
+    keep, give = call(
+        pack_fields, [((4, 4, 4, ZS, 128), F32)] * 2, [SMEM] + vmem(4), moved=2 * MIB, flops=1 << 20
+    )(scal, forward_prev, forward_now, adjoint_prev, adjoint_now)
+    fields = exchange(by_half(h, keep, to_sibling(give)))
+
+    ids_slab, ids_owner, depth, traces = call(
+        unpack_small,
+        [((NXA, 128), jnp.int32)] * 3 + [((STEPS, NXA, 128), F32)],
+        [SMEM] + vmem(2),
+        moved=MIB // 2,
+        flops=1 << 20,
+    )(scal, small_mine, small_other)
+    coef_shape = ((NXA, 2 * ZS, 128), F32)
+    half_shape = ((NXA, 2 * HALO, 128), F32)
+    (coefs,) = call(
+        functools.partial(gather_half, False), [coef_shape], [SMEM] + vmem(2), moved=MIB, flops=1 << 24
+    )(scal, table_mine, ids_slab)
+    coefs, coefs_sib, coefs_off = call(
+        functools.partial(gather_half, True),
+        [coef_shape, half_shape, half_shape],
+        [SMEM] + vmem(3),
+        moved=2 * MIB,
+        flops=1 << 24,
+    )(scal, table_other, ids_slab, coefs)
+    ext_shape = ((NXA, ZE, 128), F32)
+    own_shape = ((NXA, ZS, 128), F32)
+    slow, aniso = call(extend_coefs, [ext_shape] * 2, [SMEM] + vmem(3), moved=2 * MIB, flops=1 << 20)(
+        scal, coefs, to_sibling(coefs_sib), to_off_chip(coefs_off)
+    )
+    (index,) = call(
+        index_kernel,
+        [((2, 40, 128), jnp.int32)],
+        [SMEM] + vmem(2),
+        [pltpu.VMEM((288, 128), jnp.int32), pltpu.VMEM((256, 128), jnp.int32)],
+        moved=MIB // 4,
+        flops=1 << 24,
+    )(scal, ids_slab, ids_owner)
+
+    first_halo = ((2, NXA, HALO, 128), F32)
+    unpacked = call(
+        unpack_fields,
+        [own_shape, own_shape, first_halo, first_halo] * 2,
+        [SMEM] + vmem(1),
+        moved=4 * MIB,
+        flops=1 << 20,
+    )(scal, fields)
+    bands = matrices()
+    halo = ((1, NXA, HALO, 128), F32)
+    state = {}
+    for n, kind in enumerate("ua"):
+        prev, now, sib, off = unpacked[4 * n : 4 * n + 4]
+        state[kind] = [now, to_sibling(sib), to_off_chip(off), prev]
+    history, mids, ends, totals = {}, {}, {}, {}
+    for r in range(ROUNDS):
+        for kind in "ua":
+            later, last = r >= ROUNDS // 2, r == ROUNDS - 1
+            drive = [wavelet] if kind == "u" else [traces, depth]
+            specs = [SMEM] + ([SMEM] if kind == "u" else vmem(2))
+            args = state[kind] + [slow, aniso] + bands
+            if later:
+                partner = ROUNDS - 1 - r
+                args += [mids[partner], ends[partner]] if kind == "u" else [history[partner]]
+                if r > ROUNDS // 2:
+                    args += [totals[kind]]
+            specs = specs + vmem(len(args))
+            outs = [own_shape, ext_shape] + ([] if last else [halo, halo])
+            if later:
+                outs.append(((2, NXA, ZS, 128), F32))
+            elif kind == "u":
+                outs.append(((4, NXA, ZS, 128), F32))
+            res = call(
+                functools.partial(round_kernel, kind, r),
+                outs,
+                specs,
+                [pltpu.VMEM((NXA + 2 * PADX, ZE, 128), F32)] * 2,
+                moved=4 * MIB,
+                flops=1 << 24,
+            )(scal, *drive, *args)
+            own, mid = res[0], res[1]
+            if later:
+                totals[kind] = res[-1]
+            elif kind == "u":
+                history[r] = res[-1]
+            if kind == "a":
+                mids[r], ends[r] = mid, own
+            if last:
+                state[kind] = [own]
+            else:
+                state[kind] = [own, to_sibling(res[2]), to_off_chip(res[3]), mid]
+
+    (packed,) = call(
+        pack_out,
+        [((8, 384, 128), F32)],
+        [SMEM] + vmem(6),
+        [pltpu.VMEM((NXA, 2 * ZS, 128), F32)],
+        moved=4 * MIB,
+        flops=1 << 24,
+    )(scal, state["u"][0], state["a"][0], totals["u"], totals["a"], coefs, index)
+    got = exchange(packed).reshape(GX, GY, 384, 128)
+    other = to_sibling(lax.dynamic_index_in_dim(got, 1 - h, axis=1, keepdims=False))
+    u, a, model = call(
+        finish,
+        [((BX, BY, BZ), F32)] * 2 + [((2048, 128), F32)],
+        [SMEM] + vmem(3),
+        [pltpu.VMEM((128, 128), F32), pltpu.VMEM((256, 1024), F32)],
+        moved=4 * MIB,
+        flops=1 << 28,
+    )(scal, got, other, index)
+    return (u, a, model.reshape(1, 1024, 2, 128))
+
+
 def solution(mesh):
     in_specs = (
         P(("shots", "gx"), "gy", "gz"),
@@ -166,4 +823,5 @@
         P(("shots", "gx"), "gy", "gz"),
         P("gz", ("shots", "gx", "gy"), None, None),
     )
+    body = slab_body if slabs_fit(mesh) else block_body
     return jax.shard_map(body, mesh=mesh, in_specs=in_specs, out_specs=out_specs, check_vma=False)

time: 1350 us -> 187 us (0.14); the launches traced: 1330 us -> 186 us
  starting transfers between devices: 527 us -> 37.5 us
  other arithmetic: 348 us -> 4.02 us
  local copies, waits for them, and re-layouts: 330 us -> 4.03 us
  Pallas kernels: 0 us -> 71.6 us
  waiting for transfers between devices: 108 us -> 67.8 us
    ppermute x192 -> x39, starting transfers between devices: 515 us -> 22.8 us  [the longest x21 13.7 us: to_sibling(): return lax.ppermute(x, 'gz', SWAP)]
    add x49 -> x0, other arithmetic: 136 us -> none  [the longest x16 90.5 us: backward(): grad_aniso = grad_aniso + following * (2.0 * slow_coef * horizontal)]
    scatter-add x1 -> x0, other arithmetic: 103 us -> none  [body(): model_gradient = jnp.zeros((held_count, 2, block_z), jnp.float32).at[targ...]
    scatter x2 -> x0, local copies, waits for them, and re-layouts: 92.8 us -> none  [the longest x1 50.4 us: body(): outgoing = jnp.zeros((owners_count, capacity, 2, block_z), jnp.float32).a...]
    dynamic_update_slice x32 -> x0, other arithmetic: 73.4 us -> none  [body(): lax.scan(forward, (forward_prev, forward_now), wavelet)]
    ppermute x64 -> x0, local copies, waits for them, and re-layouts: 71.6 us -> none  [the longest x32 48.2 us: with_halo(): lax.ppermute(lax.slice_in_dim(block, 0, width, axis=dim), axis, backward)]
    pallas_call x0 -> x26, Pallas kernels: none -> 71.6 us  [the longest x16 29.5 us: slab_body(): call(functools.partial(round_kernel, kind, r), outs, specs, [pltpu.VMEM((...]
    ppermute x192 -> x39, waiting for transfers between devices: 68.1 us -> 16.9 us  [the longest x17 11.5 us: to_off_chip(): return lax.ppermute(x, ('gx', 'gy', 'gz'), OFF_PAIRS)]
  transfers between devices with their start and end apart: 194 -> 42, of which waited for: 66 -> 21; matrix products, arithmetic and copies ran while one was open for 10% -> 3% of each run, Pallas kernels for 0% -> 31%
where the time goes in v1:
time: 187 us; the launch traced here: 186 us
  Pallas kernels  71.6 us (38%)
  waiting for transfers between devices  67.8 us (36%)
  starting transfers between devices  37.5 us (20%)
  local copies, waits for them, and re-layouts  4.03 us (2%)
  other arithmetic  4.02 us (2%)
    all_to_all x3, waiting for transfers between devices, exchange(): lax.all_to_all(x, ('gx', 'gy'), split_axis=0, concat_axis=0, tiled=True)  50.9 us
    pallas_call x16, Pallas kernels, slab_body(): call(functools.partial(round_kernel, kind, r), outs, specs, [pltpu.VMEM((...  29.5 us
    all_to_all x3, starting transfers between devices, exchange(): lax.all_to_all(x, ('gx', 'gy'), split_axis=0, concat_axis=0, tiled=True)  14.7 us
    ppermute x21, starting transfers between devices, to_sibling(): return lax.ppermute(x, 'gz', SWAP)  13.7 us
    ppermute x17, waiting for transfers between devices, to_off_chip(): return lax.ppermute(x, ('gx', 'gy', 'gz'), OFF_PAIRS)  11.5 us
    pallas_call x1, Pallas kernels, slab_body(): call(index_kernel, [((2, 40, 128), jnp.int32)], [SMEM] + vmem(2), [pltpu....  10.9 us
    ppermute x17, starting transfers between devices, to_off_chip(): return lax.ppermute(x, ('gx', 'gy', 'gz'), OFF_PAIRS)  7.74 us
    pallas_call x1, Pallas kernels, slab_body(): call(functools.partial(gather_half, True), [coef_shape, half_shape, half_...  7.41 us
  transfers between devices with their start and end apart: 42, of which 21 were waited for; matrix products, arithmetic and copies ran while one was open for 3% of the time, Pallas kernels for 31%

profile of v1, /device:TPU:1, one launch (start us, length us, event | category | flops | bytes accessed | tf_op | source)
XLA Modules:
  0.0 185.9 jit_solution(262379845764872080)
XLA Ops:
  9.2 7.0 %all-to-all-start.1 = ((f32[8,168,128]{2,1,0:T(8,128)}), f32[8,168,128]{2,1,0:T(8,128)S(1)}, u32[]{:S(2)}, u32[]{:S(2)}) async-start(f32[8,168,128]{2,1,0:T(8,128)} %pad_maximum_fusion.1), calls=%async_computation.1 | async-start | bytes 1376256 | tf_op jit(solution)/shard_map/all_to_all | solution.py:654
  16.2 2.7 %shard_map.157 = (f32[4,4,4,16,128]{4,3,2,1,0:T(8,128)S(1)}, f32[4,4,4,16,128]{4,3,2,1,0:T(8,128)S(1)}) custom-call(s32[8]{0:T(128)S(1)} %stack.41.scal, f32[8,64,128]{2,1,0:T(8,128)S(1)} %copy-done.5, f32[8,64,128]{2,1,0:T(8,128)S(1)} %copy-done.6, f32[8,64,128]{2,1,0:T(8,128)S(1)} %copy-done.7, f32[8,64,128]{2,1,0:T(8,128)S(1)} %copy-done.8), custom_call_target="tpu_custom_call" | custom-call | flops 1048576 | bytes 2097152 | tf_op jit(solution)/shard_map/pallas_call | solution.py:696
  22.1 12.0 %all-to-all-done.1 = f32[8,168,128]{2,1,0:T(8,128)S(1)} async-done(((f32[8,168,128]{2,1,0:T(8,128)}), f32[8,168,128]{2,1,0:T(8,128)S(1)}, u32[]{:S(2)}, u32[]{:S(2)}) %all-to-all-start.1) | async-done | bytes 688160 | tf_op jit(solution)/shard_map/all_to_all | solution.py:654
  34.0 4.0 %all-to-all-start = ((f32[8,4,4,16,128]{4,3,2,1,0:T(8,128)}), f32[8,4,4,16,128]{4,3,2,1,0:T(8,128)S(1)}, u32[]{:S(2)}, u32[]{:S(2)}) async-start(f32[8,4,4,16,128]{4,3,2,1,0:T(8,128)} %bitcast.7), calls=%async_computation | async-start | bytes 2097152 | tf_op jit(solution)/shard_map/all_to_all | solution.py:654
  42.7 7.2 %shard_map.161.refs_0_ = f32[32,32,128]{2,1,0:T(8,128)S(1)} custom-call(s32[8]{0:T(128)S(1)} %stack.41.scal, f32[8,4,32,128]{3,2,1,0:T(8,128)S(1)} %bitcast.33, s32[32,128]{1,0:T(8,128)S(1)} %get-tuple-element.105.ids.ids_slab), custom_call_target="tpu_custom_call" | custom-call | flops 16777216 | bytes 1048576 | tf_op jit(solution)/shard_map/pallas_call | solution.py:710
  50.9 7.4 %shard_map.162 = (f32[32,32,128]{2,1,0:T(8,128)S(1)}, f32[32,16,128]{2,1,0:T(8,128)S(1)}, f32[32,16,128]{2,1,0:T(8,128)S(1)}) custom-call(s32[8]{0:T(128)S(1)} %stack.41.scal, f32[8,4,32,128]{3,2,1,0:T(8,128)S(1)} %collective-permute-done.4.table, s32[32,128]{1,0:T(8,128)S(1)} %get-tuple-element.105.ids.ids_slab, f32[32,32,128]{2,1,0:T(8,128)S(1)} %shard_map.161.refs_0_), custom_call_target="tpu_custom_call" | custom-call | flops 16777216 | bytes 2097152 | tf_op jit(solution)/shard_map/pallas_call | solution.py:713
  58.3 1.7 collective-permute-start.6
  61.4 1.8 all-to-all-done.got
  64.1 1.8 collective-permute-start.1
  65.9 1.9 %collective-permute-start.16 = (f32[2,32,8,128]{3,2,1,0:T(8,128)S(1)}, f32[2,32,8,128]{3,2,1,0:T(8,128)S(1)}, u32[]{:S(2)}, u32[]{:S(2)}) collective-permute-start(f32[2,32,8,128]{3,2,1,0:T(8,128)S(1)} %get-tuple-element.130), channel_id=1, source_target_pairs={{0,1},{1,0},{2,3},{3,2},{4,5},{5,4},{6,7},{7,6},{8,9},{9,8},{10,11... | collective-permute-start | bytes 786440 | tf_op jit(solution)/shard_map/ppermute | solution.py:197
  68.4 3.6 %collective-permute-done.2.refs_3_ = f32[2,32,8,128]{3,2,1,0:T(8,128)S(1)} collective-permute-done((f32[2,32,8,128]{3,2,1,0:T(8,128)S(1)}, f32[2,32,8,128]{3,2,1,0:T(8,128)S(1)}, u32[]{:S(2)}, u32[]{:S(2)}) %collective-permute-start.2) | collective-permute-done | bytes 262176 | tf_op jit(solution)/shard_map/ppermute | solution.py:201
  72.0 1.8 shard_map.164
  74.5 1.7 shard_map.168
  78.3 1.7 shard_map.165
  84.9 1.7 shard_map.166
  88.5 1.7 shard_map.170
  91.2 1.7 shard_map.167
  94.9 1.7 shard_map.171
  97.8 2.1 %shard_map.172 = (f32[32,16,128]{2,1,0:T(8,128)S(1)}, f32[32,32,128]{2,1,0:T(8,128)S(1)}, f32[1,32,8,128]{3,2,1,0:T(8,128)S(1)}, f32[1,32,8,128]{3,2,1,0:T(8,128)S(1)}, f32[2,32,16,128]{3,2,1,0:T(8,128)S(1)}) custom-call(s32[8]{0:T(128)S(1)} %stack.41.scal, f32[16]{0:T(128)S(1)} %copy-done.9, f32[32,16,128]{2,1,0:T(8,128)S(1)} %get-tuple-element.123.refs_1_, ...), custom_call_target="tpu_custom_call" | custom-call | flops 16777216 | bytes 4194304 | tf_op jit(solution)/shard_map/pallas_call | solution.py:766
  101.5 1.8 shard_map.176
  104.5 1.9 %shard_map.173 = (f32[32,16,128]{2,1,0:T(8,128)S(1)}, f32[32,32,128]{2,1,0:T(8,128)S(1)}, f32[1,32,8,128]{3,2,1,0:T(8,128)S(1)}, f32[1,32,8,128]{3,2,1,0:T(8,128)S(1)}, f32[2,32,16,128]{3,2,1,0:T(8,128)S(1)}) custom-call(s32[8]{0:T(128)S(1)} %stack.41.scal, f32[16]{0:T(128)S(1)} %copy-done.9, f32[32,16,128]{2,1,0:T(8,128)S(1)} %get-tuple-element.147.refs_1_, ...), custom_call_target="tpu_custom_call" | custom-call | flops 16777216 | bytes 4194304 | tf_op jit(solution)/shard_map/pallas_call | solution.py:766
  108.2 1.8 shard_map.177
  111.2 1.9 %shard_map.174 = (f32[32,16,128]{2,1,0:T(8,128)S(1)}, f32[32,32,128]{2,1,0:T(8,128)S(1)}, f32[1,32,8,128]{3,2,1,0:T(8,128)S(1)}, f32[1,32,8,128]{3,2,1,0:T(8,128)S(1)}, f32[2,32,16,128]{3,2,1,0:T(8,128)S(1)}) custom-call(s32[8]{0:T(128)S(1)} %stack.41.scal, f32[16]{0:T(128)S(1)} %copy-done.9, f32[32,16,128]{2,1,0:T(8,128)S(1)} %get-tuple-element.152.refs_1_, ...), custom_call_target="tpu_custom_call" | custom-call | flops 16777216 | bytes 4194304 | tf_op jit(solution)/shard_map/pallas_call | solution.py:766
  114.9 1.8 shard_map.178
  117.2 10.9 %shard_map.180.index = s32[2,40,128]{2,1,0:T(8,128)S(1)} custom-call(s32[8]{0:T(128)S(1)} %stack.41.scal, s32[32,128]{1,0:T(8,128)S(1)} %get-tuple-element.105.ids.ids_slab, s32[32,128]{1,0:T(8,128)S(1)} %get-tuple-element.187.ids_owner), custom_call_target="tpu_custom_call" | custom-call | flops 16777216 | bytes 262144 | tf_op jit(solution)/shard_map/pallas_call | solution.py:725
  128.2 2.2 %shard_map.175 = (f32[32,16,128]{2,1,0:T(8,128)S(1)}, f32[32,32,128]{2,1,0:T(8,128)}, f32[2,32,16,128]{3,2,1,0:T(8,128)S(1)}) custom-call(s32[8]{0:T(128)S(1)} %stack.41.scal, f32[16]{0:T(128)S(1)} %copy-done.9, f32[32,16,128]{2,1,0:T(8,128)S(1)} %get-tuple-element.157.refs_1_, f32[1,32,8,128]{3,2,1,0:T(8,128)S(1)} %collective-permute-done.28.refs_2_, ...), custom_call_target="tpu_custom_call" | custom-call | flops 16777216 | bytes 4194304 | tf_op jit(solution)/shard_map/pallas_call | solution.py:766
  130.4 2.3 %shard_map.179 = (f32[32,16,128]{2,1,0:T(8,128)S(1)}, f32[32,32,128]{2,1,0:T(8,128)}, f32[2,32,16,128]{3,2,1,0:T(8,128)S(1)}) custom-call(s32[8]{0:T(128)S(1)} %stack.41.scal, f32[16,32,128]{2,1,0:T(8,128)S(1)} %get-tuple-element.127.refs_0_, s32[32,128]{1,0:T(8,128)S(1)} %get-tuple-element.128.refs_1_, f32[32,16,128]{2,1,0:T(8,128)S(1)} %get-tuple-element.178.refs_2_, ...), custom_call_target="tpu_custom_call" | custom-call | flops 16777216 | bytes 4194304 | tf_op jit(solution)/shard_map/pallas_call | solution.py:766
  132.7 6.5 %shard_map.181 = f32[8,384,128]{2,1,0:T(8,128)} custom-call(s32[8]{0:T(128)S(1)} %stack.41.scal, f32[32,16,128]{2,1,0:T(8,128)S(1)} %get-tuple-element.162.u, f32[32,16,128]{2,1,0:T(8,128)S(1)} %get-tuple-element.184.a, f32[2,32,16,128]{3,2,1,0:T(8,128)S(1)} %get-tuple-element.185.total_u, f32[2,32,16,128]{3,2,1,0:T(8,128)S(1)} %get-tuple-element.186.total_a, ...), custom_call_target="tpu_custom_call" | custom-call | flops 16777216 | bytes 4194304 | tf_op jit(solution)/shard_map/pallas_call | solution.py:786
  139.2 3.7 %all-to-all-start.2 = ((f32[8,384,128]{2,1,0:T(8,128)}), f32[8,384,128]{2,1,0:T(8,128)S(1)}, u32[]{:S(2)}, u32[]{:S(2)}) async-start(f32[8,384,128]{2,1,0:T(8,128)} %shard_map.181), calls=%async_computation.2 | async-start | bytes 3145728 | tf_op jit(solution)/shard_map/all_to_all | solution.py:654
  142.9 37.1 %all-to-all-done.2 = f32[8,384,128]{2,1,0:T(8,128)S(1)} async-done(((f32[8,384,128]{2,1,0:T(8,128)}), f32[8,384,128]{2,1,0:T(8,128)S(1)}, u32[]{:S(2)}, u32[]{:S(2)}) %all-to-all-start.2) | async-done | bytes 1572896 | tf_op jit(solution)/shard_map/all_to_all | solution.py:654
  181.0 1.9 %collective-permute-done.38.other = f32[4,384,128]{2,1,0:T(8,128)S(1)} collective-permute-done((f32[4,384,128]{2,1,0:T(8,128)S(1)}, f32[4,384,128]{2,1,0:T(8,128)S(1)}, u32[]{:S(2)}, u32[]{:S(2)}) %collective-permute-start.38) | collective-permute-done | bytes 786464 | tf_op jit(solution)/shard_map/ppermute | solution.py:197
  182.9 3.0 %shard_map.182 = (f32[8,64,128]{2,1,0:T(8,128)}, f32[8,64,128]{2,1,0:T(8,128)}, f32[2048,128]{1,0:T(8,128)}) custom-call(s32[8]{0:T(128)S(1)} %stack.41.scal, f32[4,2,384,128]{3,2,1,0:T(8,128)S(1)} %bitcast.31, f32[4,384,128]{2,1,0:T(8,128)S(1)} %collective-permute-done.38.other, s32[2,40,128]{2,1,0:T(8,128)S(1)} %shard_map.180.index), custom_call_target="tpu_custom_call" | custom-call | flops 268435456 | bytes 4194304 | tf_op jit(solution)/shard_map/pallas_call | solution.py:796
  (122 shorter events, 43.0 us)
Async XLA Ops:
  9.2 24.9 %all-to-all-start.1 = ((f32[8,168,128]{2,1,0:T(8,128)}), f32[8,168,128]{2,1,0:T(8,128)S(1)}, u32[]{:S(2)}, u32[]{:S(2)}) async-start(f32[8,168,128]{2,1,0:T(8,128)} %pad_maximum_fusion.1), calls=%async_computation.1 | async-start | bytes 1376256 | tf_op jit(solution)/shard_map/all_to_all | solution.py:654
  34.0 29.1 %all-to-all-start = ((f32[8,4,4,16,128]{4,3,2,1,0:T(8,128)}), f32[8,4,4,16,128]{4,3,2,1,0:T(8,128)S(1)}, u32[]{:S(2)}, u32[]{:S(2)}) async-start(f32[8,4,4,16,128]{4,3,2,1,0:T(8,128)} %bitcast.7), calls=%async_computation | async-start | bytes 2097152 | tf_op jit(solution)/shard_map/all_to_all | solution.py:654
  38.1 12.8 %collective-permute-start.4 = (f32[8,4,32,128]{3,2,1,0:T(8,128)S(1)}, f32[8,4,32,128]{3,2,1,0:T(8,128)S(1)}, u32[]{:S(2)}, u32[]{:S(2)}) collective-permute-start(f32[8,4,32,128]{3,2,1,0:T(8,128)S(1)} %bitcast.32), channel_id=1, source_target_pairs={{0,16},{16,0},{1,17},{17,1},{2,18},{18,2},{3,19},{19,3},{4,20},{20... | collective-permute-start | bytes 1572872 | tf_op jit(solution)/shard_map/ppermute | solution.py:693
  58.3 9.5 %collective-permute-start.6 = (f32[32,16,128]{2,1,0:T(8,128)S(1)}, f32[32,16,128]{2,1,0:T(8,128)S(1)}, u32[]{:S(2)}, u32[]{:S(2)}) collective-permute-start(f32[32,16,128]{2,1,0:T(8,128)S(1)} %get-tuple-element.107), channel_id=1, source_target_pairs={{0,1},{1,0},{2,3},{3,2},{4,5},{5,4},{6,7},{7,6},{8,9},{9,8},{10,11... | collective-permute-start | bytes 786440 | tf_op jit(solution)/shard_map/ppermute | solution.py:197
  60.0 7.8 %collective-permute-start.7 = (f32[32,16,128]{2,1,0:T(8,128)S(1)}, f32[32,16,128]{2,1,0:T(8,128)S(1)}, u32[]{:S(2)}, u32[]{:S(2)}) collective-permute-start(f32[32,16,128]{2,1,0:T(8,128)S(1)} %get-tuple-element.108), channel_id=1, source_target_pairs={{1,4},{4,1},{5,8},{8,5},{9,12},{12,9},{13,14},{14,13},{15,10},{10,... | collective-permute-start | bytes 786440 | tf_op jit(solution)/shard_map/ppermute | solution.py:201
  64.1 4.3 %collective-permute-start.1 = (f32[2,32,8,128]{3,2,1,0:T(8,128)S(1)}, f32[2,32,8,128]{3,2,1,0:T(8,128)S(1)}, u32[]{:S(2)}, u32[]{:S(2)}) collective-permute-start(f32[2,32,8,128]{3,2,1,0:T(8,128)S(1)} %get-tuple-element.100), channel_id=1, source_target_pairs={{0,1},{1,0},{2,3},{3,2},{4,5},{5,4},{6,7},{7,6},{8,9},{9,8},{10,11... | collective-permute-start | bytes 786440 | tf_op jit(solution)/shard_map/ppermute | solution.py:197
  65.9 6.1 %collective-permute-start.2 = (f32[2,32,8,128]{3,2,1,0:T(8,128)S(1)}, f32[2,32,8,128]{3,2,1,0:T(8,128)S(1)}, u32[]{:S(2)}, u32[]{:S(2)}) collective-permute-start(f32[2,32,8,128]{3,2,1,0:T(8,128)S(1)} %get-tuple-element.101), channel_id=1, source_target_pairs={{1,4},{4,1},{5,8},{8,5},{9,12},{12,9},{13,14},{14,13},{15,10},{10,... | collective-permute-start | bytes 786440 | tf_op jit(solution)/shard_map/ppermute | solution.py:201
  65.9 8.0 %collective-permute-start.16 = (f32[2,32,8,128]{3,2,1,0:T(8,128)S(1)}, f32[2,32,8,128]{3,2,1,0:T(8,128)S(1)}, u32[]{:S(2)}, u32[]{:S(2)}) collective-permute-start(f32[2,32,8,128]{3,2,1,0:T(8,128)S(1)} %get-tuple-element.130), channel_id=1, source_target_pairs={{0,1},{1,0},{2,3},{3,2},{4,5},{5,4},{6,7},{7,6},{8,9},{9,8},{10,11... | collective-permute-start | bytes 786440 | tf_op jit(solution)/shard_map/ppermute | solution.py:197
  67.7 6.7 %collective-permute-start.17 = (f32[2,32,8,128]{3,2,1,0:T(8,128)S(1)}, f32[2,32,8,128]{3,2,1,0:T(8,128)S(1)}, u32[]{:S(2)}, u32[]{:S(2)}) collective-permute-start(f32[2,32,8,128]{3,2,1,0:T(8,128)S(1)} %get-tuple-element.131), channel_id=1, source_target_pairs={{1,4},{4,1},{5,8},{8,5},{9,12},{12,9},{13,14},{14,13},{15,10},{10,... | collective-permute-start | bytes 786440 | tf_op jit(solution)/shard_map/ppermute | solution.py:201
  73.8 4.5 %collective-permute-start.9 = (f32[1,32,8,128]{3,2,1,0:T(8,128)S(1)}, f32[1,32,8,128]{3,2,1,0:T(8,128)S(1)}, u32[]{:S(2)}, u32[]{:S(2)}) collective-permute-start(f32[1,32,8,128]{3,2,1,0:T(8,128)S(1)} %get-tuple-element.113), channel_id=1, source_target_pairs={{1,4},{4,1},{5,8},{8,5},{9,12},{12,9},{13,14},{14,13},{15,10},{10,... | collective-permute-start | bytes 393224 | tf_op jit(solution)/shard_map/ppermute | solution.py:201
  76.2 5.0 %collective-permute-start.18 = (f32[1,32,8,128]{3,2,1,0:T(8,128)S(1)}, f32[1,32,8,128]{3,2,1,0:T(8,128)S(1)}, u32[]{:S(2)}, u32[]{:S(2)}) collective-permute-start(f32[1,32,8,128]{3,2,1,0:T(8,128)S(1)} %get-tuple-element.134), channel_id=1, source_target_pairs={{0,1},{1,0},{2,3},{3,2},{4,5},{5,4},{6,7},{7,6},{8,9},{9,8},{10,11... | collective-permute-start | bytes 393224 | tf_op jit(solution)/shard_map/ppermute | solution.py:197
  77.5 4.4 %collective-permute-start.19 = (f32[1,32,8,128]{3,2,1,0:T(8,128)S(1)}, f32[1,32,8,128]{3,2,1,0:T(8,128)S(1)}, u32[]{:S(2)}, u32[]{:S(2)}) collective-permute-start(f32[1,32,8,128]{3,2,1,0:T(8,128)S(1)} %get-tuple-element.135), channel_id=1, source_target_pairs={{1,4},{4,1},{5,8},{8,5},{9,12},{12,9},{13,14},{14,13},{15,10},{10,... | collective-permute-start | bytes 393224 | tf_op jit(solution)/shard_map/ppermute | solution.py:201
  80.5 4.4 %collective-permute-start.11 = (f32[1,32,8,128]{3,2,1,0:T(8,128)S(1)}, f32[1,32,8,128]{3,2,1,0:T(8,128)S(1)}, u32[]{:S(2)}, u32[]{:S(2)}) collective-permute-start(f32[1,32,8,128]{3,2,1,0:T(8,128)S(1)} %get-tuple-element.117), channel_id=1, source_target_pairs={{1,4},{4,1},{5,8},{8,5},{9,12},{12,9},{13,14},{14,13},{15,10},{10,... | collective-permute-start | bytes 393224 | tf_op jit(solution)/shard_map/ppermute | solution.py:201
  83.6 4.2 %collective-permute-start.20 = (f32[1,32,8,128]{3,2,1,0:T(8,128)S(1)}, f32[1,32,8,128]{3,2,1,0:T(8,128)S(1)}, u32[]{:S(2)}, u32[]{:S(2)}) collective-permute-start(f32[1,32,8,128]{3,2,1,0:T(8,128)S(1)} %get-tuple-element.138), channel_id=1, source_target_pairs={{0,1},{1,0},{2,3},{3,2},{4,5},{5,4},{6,7},{7,6},{8,9},{9,8},{10,11... | collective-permute-start | bytes 393224 | tf_op jit(solution)/shard_map/ppermute | solution.py:197
  84.1 4.4 %collective-permute-start.21 = (f32[1,32,8,128]{3,2,1,0:T(8,128)S(1)}, f32[1,32,8,128]{3,2,1,0:T(8,128)S(1)}, u32[]{:S(2)}, u32[]{:S(2)}) collective-permute-start(f32[1,32,8,128]{3,2,1,0:T(8,128)S(1)} %get-tuple-element.139), channel_id=1, source_target_pairs={{1,4},{4,1},{5,8},{8,5},{9,12},{12,9},{13,14},{14,13},{15,10},{10,... | collective-permute-start | bytes 393224 | tf_op jit(solution)/shard_map/ppermute | solution.py:201
  86.8 4.4 %collective-permute-start.13 = (f32[1,32,8,128]{3,2,1,0:T(8,128)S(1)}, f32[1,32,8,128]{3,2,1,0:T(8,128)S(1)}, u32[]{:S(2)}, u32[]{:S(2)}) collective-permute-start(f32[1,32,8,128]{3,2,1,0:T(8,128)S(1)} %get-tuple-element.121), channel_id=1, source_target_pairs={{1,4},{4,1},{5,8},{8,5},{9,12},{12,9},{13,14},{14,13},{15,10},{10,... | collective-permute-start | bytes 393224 | tf_op jit(solution)/shard_map/ppermute | solution.py:201
  90.5 4.4 %collective-permute-start.23 = (f32[1,32,8,128]{3,2,1,0:T(8,128)S(1)}, f32[1,32,8,128]{3,2,1,0:T(8,128)S(1)}, u32[]{:S(2)}, u32[]{:S(2)}) collective-permute-start(f32[1,32,8,128]{3,2,1,0:T(8,128)S(1)} %get-tuple-element.143), channel_id=1, source_target_pairs={{1,4},{4,1},{5,8},{8,5},{9,12},{12,9},{13,14},{14,13},{15,10},{10,... | collective-permute-start | bytes 393224 | tf_op jit(solution)/shard_map/ppermute | solution.py:201
  93.4 4.4 %collective-permute-start.15 = (f32[1,32,8,128]{3,2,1,0:T(8,128)S(1)}, f32[1,32,8,128]{3,2,1,0:T(8,128)S(1)}, u32[]{:S(2)}, u32[]{:S(2)}) collective-permute-start(f32[1,32,8,128]{3,2,1,0:T(8,128)S(1)} %get-tuple-element.125), channel_id=1, source_target_pairs={{1,4},{4,1},{5,8},{8,5},{9,12},{12,9},{13,14},{14,13},{15,10},{10,... | collective-permute-start | bytes 393224 | tf_op jit(solution)/shard_map/ppermute | solution.py:201
  96.6 4.5 %collective-permute-start.30 = (f32[1,32,8,128]{3,2,1,0:T(8,128)S(1)}, f32[1,32,8,128]{3,2,1,0:T(8,128)S(1)}, u32[]{:S(2)}, u32[]{:S(2)}) collective-permute-start(f32[1,32,8,128]{3,2,1,0:T(8,128)S(1)} %get-tuple-element.163), channel_id=1, source_target_pairs={{0,1},{1,0},{2,3},{3,2},{4,5},{5,4},{6,7},{7,6},{8,9},{9,8},{10,11... | collective-permute-start | bytes 393224 | tf_op jit(solution)/shard_map/ppermute | solution.py:197
  97.1 4.4 %collective-permute-start.31 = (f32[1,32,8,128]{3,2,1,0:T(8,128)S(1)}, f32[1,32,8,128]{3,2,1,0:T(8,128)S(1)}, u32[]{:S(2)}, u32[]{:S(2)}) collective-permute-start(f32[1,32,8,128]{3,2,1,0:T(8,128)S(1)} %get-tuple-element.164), channel_id=1, source_target_pairs={{1,4},{4,1},{5,8},{8,5},{9,12},{12,9},{13,14},{14,13},{15,10},{10,... | collective-permute-start | bytes 393224 | tf_op jit(solution)/shard_map/ppermute | solution.py:201
  100.1 4.4 %collective-permute-start.25 = (f32[1,32,8,128]{3,2,1,0:T(8,128)S(1)}, f32[1,32,8,128]{3,2,1,0:T(8,128)S(1)}, u32[]{:S(2)}, u32[]{:S(2)}) collective-permute-start(f32[1,32,8,128]{3,2,1,0:T(8,128)S(1)} %get-tuple-element.149), channel_id=1, source_target_pairs={{1,4},{4,1},{5,8},{8,5},{9,12},{12,9},{13,14},{14,13},{15,10},{10,... | collective-permute-start | bytes 393224 | tf_op jit(solution)/shard_map/ppermute | solution.py:201
  103.3 4.6 %collective-permute-start.32 = (f32[1,32,8,128]{3,2,1,0:T(8,128)S(1)}, f32[1,32,8,128]{3,2,1,0:T(8,128)S(1)}, u32[]{:S(2)}, u32[]{:S(2)}) collective-permute-start(f32[1,32,8,128]{3,2,1,0:T(8,128)S(1)} %get-tuple-element.167), channel_id=1, source_target_pairs={{0,1},{1,0},{2,3},{3,2},{4,5},{5,4},{6,7},{7,6},{8,9},{9,8},{10,11... | collective-permute-start | bytes 393224 | tf_op jit(solution)/shard_map/ppermute | solution.py:197
  103.8 4.4 %collective-permute-start.33 = (f32[1,32,8,128]{3,2,1,0:T(8,128)S(1)}, f32[1,32,8,128]{3,2,1,0:T(8,128)S(1)}, u32[]{:S(2)}, u32[]{:S(2)}) collective-permute-start(f32[1,32,8,128]{3,2,1,0:T(8,128)S(1)} %get-tuple-element.168), channel_id=1, source_target_pairs={{1,4},{4,1},{5,8},{8,5},{9,12},{12,9},{13,14},{14,13},{15,10},{10,... | collective-permute-start | bytes 393224 | tf_op jit(solution)/shard_map/ppermute | solution.py:201
  106.3 4.2 %collective-permute-start.26 = (f32[1,32,8,128]{3,2,1,0:T(8,128)S(1)}, f32[1,32,8,128]{3,2,1,0:T(8,128)S(1)}, u32[]{:S(2)}, u32[]{:S(2)}) collective-permute-start(f32[1,32,8,128]{3,2,1,0:T(8,128)S(1)} %get-tuple-element.153), channel_id=1, source_target_pairs={{0,1},{1,0},{2,3},{3,2},{4,5},{5,4},{6,7},{7,6},{8,9},{9,8},{10,11... | collective-permute-start | bytes 393224 | tf_op jit(solution)/shard_map/ppermute | solution.py:197
  106.8 4.4 %collective-permute-start.27 = (f32[1,32,8,128]{3,2,1,0:T(8,128)S(1)}, f32[1,32,8,128]{3,2,1,0:T(8,128)S(1)}, u32[]{:S(2)}, u32[]{:S(2)}) collective-permute-start(f32[1,32,8,128]{3,2,1,0:T(8,128)S(1)} %get-tuple-element.154), channel_id=1, source_target_pairs={{1,4},{4,1},{5,8},{8,5},{9,12},{12,9},{13,14},{14,13},{15,10},{10,... | collective-permute-start | bytes 393224 | tf_op jit(solution)/shard_map/ppermute | solution.py:201
  110.0 4.3 %collective-permute-start.34 = (f32[1,32,8,128]{3,2,1,0:T(8,128)S(1)}, f32[1,32,8,128]{3,2,1,0:T(8,128)S(1)}, u32[]{:S(2)}, u32[]{:S(2)}) collective-permute-start(f32[1,32,8,128]{3,2,1,0:T(8,128)S(1)} %get-tuple-element.173), channel_id=1, source_target_pairs={{0,1},{1,0},{2,3},{3,2},{4,5},{5,4},{6,7},{7,6},{8,9},{9,8},{10,11... | collective-permute-start | bytes 393224 | tf_op jit(solution)/shard_map/ppermute | solution.py:197
  110.5 4.4 %collective-permute-start.35 = (f32[1,32,8,128]{3,2,1,0:T(8,128)S(1)}, f32[1,32,8,128]{3,2,1,0:T(8,128)S(1)}, u32[]{:S(2)}, u32[]{:S(2)}) collective-permute-start(f32[1,32,8,128]{3,2,1,0:T(8,128)S(1)} %get-tuple-element.174), channel_id=1, source_target_pairs={{1,4},{4,1},{5,8},{8,5},{9,12},{12,9},{13,14},{14,13},{15,10},{10,... | collective-permute-start | bytes 393224 | tf_op jit(solution)/shard_map/ppermute | solution.py:201
  113.1 15.1 %collective-permute-start.28 = (f32[1,32,8,128]{3,2,1,0:T(8,128)S(1)}, f32[1,32,8,128]{3,2,1,0:T(8,128)S(1)}, u32[]{:S(2)}, u32[]{:S(2)}) collective-permute-start(f32[1,32,8,128]{3,2,1,0:T(8,128)S(1)} %get-tuple-element.158), channel_id=1, source_target_pairs={{0,1},{1,0},{2,3},{3,2},{4,5},{5,4},{6,7},{7,6},{8,9},{9,8},{10,11... | collective-permute-start | bytes 393224 | tf_op jit(solution)/shard_map/ppermute | solution.py:197
  113.2 14.9 %collective-permute-start.29 = (f32[1,32,8,128]{3,2,1,0:T(8,128)S(1)}, f32[1,32,8,128]{3,2,1,0:T(8,128)S(1)}, u32[]{:S(2)}, u32[]{:S(2)}) collective-permute-start(f32[1,32,8,128]{3,2,1,0:T(8,128)S(1)} %get-tuple-element.159), channel_id=1, source_target_pairs={{1,4},{4,1},{5,8},{8,5},{9,12},{12,9},{13,14},{14,13},{15,10},{10,... | collective-permute-start | bytes 393224 | tf_op jit(solution)/shard_map/ppermute | solution.py:201
  116.8 13.6 %collective-permute-start.36 = (f32[1,32,8,128]{3,2,1,0:T(8,128)S(1)}, f32[1,32,8,128]{3,2,1,0:T(8,128)S(1)}, u32[]{:S(2)}, u32[]{:S(2)}) collective-permute-start(f32[1,32,8,128]{3,2,1,0:T(8,128)S(1)} %get-tuple-element.179), channel_id=1, source_target_pairs={{0,1},{1,0},{2,3},{3,2},{4,5},{5,4},{6,7},{7,6},{8,9},{9,8},{10,11... | collective-permute-start | bytes 393224 | tf_op jit(solution)/shard_map/ppermute | solution.py:197
  117.0 13.4 %collective-permute-start.37 = (f32[1,32,8,128]{3,2,1,0:T(8,128)S(1)}, f32[1,32,8,128]{3,2,1,0:T(8,128)S(1)}, u32[]{:S(2)}, u32[]{:S(2)}) collective-permute-start(f32[1,32,8,128]{3,2,1,0:T(8,128)S(1)} %get-tuple-element.180), channel_id=1, source_target_pairs={{1,4},{4,1},{5,8},{8,5},{9,12},{12,9},{13,14},{14,13},{15,10},{10,... | collective-permute-start | bytes 393224 | tf_op jit(solution)/shard_map/ppermute | solution.py:201
  139.2 40.8 %all-to-all-start.2 = ((f32[8,384,128]{2,1,0:T(8,128)}), f32[8,384,128]{2,1,0:T(8,128)S(1)}, u32[]{:S(2)}, u32[]{:S(2)}) async-start(f32[8,384,128]{2,1,0:T(8,128)} %shard_map.181), calls=%async_computation.2 | async-start | bytes 3145728 | tf_op jit(solution)/shard_map/all_to_all | solution.py:654
  (20 other events, 162.8 us)

commit v2 on v1

--- a/solution.py
+++ b/solution.py
@@ -160,6 +160,7 @@
 HALO = 8
 OWN = slice(HALO, HALO + ZS)
 SCALE = 5040.0
+UNSCALE = 1.0
 PADX = 4
 STEPS = 16
 ROUNDS = STEPS // 2
@@ -199,6 +200,28 @@
 
 def to_off_chip(x):
     return lax.ppermute(x, ("gx", "gy", "gz"), OFF_PAIRS)
+
+
+def spread(e):
+    return [(2 * s + c, 2 * (s ^ e ^ c) + (s & 1)) for s in range(GX * GY) for c in range(2)]
+
+
+def to_blocks(x, e):
+    return lax.ppermute(x, ("gx", "gy", "gz"), spread(e))
+
+
+FAR_FIRST = (6, 7, 4, 5, 2, 3, 0, 1)
+
+
+def slab_of(scal, e):
+    ix = scal[IX] ^ (e >> 1)
+    core = scal[IY] ^ (e & 1) ^ scal[H]
+    chip = jnp.where(scal[H] == 0, ix, GX - 1 - ix)
+    return pl.multiple_of(chip * 2 * ZS + core * ZS, ZS)
+
+
+def block_of(scal, e):
+    return (scal[IX] * GY + scal[IY]) ^ e ^ scal[H]
 
 
 def band(size):
@@ -254,23 +277,47 @@
     return mine, jnp.where(scal[H] == 0, chip, GX - 1 - chip)
 
 
+def pack_small(owner, slot, depth, traces, out):
+    for tt in range(4):
+        out[tt] = jnp.concatenate([traces[2 * tt], traces[2 * tt + 1]], axis=1)
+    low = half_lanes((1, 128))
+    ids = owner[...] * 1024 + slot[...]
+    rows = []
+    for x in range(BX):
+        pair = ids[:, (x // 2) * 128 : (x // 2 + 1) * 128].astype(F32)
+        rows.append(roll_half(pair) if x % 2 else pair)
+    rows = jnp.concatenate(rows, axis=0)
+    depths = depth[...].astype(F32)
+    depths = jnp.concatenate([depths, depths], axis=1)
+    out[4] = jnp.where(half_lanes((8, 128)), rows, depths)
+
+
 def pack_table(scal, table, keep, give):
     first = scal[SHOT] * 1024
     for q in range(4):
         for comp in range(2):
-            rows = table[pl.ds(first + q * 256 + comp, 128, stride=2), :]
-            turned = rows.T
+            turned = table[pl.ds(first + q * 256 + comp, 128, stride=2), :].T
+            at = q * 32 + comp * ZS
             for chunk in range(8):
                 mine, g = place(scal, chunk)
                 piece = turned[chunk * ZS : (chunk + 1) * ZS][None]
 
                 @pl.when(mine)
                 def _():
-                    keep[pl.ds(g, 1), q, comp * ZS : (comp + 1) * ZS, :] = piece
+                    keep[pl.ds(g, 1), at : at + ZS, :] = piece
 
                 @pl.when(jnp.logical_not(mine))
                 def _():
-                    give[pl.ds(g, 1), q, comp * ZS : (comp + 1) * ZS, :] = piece
+                    give[pl.ds(g, 1), at : at + ZS, :] = piece
+
+
+def assemble(scal, keep, got, small, out):
+    h = scal[H]
+    for ix in range(GX):
+        out[pl.ds(ix * GY + h, 1), 0:128, :] = keep[ix][None]
+        out[pl.ds(ix * GY + 1 - h, 1), 0:128, :] = got[ix][None]
+    for n in range(GX * GY):
+        out[n, 128:, :] = small[...].reshape(40, 128)
 
 
 def pack_fields(scal, *refs):
@@ -324,16 +371,14 @@
 
     def column(x, carry):
         row = ids[pl.ds(x, 1), :]
-        chunk = row >> 7
-        local = jnp.where(((chunk >> 2) & 1) == half, ((chunk >> 3) << 2) | (chunk & 3), -1)
         lane = jnp.broadcast_to(row & 127, (8, 128))
-        local = jnp.broadcast_to(local, (8, 128))
+        chunk = jnp.broadcast_to(row >> 7, (8, 128))
         if second:
             totals = [before[x, 8 * t : 8 * t + 8, :] for t in range(4)]
         else:
             totals = [jnp.zeros((8, 128), F32) for t in range(4)]
         for j in range(32):
-            hit = local == j
+            hit = chunk == (j // 4) * 8 + half * 4 + j % 4
             for t in range(4):
                 value = jnp.take_along_axis(
                     table[j // 4, j % 4, 8 * t : 8 * t + 8, :], lane, axis=1, mode="promise_in_bounds"
@@ -385,50 +430,53 @@
             off[step] = own[:, pl.ds(HALO * h, HALO), :]
 
 
-def ranks_of(owner, owners):
-    masks = jnp.concatenate(
-        [(owner[ix * BX : (ix + 1) * BX] == o).astype(F32) for ix in range(GX) for o in owners], axis=0
-    )
-    rows = masks.shape[0]
+def index_kernel(scal, ids_slab, ids_owner, out):
+    me = scal[IX] * GY + scal[IY]
+    sub = lax.broadcasted_iota(jnp.int32, (8, 128), 0)
+    lane = lax.broadcasted_iota(jnp.int32, (8, 128), 1)
+    slots = []
+    masks = [(jnp.broadcast_to(ids_slab[x : x + 1, :] >> 10, (8, 128)) == sub).astype(F32) for x in range(NXA)]
+    for x in range(BX):
+        rows = jnp.concatenate([ids_owner[s * BX + x : s * BX + x + 1, :] for s in range(GX)] * 2, axis=0)
+        masks.append((((rows >> 10) == me) & (sub < GX)).astype(F32))
+        slots.append((rows & 1023).astype(F32))
+    bits = jnp.concatenate(masks, axis=0).astype(BF16)
     first = lax.broadcasted_iota(jnp.int32, (128, 128), 0)
     second = lax.broadcasted_iota(jnp.int32, (128, 128), 1)
-    before = (first < second).astype(F32).astype(BF16)
-    bits = masks.astype(BF16)
-    along = jnp.dot(bits, before, preferred_element_type=F32)
+    upto = (first <= second).astype(F32).astype(BF16)
+    along = jnp.dot(bits, upto, preferred_element_type=F32)
     sums = jnp.dot(bits, jnp.ones((128, 128), BF16), preferred_element_type=F32)
-    r0 = lax.broadcasted_iota(jnp.int32, (rows, rows), 0)
-    r1 = lax.broadcasted_iota(jnp.int32, (rows, rows), 1)
-    earlier = (((r0 >> 3) == (r1 >> 3)) & (r1 < r0)).astype(F32).astype(BF16)
-    above = jnp.dot(earlier, sums.astype(BF16), preferred_element_type=F32)
-    return jnp.where(masks > 0.0, along + above, -1.0).astype(jnp.int32)
-
-
-def index_kernel(scal, ids_slab, ids_owner, out, ranks, acc):
-    me = scal[IX] * GY + scal[IY]
-    ranks[0:256] = ranks_of(ids_slab[...] >> 10, list(range(8)))
-    ranks[256:288] = ranks_of(ids_owner[...] >> 10, [me])
-    acc[...] = jnp.full((256, 128), -1, jnp.int32)
-    lanes = lax.broadcasted_iota(jnp.int32, (256, 128), 1)
-    places = lax.broadcasted_iota(jnp.int32, (256, 128), 0)
-
-    def combo(n, carry):
-        is_slab = n < 32
-        ix = jnp.where(is_slab, n >> 3, n - 32)
-        found = jnp.full((256, 128), -1, jnp.int32)
-        for x in range(BX):
-            row = jnp.broadcast_to(ranks[pl.ds(n * BX + x, 1), :], (256, 128))
-            slots = ids_owner[pl.ds(ix * BX + x, 1), :] & 1023
-            column = x * 128 + lax.broadcasted_iota(jnp.int32, (1, 128), 1)
-            value = jnp.broadcast_to(jnp.where(is_slab, column, slots), (256, 128))
-            found = jnp.where(row == places, value, found)
-        best = jnp.max(found, axis=1, keepdims=True)
-        acc[...] = jnp.where(lanes == n, jnp.broadcast_to(best, (256, 128)), acc[...])
-        return carry
-
-    lax.fori_loop(0, 36, combo, 0)
-    turned = acc[...].astype(F32).T[0:40].astype(jnp.int32)
-    out[0] = turned[:, 0:128]
-    out[1] = turned[:, 128:256]
+    r0 = lax.broadcasted_iota(jnp.int32, (64, 64), 0)
+    r1 = lax.broadcasted_iota(jnp.int32, (64, 64), 1)
+    earlier = (((r0 & 7) == (r1 & 7)) & (r1 < r0)).astype(F32).astype(BF16)
+    for group in range(GX + 1):
+        rows = slice(64 * group, 64 * group + 64)
+        above = jnp.dot(earlier, sums[rows].astype(BF16), preferred_element_type=F32)
+        counts = along[rows] + above
+        ends = sums[rows] + above
+        for part in range(2):
+            r = (lane + 128 * part).astype(F32)
+            at_x = jnp.zeros((8, 128), jnp.int32)
+            for x in range(BX):
+                at_x = at_x + (ends[8 * x : 8 * x + 8] <= r).astype(jnp.int32)
+
+            def pick(tables, at):
+                value = jnp.zeros((8, 128), F32)
+                for x in range(BX):
+                    taken = jnp.take_along_axis(tables[x], at, axis=1, mode="promise_in_bounds")
+                    value = jnp.where(at_x == x, taken, value)
+                return value
+
+            tables = [counts[8 * x : 8 * x + 8] for x in range(BX)]
+            at_y = jnp.zeros((8, 128), jnp.int32)
+            for step in (64, 32, 16, 8, 4, 2, 1):
+                at_y = jnp.where(pick(tables, at_y + (step - 1)) <= r, at_y + step, at_y)
+            at_y = jnp.minimum(at_y, 127)
+            if group < GX:
+                found = at_x * 128 + at_y
+            else:
+                found = pick(slots, at_y).astype(jnp.int32)
+            out[part, 8 * group : 8 * group + 8] = jnp.where(at_x < BX, found, -1)
 
 
 def stencil(field, g, along_y, along_z, own):
@@ -565,77 +613,75 @@
         out_off[0] = out_own[:, pl.ds(HALO * h, HALO), :]
 
 
-def pack_out(scal, u, a, total_u, total_a, coefs, index, out, grads):
+def pack_out(scal, u, a, index, total_u, total_a, coefs, *refs):
+    outs, grads = refs[:8], refs[8]
     for x in range(NXA):
-        gh = total_u[0, x] + total_a[0, x]
-        gv = total_u[1, x] + total_a[1, x]
+        gh = (total_u[0, x] + total_a[0, x]) * UNSCALE
+        gv = (total_u[1, x] + total_a[1, x]) * UNSCALE
         slow, aniso = coefs[x, 0:ZS, :], coefs[x, ZS:, :]
         grads[x, 0:ZS, :] = (1.0 + 2.0 * aniso) * gh + gv
         grads[x, ZS:, :] = (2.0 * slow) * gh
     low = half_lanes((ZS, 128))
-    for f, field in enumerate((u, a)):
-        for ix in range(GX):
+    for n, out in enumerate(outs):
+        block = block_of(scal, FAR_FIRST[n])
+        for f, field in enumerate((u, a)):
             for i in range(4):
-                x0, x1 = field[ix * BX + 2 * i], field[ix * BX + 2 * i + 1]
+                x = (block >> 1) * BX + 2 * i
+                x0 = field[pl.ds(x, 1)].reshape(ZS, 128)
+                x1 = field[pl.ds(x + 1, 1)].reshape(ZS, 128)
+                piece = jnp.where(low, x0, roll_half(x1))
+                upper = jnp.where(low, roll_half(x0), x1)
                 at = 256 + (f * 4 + i) * ZS
-                out[ix * GY, at : at + ZS, :] = jnp.where(low, x0, roll_half(x1))
-                out[ix * GY + 1, at : at + ZS, :] = jnp.where(low, roll_half(x0), x1)
-
-    def combo(n, carry):
-        ix, o = n >> 3, n & 7
-        for part in range(2):
-            row = index[part, pl.ds(n, 1), :]
-            lane = jnp.broadcast_to(row & 127, (8, 128))
-            which = jnp.broadcast_to(row >> 7, (8, 128))
-            totals = [jnp.zeros((8, 128), F32) for t in range(4)]
-            for x in range(BX):
-                hit = which == x
+                out[at : at + ZS, :] = jnp.where((block & 1) == 0, piece, upper)
+
+        def stripe(ix, carry, out=out, block=block):
+            for part in range(2):
+                row = index[part, pl.ds(ix * 8 + block, 1), :]
+                lane = jnp.broadcast_to(row & 127, (8, 128))
+                which = jnp.broadcast_to(row >> 7, (8, 128))
+                totals = [jnp.zeros((8, 128), F32) for t in range(4)]
+                for x in range(BX):
+                    hit = which == x
+                    for t in range(4):
+                        value = jnp.take_along_axis(
+                            grads[ix * BX + x, 8 * t : 8 * t + 8, :], lane, axis=1, mode="promise_in_bounds"
+                        )
+                        totals[t] = jnp.where(hit, value, totals[t])
                 for t in range(4):
-                    value = jnp.take_along_axis(
-                        grads[ix * BX + x, 8 * t : 8 * t + 8, :], lane, axis=1, mode="promise_in_bounds"
-                    )
-                    totals[t] = jnp.where(hit, value, totals[t])
-            for t in range(4):
-                at = pl.multiple_of((ix * 2 + part) * 32 + 8 * t, 8)
-                out[o, pl.ds(at, 8), :] = totals[t]
-        return carry
-
-    lax.fori_loop(0, 32, combo, 0)
-
-
-def finish(scal, got, other, index, u_out, a_out, model, turned, columns):
-    h = scal[H]
-    sources = []
-    for ix in range(GX):
-        chip = jnp.where(h == 0, ix, GX - 1 - ix)
-        base = chip * 2 * ZS
-        sources.append((got, ix, True, base + h * ZS))
-        sources.append((other, ix, False, base + (1 - h) * ZS))
-
-    def piece(ref, ix, mine, start, count):
-        if mine:
-            return ref[ix, pl.ds(h, 1), start : start + count, :].reshape(count, 128)
-        return ref[ix, start : start + count, :]
-
+                    at = pl.multiple_of((ix * 2 + part) * 32 + 8 * t, 8)
+                    out[pl.ds(at, 8), :] = totals[t]
+            return carry
+
+        lax.fori_loop(0, GX, stripe, 0)
+
+
+def name_slots(index, picks):
+    named = jnp.concatenate([index[n % 2, 32 + n // 2 : 33 + n // 2, :] for n in range(8)], axis=1)
+    for block in range(4):
+        slot = lax.broadcasted_iota(jnp.int32, (256, 1024), 0) + block * 256
+        pick = slot == jnp.broadcast_to(named, (256, 1024))
+        picks[block * 256 : (block + 1) * 256, :] = pick.astype(F32).astype(BF16)
+
+
+def finish(scal, picks, *refs):
+    gots, (u_out, a_out, model, turned, columns) = refs[:8], refs[8:]
     for f, out in enumerate((u_out, a_out)):
         for i in range(4):
-            for ref, ix, mine, z0 in sources:
-                turned[pl.ds(pl.multiple_of(z0, ZS), ZS), :] = piece(ref, ix, mine, 256 + (f * 4 + i) * ZS, ZS)
+            for n, e in enumerate(FAR_FIRST):
+                at = 256 + (f * 4 + i) * ZS
+                turned[pl.ds(slab_of(scal, e), ZS), :] = gots[n][at : at + ZS, :]
             out[2 * i : 2 * i + 2] = turned[...].T.reshape(2, BY, 128)
-    for n in range(8):
-        for comp in range(2):
-            for ref, ix, mine, z0 in sources:
-                rows = pl.ds(pl.multiple_of(comp * 128 + z0, ZS), ZS)
-                columns[rows, n * 128 : (n + 1) * 128] = piece(ref, ix, mine, n * 32 + comp * ZS, ZS)
+    for n, e in enumerate(FAR_FIRST):
+        for m in range(8):
+            for comp in range(2):
+                rows = pl.ds(pl.multiple_of(comp * 128 + slab_of(scal, e), ZS), ZS)
+                at = m * 32 + comp * ZS
+                columns[rows, m * 128 : (m + 1) * 128] = gots[n][at : at + ZS, :]
     values = columns[...]
     high = values.astype(BF16)
     rest = (values - high.astype(F32)).astype(BF16)
-    named = jnp.concatenate(
-        [index[n % 2, 32 + n // 2 : 33 + n // 2, :] for n in range(8)], axis=1
-    )
     for block in range(4):
-        slot = lax.broadcasted_iota(jnp.int32, (256, 1024), 0) + block * 256
-        pick = (slot == jnp.broadcast_to(named, (256, 1024))).astype(F32).astype(BF16)
+        pick = picks[block * 256 : (block + 1) * 256, :]
         dims = (((1,), (1,)), ((), ()))
         sums = lax.dot_general(pick, high, dims, preferred_element_type=F32)
         sums = sums + lax.dot_general(pick, rest, dims, preferred_element_type=F32)
@@ -675,21 +721,19 @@
         [h, ix, iy, lax.axis_index("shots"), line, source_index[0], source_index[1], source_index[2]]
     ).astype(jnp.int32)
 
-    table = model_table.reshape(2048, 128)
+    trace_half = lax.dynamic_slice_in_dim(traces, h * 8, 8, axis=0)
+    (small,) = call(pack_small, [((5, BX, 128), F32)], vmem(4), moved=MIB // 16, flops=1 << 16)(
+        tile_owner.reshape(1, BX * BY), tile_slot.reshape(1, BX * BY), receiver_depth, trace_half
+    )
     keep, give = call(
-        pack_table, [((4, 4, 32, 128), F32)] * 2, [SMEM] + vmem(1), moved=2 * MIB, flops=1 << 20
-    )(scal, table)
-    table_chunks = by_half(h, keep, to_sibling(give))
-    ids = (tile_owner.reshape(BX, BY) * 1024 + tile_slot.reshape(BX, BY)).astype(F32)
-    small = jnp.concatenate([ids, receiver_depth.astype(F32)], axis=1)[None]
-    trace_half = lax.dynamic_slice_in_dim(traces, h * 8, 8, axis=0).reshape(4, 2, BX, BY)
-    trace_half = trace_half.transpose(0, 2, 1, 3).reshape(4, BX, 128)
-    small = jnp.concatenate([trace_half, small], axis=0).reshape(1, 40, 128)
-    small = jnp.broadcast_to(small, (8, 40, 128))
-    sent = jnp.concatenate([table_chunks.reshape(8, 128, 128), small], axis=1)
+        pack_table, [((GX, 128, 128), F32)] * 2, [SMEM] + vmem(1), moved=2 * MIB, flops=1 << 20
+    )(scal, model_table.reshape(2048, 128))
+    (sent,) = call(assemble, [((GX * GY, 168, 128), F32)], [SMEM] + vmem(3), moved=2 * MIB, flops=1 << 20)(
+        scal, keep, to_sibling(give), small
+    )
     arrived = exchange(sent)
     table_mine = arrived[:, :128].reshape(8, 4, 32, 128)
-    small_mine = arrived[:, 128:].reshape(8, 5, 8, 128)
+    small_mine = arrived[:, 128:].reshape(8, 5, BX, 128)
     table_other = lax.ppermute(table_mine, "shots", SWAP)
     small_other = to_sibling(small_mine)
 
@@ -726,11 +770,11 @@
         index_kernel,
         [((2, 40, 128), jnp.int32)],
         [SMEM] + vmem(2),
-        [pltpu.VMEM((288, 128), jnp.int32), pltpu.VMEM((256, 128), jnp.int32)],
         moved=MIB // 4,
         flops=1 << 24,
     )(scal, ids_slab, ids_owner)
 
+    fields, index = lax.optimization_barrier((fields, index))
     first_halo = ((2, NXA, HALO, 128), F32)
     unpacked = call(
         unpack_fields,
@@ -783,24 +827,25 @@
             else:
                 state[kind] = [own, to_sibling(res[2]), to_off_chip(res[3]), mid]
 
-    (packed,) = call(
+    packed = call(
         pack_out,
-        [((8, 384, 128), F32)],
+        [((384, 128), F32)] * 8,
         [SMEM] + vmem(6),
         [pltpu.VMEM((NXA, 2 * ZS, 128), F32)],
         moved=4 * MIB,
-        flops=1 << 24,
-    )(scal, state["u"][0], state["a"][0], totals["u"], totals["a"], coefs, index)
-    got = exchange(packed).reshape(GX, GY, 384, 128)
-    other = to_sibling(lax.dynamic_index_in_dim(got, 1 - h, axis=1, keepdims=False))
+        flops=1 << 22,
+    )(scal, state["u"][0], state["a"][0], index, totals["u"], totals["a"], coefs)
+    index, _ = lax.optimization_barrier((index, packed[7]))
+    (picks,) = call(name_slots, [((1024, 1024), BF16)], vmem(1), moved=4 * MIB, flops=1 << 22)(index)
+    arrived = [to_blocks(x, e) for x, e in zip(packed, FAR_FIRST)]
     u, a, model = call(
         finish,
         [((BX, BY, BZ), F32)] * 2 + [((2048, 128), F32)],
-        [SMEM] + vmem(3),
+        [SMEM] + vmem(9),
         [pltpu.VMEM((128, 128), F32), pltpu.VMEM((256, 1024), F32)],
         moved=4 * MIB,
         flops=1 << 28,
-    )(scal, got, other, index)
+    )(scal, picks, *arrived)
     return (u, a, model.reshape(1, 1024, 2, 128))
 
 

time: 187 us -> 172 us (0.920)
  waiting for transfers between devices: 67.8 us -> 35 us
  starting transfers between devices: 37.5 us -> 67.3 us
  Pallas kernels: 71.6 us -> 63.3 us
  other arithmetic: 4.02 us -> 0.21 us
    all_to_all x3 -> x2, waiting for transfers between devices: 50.9 us -> 11.9 us  [exchange(): lax.all_to_all(x, ('gx', 'gy'), split_axis=0, concat_axis=0, tiled=True)]
    ppermute x0 -> x8, starting transfers between devices: none -> 29.6 us  [to_blocks(): return lax.ppermute(x, ('gx', 'gy', 'gz'), spread(e))]
    ppermute x0 -> x8, waiting for transfers between devices: none -> 11.4 us  [to_blocks(): return lax.ppermute(x, ('gx', 'gy', 'gz'), spread(e))]
    pallas_call x3 -> x6, Pallas kernels: 19 us -> 11.1 us  [the longest x1 5.75 us: slab_body(): call(pack_out, [((384, 128), F32)] * 8, [SMEM] + vmem(6), [pltpu.VMEM((NX...]
    ppermute x17, starting transfers between devices: 7.74 us -> 13.7 us  [to_off_chip(): return lax.ppermute(x, ('gx', 'gy', 'gz'), OFF_PAIRS)]
    all_to_all x3 -> x2, starting transfers between devices: 14.7 us -> 11 us  [exchange(): lax.all_to_all(x, ('gx', 'gy'), split_axis=0, concat_axis=0, tiled=True)]
    ppermute x17, waiting for transfers between devices: 11.5 us -> 8.2 us  [to_off_chip(): return lax.ppermute(x, ('gx', 'gy', 'gz'), OFF_PAIRS)]
    ppermute x21 -> x20, starting transfers between devices: 13.7 us -> 11.7 us  [to_sibling(): return lax.ppermute(x, 'gz', SWAP)]
  transfers between devices with their start and end apart: 42 -> 48, of which waited for: 21 -> 23; matrix products, arithmetic and copies ran while one was open for 3% -> 1% of each run, Pallas kernels for 31% -> 29%
where the time goes in v2:
time: 172 us
  starting transfers between devices  67.3 us (39%)
  Pallas kernels  63.3 us (37%)
  waiting for transfers between devices  35 us (20%)
  local copies, waits for them, and re-layouts  5.19 us (3%)
    ppermute x8, starting transfers between devices, to_blocks(): return lax.ppermute(x, ('gx', 'gy', 'gz'), spread(e))  29.6 us
    pallas_call x16, Pallas kernels, slab_body(): call(functools.partial(round_kernel, kind, r), outs, specs, [pltpu.VMEM((...  29.3 us
    ppermute x17, starting transfers between devices, to_off_chip(): return lax.ppermute(x, ('gx', 'gy', 'gz'), OFF_PAIRS)  13.7 us
    all_to_all x2, waiting for transfers between devices, exchange(): lax.all_to_all(x, ('gx', 'gy'), split_axis=0, concat_axis=0, tiled=True)  11.9 us
    ppermute x20, starting transfers between devices, to_sibling(): return lax.ppermute(x, 'gz', SWAP)  11.7 us
    ppermute x8, waiting for transfers between devices, to_blocks(): return lax.ppermute(x, ('gx', 'gy', 'gz'), spread(e))  11.4 us
    all_to_all x2, starting transfers between devices, exchange(): lax.all_to_all(x, ('gx', 'gy'), split_axis=0, concat_axis=0, tiled=True)  11 us
    ppermute x17, waiting for transfers between devices, to_off_chip(): return lax.ppermute(x, ('gx', 'gy', 'gz'), OFF_PAIRS)  8.2 us
  transfers between devices with their start and end apart: 48, of which 23 were waited for; matrix products, arithmetic and copies ran while one was open for 1% of the time, Pallas kernels for 29%

profile of v2, /device:TPU:1, one launch (start us, length us, event | category | flops | bytes accessed | tf_op | source)
XLA Modules:
  0.0 172.1 jit_solution(12630225946147282020)
XLA Ops:
  8.1 7.0 %all-to-all-start.1 = ((f32[8,168,128]{2,1,0:T(8,128)}), f32[8,168,128]{2,1,0:T(8,128)S(1)}, u32[]{:S(2)}, u32[]{:S(2)}) async-start(f32[8,168,128]{2,1,0:T(8,128)} %shard_map.160), calls=%async_computation.1 | async-start | bytes 1376256 | tf_op jit(solution)/shard_map/all_to_all | solution.py:700
  15.1 2.7 %shard_map.157 = (f32[4,4,4,16,128]{4,3,2,1,0:T(8,128)S(1)}, f32[4,4,4,16,128]{4,3,2,1,0:T(8,128)S(1)}) custom-call(s32[8]{0:T(128)S(1)} %stack.32.scal, f32[8,64,128]{2,1,0:T(8,128)S(1)} %copy-done.5, f32[8,64,128]{2,1,0:T(8,128)S(1)} %copy-done.6, f32[8,64,128]{2,1,0:T(8,128)S(1)} %copy-done.7, f32[8,64,128]{2,1,0:T(8,128)S(1)} %copy-done.8), custom_call_target="tpu_custom_call" | custom-call | flops 1048576 | bytes 2097152 | tf_op jit(solution)/shard_map/pallas_call | solution.py:740
  21.0 11.9 %all-to-all-done.1 = f32[8,168,128]{2,1,0:T(8,128)S(1)} async-done(((f32[8,168,128]{2,1,0:T(8,128)}), f32[8,168,128]{2,1,0:T(8,128)S(1)}, u32[]{:S(2)}, u32[]{:S(2)}) %all-to-all-start.1) | async-done | bytes 688160 | tf_op jit(solution)/shard_map/all_to_all | solution.py:700
  32.9 4.0 %all-to-all-start = ((f32[8,4,4,16,128]{4,3,2,1,0:T(8,128)}), f32[8,4,4,16,128]{4,3,2,1,0:T(8,128)S(1)}, u32[]{:S(2)}, u32[]{:S(2)}) async-start(f32[8,4,4,16,128]{4,3,2,1,0:T(8,128)} %bitcast.7), calls=%async_computation | async-start | bytes 2097152 | tf_op jit(solution)/shard_map/all_to_all | solution.py:700
  41.6 7.2 %shard_map.164.refs_0_ = f32[32,32,128]{2,1,0:T(8,128)S(1)} custom-call(s32[8]{0:T(128)S(1)} %stack.32.scal, f32[8,4,32,128]{3,2,1,0:T(8,128)S(1)} %bitcast.18, s32[32,128]{1,0:T(8,128)S(1)} %get-tuple-element.112.ids_slab.ids), custom_call_target="tpu_custom_call" | custom-call | flops 16777216 | bytes 1048576 | tf_op jit(solution)/shard_map/pallas_call | solution.py:754
  49.7 7.4 %shard_map.165 = (f32[32,32,128]{2,1,0:T(8,128)S(1)}, f32[32,16,128]{2,1,0:T(8,128)S(1)}, f32[32,16,128]{2,1,0:T(8,128)S(1)}) custom-call(s32[8]{0:T(128)S(1)} %stack.32.scal, f32[8,4,32,128]{3,2,1,0:T(8,128)S(1)} %collective-permute-done.5.table, s32[32,128]{1,0:T(8,128)S(1)} %get-tuple-element.112.ids_slab.ids, f32[32,32,128]{2,1,0:T(8,128)S(1)} %shard_map.164.refs_0_), custom_call_target="tpu_custom_call" | custom-call | flops 16777216 | bytes 2097152 | tf_op jit(solution)/shard_map/pallas_call | solution.py:757
  57.1 1.7 collective-permute-start.6
  58.8 1.8 %shard_map.162.index = s32[2,40,128]{2,1,0:T(8,128)S(1)} custom-call(s32[8]{0:T(128)S(1)} %stack.32.scal, s32[32,128]{1,0:T(8,128)S(1)} %get-tuple-element.112.ids_slab.ids, s32[32,128]{1,0:T(8,128)S(1)} %get-tuple-element.113.ids_owner), custom_call_target="tpu_custom_call" | custom-call | flops 16777216 | bytes 262144 | tf_op jit(solution)/shard_map/pallas_call | solution.py:769
  67.2 3.5 %collective-permute-done.4.refs_3_ = f32[2,32,8,128]{3,2,1,0:T(8,128)S(1)} collective-permute-done((f32[2,32,8,128]{3,2,1,0:T(8,128)S(1)}, f32[2,32,8,128]{3,2,1,0:T(8,128)S(1)}, u32[]{:S(2)}, u32[]{:S(2)}) %collective-permute-start.4) | collective-permute-done | bytes 262176 | tf_op jit(solution)/shard_map/ppermute | solution.py:202
  70.7 1.7 %shard_map.167 = (f32[32,16,128]{2,1,0:T(8,128)S(1)}, f32[32,32,128]{2,1,0:T(8,128)S(1)}, f32[1,32,8,128]{3,2,1,0:T(8,128)S(1)}, f32[1,32,8,128]{3,2,1,0:T(8,128)S(1)}, f32[4,32,16,128]{3,2,1,0:T(8,128)S(1)}) custom-call(s32[8]{0:T(128)S(1)} %stack.32.scal, f32[16]{0:T(128)S(1)} %copy-done.9, f32[32,16,128]{2,1,0:T(8,128)S(1)} %get-tuple-element.116.refs_1_, ...), custom_call_target="tpu_custom_call" | custom-call | flops 16777216 | bytes 4194304 | tf_op jit(solution)/shard_map/pallas_call | solution.py:810
  73.3 1.7 shard_map.171
  77.1 1.7 shard_map.168
  83.6 1.7 %shard_map.169 = (f32[32,16,128]{2,1,0:T(8,128)S(1)}, f32[32,32,128]{2,1,0:T(8,128)S(1)}, f32[1,32,8,128]{3,2,1,0:T(8,128)S(1)}, f32[1,32,8,128]{3,2,1,0:T(8,128)S(1)}, f32[4,32,16,128]{3,2,1,0:T(8,128)S(1)}) custom-call(s32[8]{0:T(128)S(1)} %stack.32.scal, f32[16]{0:T(128)S(1)} %copy-done.9, f32[32,16,128]{2,1,0:T(8,128)S(1)} %get-tuple-element.129.refs_1_, ...), custom_call_target="tpu_custom_call" | custom-call | flops 16777216 | bytes 4194304 | tf_op jit(solution)/shard_map/pallas_call | solution.py:810
  89.9 1.7 %shard_map.170 = (f32[32,16,128]{2,1,0:T(8,128)S(1)}, f32[32,32,128]{2,1,0:T(8,128)S(1)}, f32[1,32,8,128]{3,2,1,0:T(8,128)S(1)}, f32[1,32,8,128]{3,2,1,0:T(8,128)S(1)}, f32[4,32,16,128]{3,2,1,0:T(8,128)S(1)}) custom-call(s32[8]{0:T(128)S(1)} %stack.32.scal, f32[16]{0:T(128)S(1)} %copy-done.9, f32[32,16,128]{2,1,0:T(8,128)S(1)} %get-tuple-element.133.refs_1_, ...), custom_call_target="tpu_custom_call" | custom-call | flops 16777216 | bytes 4194304 | tf_op jit(solution)/shard_map/pallas_call | solution.py:810
  93.3 1.7 %shard_map.174 = (f32[32,16,128]{2,1,0:T(8,128)S(1)}, f32[32,32,128]{2,1,0:T(8,128)S(1)}, f32[1,32,8,128]{3,2,1,0:T(8,128)S(1)}, f32[1,32,8,128]{3,2,1,0:T(8,128)S(1)}) custom-call(s32[8]{0:T(128)S(1)} %stack.32.scal, f32[16,32,128]{2,1,0:T(8,128)S(1)} %get-tuple-element.141.refs_0_, s32[32,128]{1,0:T(8,128)S(1)} %get-tuple-element.142.refs_1_, ...), custom_call_target="tpu_custom_call" | custom-call | flops 16777216 | bytes 4194304 | tf_op jit(solution)/shard_map/pallas_call | solution.py:810
  96.5 1.8 %shard_map.175 = (f32[32,16,128]{2,1,0:T(8,128)S(1)}, f32[32,32,128]{2,1,0:T(8,128)S(1)}, f32[1,32,8,128]{3,2,1,0:T(8,128)S(1)}, f32[1,32,8,128]{3,2,1,0:T(8,128)S(1)}, f32[2,32,16,128]{3,2,1,0:T(8,128)S(1)}) custom-call(s32[8]{0:T(128)S(1)} %stack.32.scal, f32[16]{0:T(128)S(1)} %copy-done.9, f32[32,16,128]{2,1,0:T(8,128)S(1)} %get-tuple-element.137.refs_1_, ...), custom_call_target="tpu_custom_call" | custom-call | flops 16777216 | bytes 4194304 | tf_op jit(solution)/shard_map/pallas_call | solution.py:810
  99.9 1.8 %shard_map.179 = (f32[32,16,128]{2,1,0:T(8,128)S(1)}, f32[32,32,128]{2,1,0:T(8,128)S(1)}, f32[1,32,8,128]{3,2,1,0:T(8,128)S(1)}, f32[1,32,8,128]{3,2,1,0:T(8,128)S(1)}, f32[2,32,16,128]{3,2,1,0:T(8,128)S(1)}) custom-call(s32[8]{0:T(128)S(1)} %stack.32.scal, f32[16,32,128]{2,1,0:T(8,128)S(1)} %get-tuple-element.141.refs_0_, ...), custom_call_target="tpu_custom_call" | custom-call | flops 16777216 | bytes 4194304 | tf_op jit(solution)/shard_map/pallas_call | solution.py:810
  102.9 1.9 %shard_map.176 = (f32[32,16,128]{2,1,0:T(8,128)S(1)}, f32[32,32,128]{2,1,0:T(8,128)S(1)}, f32[1,32,8,128]{3,2,1,0:T(8,128)S(1)}, f32[1,32,8,128]{3,2,1,0:T(8,128)S(1)}, f32[2,32,16,128]{3,2,1,0:T(8,128)S(1)}) custom-call(s32[8]{0:T(128)S(1)} %stack.32.scal, f32[16]{0:T(128)S(1)} %copy-done.9, f32[32,16,128]{2,1,0:T(8,128)S(1)} %get-tuple-element.161.refs_1_, ...), custom_call_target="tpu_custom_call" | custom-call | flops 16777216 | bytes 4194304 | tf_op jit(solution)/shard_map/pallas_call | solution.py:810
  106.3 1.8 %shard_map.180 = (f32[32,16,128]{2,1,0:T(8,128)S(1)}, f32[32,32,128]{2,1,0:T(8,128)S(1)}, f32[1,32,8,128]{3,2,1,0:T(8,128)S(1)}, f32[1,32,8,128]{3,2,1,0:T(8,128)S(1)}, f32[2,32,16,128]{3,2,1,0:T(8,128)S(1)}) custom-call(s32[8]{0:T(128)S(1)} %stack.32.scal, f32[16,32,128]{2,1,0:T(8,128)S(1)} %get-tuple-element.141.refs_0_, ...), custom_call_target="tpu_custom_call" | custom-call | flops 16777216 | bytes 4194304 | tf_op jit(solution)/shard_map/pallas_call | solution.py:810
  109.7 1.9 %shard_map.177 = (f32[32,16,128]{2,1,0:T(8,128)S(1)}, f32[32,32,128]{2,1,0:T(8,128)S(1)}, f32[1,32,8,128]{3,2,1,0:T(8,128)S(1)}, f32[1,32,8,128]{3,2,1,0:T(8,128)S(1)}, f32[2,32,16,128]{3,2,1,0:T(8,128)S(1)}) custom-call(s32[8]{0:T(128)S(1)} %stack.32.scal, f32[16]{0:T(128)S(1)} %copy-done.9, f32[32,16,128]{2,1,0:T(8,128)S(1)} %get-tuple-element.166.refs_1_, ...), custom_call_target="tpu_custom_call" | custom-call | flops 16777216 | bytes 4194304 | tf_op jit(solution)/shard_map/pallas_call | solution.py:810
  113.1 1.8 %shard_map.181 = (f32[32,16,128]{2,1,0:T(8,128)S(1)}, f32[32,32,128]{2,1,0:T(8,128)S(1)}, f32[1,32,8,128]{3,2,1,0:T(8,128)S(1)}, f32[1,32,8,128]{3,2,1,0:T(8,128)S(1)}, f32[2,32,16,128]{3,2,1,0:T(8,128)S(1)}) custom-call(s32[8]{0:T(128)S(1)} %stack.32.scal, f32[16,32,128]{2,1,0:T(8,128)S(1)} %get-tuple-element.141.refs_0_, ...), custom_call_target="tpu_custom_call" | custom-call | flops 16777216 | bytes 4194304 | tf_op jit(solution)/shard_map/pallas_call | solution.py:810
  116.2 2.2 %shard_map.178 = (f32[32,16,128]{2,1,0:T(8,128)S(1)}, f32[32,32,128]{2,1,0:T(8,128)}, f32[2,32,16,128]{3,2,1,0:T(8,128)S(1)}) custom-call(s32[8]{0:T(128)S(1)} %stack.32.scal, f32[16]{0:T(128)S(1)} %copy-done.9, f32[32,16,128]{2,1,0:T(8,128)S(1)} %get-tuple-element.171.refs_1_, f32[1,32,8,128]{3,2,1,0:T(8,128)S(1)} %collective-permute-done.28.refs_2_, ...), custom_call_target="tpu_custom_call" | custom-call | flops 16777216 | bytes 4194304 | tf_op jit(solution)/shard_map/pallas_call | solution.py:810
  119.6 2.3 %shard_map.182 = (f32[32,16,128]{2,1,0:T(8,128)S(1)}, f32[32,32,128]{2,1,0:T(8,128)}, f32[2,32,16,128]{3,2,1,0:T(8,128)S(1)}) custom-call(s32[8]{0:T(128)S(1)} %stack.32.scal, f32[16,32,128]{2,1,0:T(8,128)S(1)} %get-tuple-element.141.refs_0_, s32[32,128]{1,0:T(8,128)S(1)} %get-tuple-element.142.refs_1_, f32[32,16,128]{2,1,0:T(8,128)S(1)} %get-tuple-element.192.refs_2_, ...), custom_call_target="tpu_custom_call" | custom-call | flops 16777216 | bytes 4194304 | tf_op jit(solution)/shard_map/pallas_call | solution.py:810
  121.9 5.8 %shard_map.183 = (f32[384,128]{1,0:T(8,128)S(1)}, f32[384,128]{1,0:T(8,128)S(1)}, f32[384,128]{1,0:T(8,128)S(1)}, f32[384,128]{1,0:T(8,128)S(1)}, f32[384,128]{1...) custom-call(s32[8]{0:T(128)S(1)} %stack.32.scal, ...), custom_call_target="tpu_custom_call" | custom-call | flops 4194304 | bytes 4194304 | tf_op jit(solution)/shard_map/pallas_call | solution.py:830
  127.6 2.6 %collective-permute-start.38 = (f32[384,128]{1,0:T(8,128)S(1)}, f32[384,128]{1,0:T(8,128)S(1)}, u32[]{:S(2)}, u32[]{:S(2)}) collective-permute-start(f32[384,128]{1,0:T(8,128)S(1)} %get-tuple-element.203), channel_id=1, source_target_pairs={{0,12},{1,14},{2,15},{3,13},{4,8},{5,10},{6,11},{7,9},{8,4},{9,6},... | collective-permute-start | bytes 589832 | tf_op jit(solution)/shard_map/ppermute | solution.py:210
  132.8 2.1 %collective-permute-start.41 = (f32[384,128]{1,0:T(8,128)S(1)}, f32[384,128]{1,0:T(8,128)S(1)}, u32[]{:S(2)}, u32[]{:S(2)}) collective-permute-start(f32[384,128]{1,0:T(8,128)S(1)} %get-tuple-element.206), channel_id=1, source_target_pairs={{0,10},{1,8},{2,9},{3,11},{4,14},{5,12},{6,13},{7,15},{8,2},{9,0},... | collective-permute-start | bytes 589832 | tf_op jit(solution)/shard_map/ppermute | solution.py:210
  136.8 16.4 %collective-permute-start.43 = (f32[384,128]{1,0:T(8,128)S(1)}, f32[384,128]{1,0:T(8,128)S(1)}, u32[]{:S(2)}, u32[]{:S(2)}) collective-permute-start(f32[384,128]{1,0:T(8,128)S(1)} %get-tuple-element.208), channel_id=1, source_target_pairs={{0,6},{1,4},{2,5},{3,7},{4,2},{5,0},{6,1},{7,3},{8,14},{9,12},{10,... | collective-permute-start | bytes 589832 | tf_op jit(solution)/shard_map/ppermute | solution.py:210
  153.3 2.9 %collective-permute-start.44 = (f32[384,128]{1,0:T(8,128)S(1)}, f32[384,128]{1,0:T(8,128)S(1)}, u32[]{:S(2)}, u32[]{:S(2)}) collective-permute-start(f32[384,128]{1,0:T(8,128)S(1)} %get-tuple-element.209), channel_id=1, source_target_pairs={{0,0},{1,2},{2,3},{3,1},{4,4},{5,6},{6,7},{7,5},{8,8},{9,10},{10,1... | collective-permute-start | bytes 589832 | tf_op jit(solution)/shard_map/ppermute | solution.py:210
  156.2 4.9 %collective-permute-done.40.refs_2_ = f32[384,128]{1,0:T(8,128)S(1)} collective-permute-done((f32[384,128]{1,0:T(8,128)S(1)}, f32[384,128]{1,0:T(8,128)S(1)}, u32[]{:S(2)}, u32[]{:S(2)}) %collective-permute-start.40) | collective-permute-done | bytes 196640 | tf_op jit(solution)/shard_map/ppermute | solution.py:210
  161.1 2.4 %collective-permute-start.45 = (f32[384,128]{1,0:T(8,128)S(1)}, f32[384,128]{1,0:T(8,128)S(1)}, u32[]{:S(2)}, u32[]{:S(2)}) collective-permute-start(f32[384,128]{1,0:T(8,128)S(1)} %get-tuple-element.201), channel_id=1, source_target_pairs={{0,2},{1,0},{2,1},{3,3},{4,6},{5,4},{6,5},{7,7},{8,10},{9,8},{10,9... | collective-permute-start | bytes 589832 | tf_op jit(solution)/shard_map/ppermute | solution.py:210
  167.1 2.0 %collective-permute-done.45.refs_7_ = f32[384,128]{1,0:T(8,128)S(1)} collective-permute-done((f32[384,128]{1,0:T(8,128)S(1)}, f32[384,128]{1,0:T(8,128)S(1)}, u32[]{:S(2)}, u32[]{:S(2)}) %collective-permute-start.45) | collective-permute-done | bytes 196640 | tf_op jit(solution)/shard_map/ppermute | solution.py:210
  169.1 3.0 %shard_map.185 = (f32[8,64,128]{2,1,0:T(8,128)}, f32[8,64,128]{2,1,0:T(8,128)}, f32[2048,128]{1,0:T(8,128)}) custom-call(s32[8]{0:T(128)S(1)} %stack.32.scal, bf16[1024,1024]{1,0:T(8,128)(2,1)S(1)} %shard_map.184.picks, f32[384,128]{1,0:T(8,128)S(1)} %collective-permute-done.38.refs_0_, f32[384,128]{1,0:T(8,128)S(1)} %collective-permute-done.39.refs_1_, ...), custom_call_target="tpu_custom_call" | custom-call | flops 268435456 | bytes 4194304 | tf_op jit(solution)/shard_map/pallas_call | solution.py:841
  (126 shorter events, 55.9 us)
Async XLA Ops:
  8.1 24.8 %all-to-all-start.1 = ((f32[8,168,128]{2,1,0:T(8,128)}), f32[8,168,128]{2,1,0:T(8,128)S(1)}, u32[]{:S(2)}, u32[]{:S(2)}) async-start(f32[8,168,128]{2,1,0:T(8,128)} %shard_map.160), calls=%async_computation.1 | async-start | bytes 1376256 | tf_op jit(solution)/shard_map/all_to_all | solution.py:700
  32.9 29.2 %all-to-all-start = ((f32[8,4,4,16,128]{4,3,2,1,0:T(8,128)}), f32[8,4,4,16,128]{4,3,2,1,0:T(8,128)S(1)}, u32[]{:S(2)}, u32[]{:S(2)}) async-start(f32[8,4,4,16,128]{4,3,2,1,0:T(8,128)} %bitcast.7), calls=%async_computation | async-start | bytes 2097152 | tf_op jit(solution)/shard_map/all_to_all | solution.py:700
  36.9 12.8 %collective-permute-start.5 = (f32[8,4,32,128]{3,2,1,0:T(8,128)S(1)}, f32[8,4,32,128]{3,2,1,0:T(8,128)S(1)}, u32[]{:S(2)}, u32[]{:S(2)}) collective-permute-start(f32[8,4,32,128]{3,2,1,0:T(8,128)S(1)} %bitcast.17), channel_id=1, source_target_pairs={{0,16},{16,0},{1,17},{17,1},{2,18},{18,2},{3,19},{19,3},{4,20},{20... | collective-permute-start | bytes 1572872 | tf_op jit(solution)/shard_map/ppermute | solution.py:737
  57.1 9.0 %collective-permute-start.6 = (f32[32,16,128]{2,1,0:T(8,128)S(1)}, f32[32,16,128]{2,1,0:T(8,128)S(1)}, u32[]{:S(2)}, u32[]{:S(2)}) collective-permute-start(f32[32,16,128]{2,1,0:T(8,128)S(1)} %get-tuple-element.121), channel_id=1, source_target_pairs={{0,1},{1,0},{2,3},{3,2},{4,5},{5,4},{6,7},{7,6},{8,9},{9,8},{10,11... | collective-permute-start | bytes 786440 | tf_op jit(solution)/shard_map/ppermute | solution.py:198
  60.6 5.9 %collective-permute-start.7 = (f32[32,16,128]{2,1,0:T(8,128)S(1)}, f32[32,16,128]{2,1,0:T(8,128)S(1)}, u32[]{:S(2)}, u32[]{:S(2)}) collective-permute-start(f32[32,16,128]{2,1,0:T(8,128)S(1)} %get-tuple-element.122), channel_id=1, source_target_pairs={{1,4},{4,1},{5,8},{8,5},{9,12},{12,9},{13,14},{14,13},{15,10},{10,... | collective-permute-start | bytes 786440 | tf_op jit(solution)/shard_map/ppermute | solution.py:202
  64.6 6.1 %collective-permute-start.4 = (f32[2,32,8,128]{3,2,1,0:T(8,128)S(1)}, f32[2,32,8,128]{3,2,1,0:T(8,128)S(1)}, u32[]{:S(2)}, u32[]{:S(2)}) collective-permute-start(f32[2,32,8,128]{3,2,1,0:T(8,128)S(1)} %get-tuple-element.118), channel_id=1, source_target_pairs={{1,4},{4,1},{5,8},{8,5},{9,12},{12,9},{13,14},{14,13},{15,10},{10,... | collective-permute-start | bytes 786440 | tf_op jit(solution)/shard_map/ppermute | solution.py:202
  64.6 8.7 %collective-permute-start.16 = (f32[2,32,8,128]{3,2,1,0:T(8,128)S(1)}, f32[2,32,8,128]{3,2,1,0:T(8,128)S(1)}, u32[]{:S(2)}, u32[]{:S(2)}) collective-permute-start(f32[2,32,8,128]{3,2,1,0:T(8,128)S(1)} %get-tuple-element.144), channel_id=1, source_target_pairs={{0,1},{1,0},{2,3},{3,2},{4,5},{5,4},{6,7},{7,6},{8,9},{9,8},{10,11... | collective-permute-start | bytes 786440 | tf_op jit(solution)/shard_map/ppermute | solution.py:198
  66.2 7.1 %collective-permute-start.17 = (f32[2,32,8,128]{3,2,1,0:T(8,128)S(1)}, f32[2,32,8,128]{3,2,1,0:T(8,128)S(1)}, u32[]{:S(2)}, u32[]{:S(2)}) collective-permute-start(f32[2,32,8,128]{3,2,1,0:T(8,128)S(1)} %get-tuple-element.145), channel_id=1, source_target_pairs={{1,4},{4,1},{5,8},{8,5},{9,12},{12,9},{13,14},{14,13},{15,10},{10,... | collective-permute-start | bytes 786440 | tf_op jit(solution)/shard_map/ppermute | solution.py:202
  72.6 4.5 %collective-permute-start.9 = (f32[1,32,8,128]{3,2,1,0:T(8,128)S(1)}, f32[1,32,8,128]{3,2,1,0:T(8,128)S(1)}, u32[]{:S(2)}, u32[]{:S(2)}) collective-permute-start(f32[1,32,8,128]{3,2,1,0:T(8,128)S(1)} %get-tuple-element.127), channel_id=1, source_target_pairs={{1,4},{4,1},{5,8},{8,5},{9,12},{12,9},{13,14},{14,13},{15,10},{10,... | collective-permute-start | bytes 393224 | tf_op jit(solution)/shard_map/ppermute | solution.py:202
  75.0 5.0 %collective-permute-start.18 = (f32[1,32,8,128]{3,2,1,0:T(8,128)S(1)}, f32[1,32,8,128]{3,2,1,0:T(8,128)S(1)}, u32[]{:S(2)}, u32[]{:S(2)}) collective-permute-start(f32[1,32,8,128]{3,2,1,0:T(8,128)S(1)} %get-tuple-element.148), channel_id=1, source_target_pairs={{0,1},{1,0},{2,3},{3,2},{4,5},{5,4},{6,7},{7,6},{8,9},{9,8},{10,11... | collective-permute-start | bytes 393224 | tf_op jit(solution)/shard_map/ppermute | solution.py:198
  75.9 4.4 %collective-permute-start.19 = (f32[1,32,8,128]{3,2,1,0:T(8,128)S(1)}, f32[1,32,8,128]{3,2,1,0:T(8,128)S(1)}, u32[]{:S(2)}, u32[]{:S(2)}) collective-permute-start(f32[1,32,8,128]{3,2,1,0:T(8,128)S(1)} %get-tuple-element.149), channel_id=1, source_target_pairs={{1,4},{4,1},{5,8},{8,5},{9,12},{12,9},{13,14},{14,13},{15,10},{10,... | collective-permute-start | bytes 393224 | tf_op jit(solution)/shard_map/ppermute | solution.py:202
  78.8 4.6 %collective-permute-start.10 = (f32[1,32,8,128]{3,2,1,0:T(8,128)S(1)}, f32[1,32,8,128]{3,2,1,0:T(8,128)S(1)}, u32[]{:S(2)}, u32[]{:S(2)}) collective-permute-start(f32[1,32,8,128]{3,2,1,0:T(8,128)S(1)} %get-tuple-element.130), channel_id=1, source_target_pairs={{0,1},{1,0},{2,3},{3,2},{4,5},{5,4},{6,7},{7,6},{8,9},{9,8},{10,11... | collective-permute-start | bytes 393224 | tf_op jit(solution)/shard_map/ppermute | solution.py:198
  79.2 4.4 %collective-permute-start.11 = (f32[1,32,8,128]{3,2,1,0:T(8,128)S(1)}, f32[1,32,8,128]{3,2,1,0:T(8,128)S(1)}, u32[]{:S(2)}, u32[]{:S(2)}) collective-permute-start(f32[1,32,8,128]{3,2,1,0:T(8,128)S(1)} %get-tuple-element.131), channel_id=1, source_target_pairs={{1,4},{4,1},{5,8},{8,5},{9,12},{12,9},{13,14},{14,13},{15,10},{10,... | collective-permute-start | bytes 393224 | tf_op jit(solution)/shard_map/ppermute | solution.py:202
  82.5 4.4 %collective-permute-start.21 = (f32[1,32,8,128]{3,2,1,0:T(8,128)S(1)}, f32[1,32,8,128]{3,2,1,0:T(8,128)S(1)}, u32[]{:S(2)}, u32[]{:S(2)}) collective-permute-start(f32[1,32,8,128]{3,2,1,0:T(8,128)S(1)} %get-tuple-element.153), channel_id=1, source_target_pairs={{1,4},{4,1},{5,8},{8,5},{9,12},{12,9},{13,14},{14,13},{15,10},{10,... | collective-permute-start | bytes 393224 | tf_op jit(solution)/shard_map/ppermute | solution.py:202
  88.9 4.4 %collective-permute-start.23 = (f32[1,32,8,128]{3,2,1,0:T(8,128)S(1)}, f32[1,32,8,128]{3,2,1,0:T(8,128)S(1)}, u32[]{:S(2)}, u32[]{:S(2)}) collective-permute-start(f32[1,32,8,128]{3,2,1,0:T(8,128)S(1)} %get-tuple-element.157), channel_id=1, source_target_pairs={{1,4},{4,1},{5,8},{8,5},{9,12},{12,9},{13,14},{14,13},{15,10},{10,... | collective-permute-start | bytes 393224 | tf_op jit(solution)/shard_map/ppermute | solution.py:202
  91.7 4.7 %collective-permute-start.14 = (f32[1,32,8,128]{3,2,1,0:T(8,128)S(1)}, f32[1,32,8,128]{3,2,1,0:T(8,128)S(1)}, u32[]{:S(2)}, u32[]{:S(2)}) collective-permute-start(f32[1,32,8,128]{3,2,1,0:T(8,128)S(1)} %get-tuple-element.138), channel_id=1, source_target_pairs={{0,1},{1,0},{2,3},{3,2},{4,5},{5,4},{6,7},{7,6},{8,9},{9,8},{10,11... | collective-permute-start | bytes 393224 | tf_op jit(solution)/shard_map/ppermute | solution.py:198
  92.1 4.4 %collective-permute-start.15 = (f32[1,32,8,128]{3,2,1,0:T(8,128)S(1)}, f32[1,32,8,128]{3,2,1,0:T(8,128)S(1)}, u32[]{:S(2)}, u32[]{:S(2)}) collective-permute-start(f32[1,32,8,128]{3,2,1,0:T(8,128)S(1)} %get-tuple-element.139), channel_id=1, source_target_pairs={{1,4},{4,1},{5,8},{8,5},{9,12},{12,9},{13,14},{14,13},{15,10},{10,... | collective-permute-start | bytes 393224 | tf_op jit(solution)/shard_map/ppermute | solution.py:202
  95.0 4.4 %collective-permute-start.30 = (f32[1,32,8,128]{3,2,1,0:T(8,128)S(1)}, f32[1,32,8,128]{3,2,1,0:T(8,128)S(1)}, u32[]{:S(2)}, u32[]{:S(2)}) collective-permute-start(f32[1,32,8,128]{3,2,1,0:T(8,128)S(1)} %get-tuple-element.177), channel_id=1, source_target_pairs={{0,1},{1,0},{2,3},{3,2},{4,5},{5,4},{6,7},{7,6},{8,9},{9,8},{10,11... | collective-permute-start | bytes 393224 | tf_op jit(solution)/shard_map/ppermute | solution.py:198
  98.4 4.5 %collective-permute-start.24 = (f32[1,32,8,128]{3,2,1,0:T(8,128)S(1)}, f32[1,32,8,128]{3,2,1,0:T(8,128)S(1)}, u32[]{:S(2)}, u32[]{:S(2)}) collective-permute-start(f32[1,32,8,128]{3,2,1,0:T(8,128)S(1)} %get-tuple-element.162), channel_id=1, source_target_pairs={{0,1},{1,0},{2,3},{3,2},{4,5},{5,4},{6,7},{7,6},{8,9},{9,8},{10,11... | collective-permute-start | bytes 393224 | tf_op jit(solution)/shard_map/ppermute | solution.py:198
  101.7 4.5 %collective-permute-start.32 = (f32[1,32,8,128]{3,2,1,0:T(8,128)S(1)}, f32[1,32,8,128]{3,2,1,0:T(8,128)S(1)}, u32[]{:S(2)}, u32[]{:S(2)}) collective-permute-start(f32[1,32,8,128]{3,2,1,0:T(8,128)S(1)} %get-tuple-element.181), channel_id=1, source_target_pairs={{0,1},{1,0},{2,3},{3,2},{4,5},{5,4},{6,7},{7,6},{8,9},{9,8},{10,11... | collective-permute-start | bytes 393224 | tf_op jit(solution)/shard_map/ppermute | solution.py:198
  104.8 4.8 %collective-permute-start.26 = (f32[1,32,8,128]{3,2,1,0:T(8,128)S(1)}, f32[1,32,8,128]{3,2,1,0:T(8,128)S(1)}, u32[]{:S(2)}, u32[]{:S(2)}) collective-permute-start(f32[1,32,8,128]{3,2,1,0:T(8,128)S(1)} %get-tuple-element.167), channel_id=1, source_target_pairs={{0,1},{1,0},{2,3},{3,2},{4,5},{5,4},{6,7},{7,6},{8,9},{9,8},{10,11... | collective-permute-start | bytes 393224 | tf_op jit(solution)/shard_map/ppermute | solution.py:198
  108.2 4.5 %collective-permute-start.34 = (f32[1,32,8,128]{3,2,1,0:T(8,128)S(1)}, f32[1,32,8,128]{3,2,1,0:T(8,128)S(1)}, u32[]{:S(2)}, u32[]{:S(2)}) collective-permute-start(f32[1,32,8,128]{3,2,1,0:T(8,128)S(1)} %get-tuple-element.187), channel_id=1, source_target_pairs={{0,1},{1,0},{2,3},{3,2},{4,5},{5,4},{6,7},{7,6},{8,9},{9,8},{10,11... | collective-permute-start | bytes 393224 | tf_op jit(solution)/shard_map/ppermute | solution.py:198
  111.6 4.6 %collective-permute-start.28 = (f32[1,32,8,128]{3,2,1,0:T(8,128)S(1)}, f32[1,32,8,128]{3,2,1,0:T(8,128)S(1)}, u32[]{:S(2)}, u32[]{:S(2)}) collective-permute-start(f32[1,32,8,128]{3,2,1,0:T(8,128)S(1)} %get-tuple-element.172), channel_id=1, source_target_pairs={{0,1},{1,0},{2,3},{3,2},{4,5},{5,4},{6,7},{7,6},{8,9},{9,8},{10,11... | collective-permute-start | bytes 393224 | tf_op jit(solution)/shard_map/ppermute | solution.py:198
  111.7 4.4 %collective-permute-start.29 = (f32[1,32,8,128]{3,2,1,0:T(8,128)S(1)}, f32[1,32,8,128]{3,2,1,0:T(8,128)S(1)}, u32[]{:S(2)}, u32[]{:S(2)}) collective-permute-start(f32[1,32,8,128]{3,2,1,0:T(8,128)S(1)} %get-tuple-element.173), channel_id=1, source_target_pairs={{1,4},{4,1},{5,8},{8,5},{9,12},{12,9},{13,14},{14,13},{15,10},{10,... | collective-permute-start | bytes 393224 | tf_op jit(solution)/shard_map/ppermute | solution.py:202
  127.6 9.2 %collective-permute-start.38 = (f32[384,128]{1,0:T(8,128)S(1)}, f32[384,128]{1,0:T(8,128)S(1)}, u32[]{:S(2)}, u32[]{:S(2)}) collective-permute-start(f32[384,128]{1,0:T(8,128)S(1)} %get-tuple-element.203), channel_id=1, source_target_pairs={{0,12},{1,14},{2,15},{3,13},{4,8},{5,10},{6,11},{7,9},{8,4},{9,6},... | collective-permute-start | bytes 589832 | tf_op jit(solution)/shard_map/ppermute | solution.py:210
  130.2 23.1 %collective-permute-start.39 = (f32[384,128]{1,0:T(8,128)S(1)}, f32[384,128]{1,0:T(8,128)S(1)}, u32[]{:S(2)}, u32[]{:S(2)}) collective-permute-start(f32[384,128]{1,0:T(8,128)S(1)} %get-tuple-element.204), channel_id=1, source_target_pairs={{0,14},{1,12},{2,13},{3,15},{4,10},{5,8},{6,9},{7,11},{8,6},{9,4},... | collective-permute-start | bytes 589832 | tf_op jit(solution)/shard_map/ppermute | solution.py:210
  131.4 29.7 %collective-permute-start.40 = (f32[384,128]{1,0:T(8,128)S(1)}, f32[384,128]{1,0:T(8,128)S(1)}, u32[]{:S(2)}, u32[]{:S(2)}) collective-permute-start(f32[384,128]{1,0:T(8,128)S(1)} %get-tuple-element.205), channel_id=1, source_target_pairs={{0,8},{1,10},{2,11},{3,9},{4,12},{5,14},{6,15},{7,13},{8,0},{9,2},... | collective-permute-start | bytes 589832 | tf_op jit(solution)/shard_map/ppermute | solution.py:210
  132.8 32.7 %collective-permute-start.41 = (f32[384,128]{1,0:T(8,128)S(1)}, f32[384,128]{1,0:T(8,128)S(1)}, u32[]{:S(2)}, u32[]{:S(2)}) collective-permute-start(f32[384,128]{1,0:T(8,128)S(1)} %get-tuple-element.206), channel_id=1, source_target_pairs={{0,10},{1,8},{2,9},{3,11},{4,14},{5,12},{6,13},{7,15},{8,2},{9,0},... | collective-permute-start | bytes 589832 | tf_op jit(solution)/shard_map/ppermute | solution.py:210
  134.8 30.6 %collective-permute-start.42 = (f32[384,128]{1,0:T(8,128)S(1)}, f32[384,128]{1,0:T(8,128)S(1)}, u32[]{:S(2)}, u32[]{:S(2)}) collective-permute-start(f32[384,128]{1,0:T(8,128)S(1)} %get-tuple-element.207), channel_id=1, source_target_pairs={{0,4},{1,6},{2,7},{3,5},{4,0},{5,2},{6,3},{7,1},{8,12},{9,14},{10,... | collective-permute-start | bytes 589832 | tf_op jit(solution)/shard_map/ppermute | solution.py:210
  136.8 30.2 %collective-permute-start.43 = (f32[384,128]{1,0:T(8,128)S(1)}, f32[384,128]{1,0:T(8,128)S(1)}, u32[]{:S(2)}, u32[]{:S(2)}) collective-permute-start(f32[384,128]{1,0:T(8,128)S(1)} %get-tuple-element.208), channel_id=1, source_target_pairs={{0,6},{1,4},{2,5},{3,7},{4,2},{5,0},{6,1},{7,3},{8,14},{9,12},{10,... | collective-permute-start | bytes 589832 | tf_op jit(solution)/shard_map/ppermute | solution.py:210
  153.3 13.8 %collective-permute-start.44 = (f32[384,128]{1,0:T(8,128)S(1)}, f32[384,128]{1,0:T(8,128)S(1)}, u32[]{:S(2)}, u32[]{:S(2)}) collective-permute-start(f32[384,128]{1,0:T(8,128)S(1)} %get-tuple-element.209), channel_id=1, source_target_pairs={{0,0},{1,2},{2,3},{3,1},{4,4},{5,6},{6,7},{7,5},{8,8},{9,10},{10,1... | collective-permute-start | bytes 589832 | tf_op jit(solution)/shard_map/ppermute | solution.py:210
  161.1 8.0 %collective-permute-start.45 = (f32[384,128]{1,0:T(8,128)S(1)}, f32[384,128]{1,0:T(8,128)S(1)}, u32[]{:S(2)}, u32[]{:S(2)}) collective-permute-start(f32[384,128]{1,0:T(8,128)S(1)} %get-tuple-element.201), channel_id=1, source_target_pairs={{0,2},{1,0},{2,1},{3,3},{4,6},{5,4},{6,5},{7,7},{8,10},{9,8},{10,9... | collective-permute-start | bytes 589832 | tf_op jit(solution)/shard_map/ppermute | solution.py:210
  (29 other events, 235.2 us)

commit v3 on v2

--- a/solution.py
+++ b/solution.py
@@ -160,8 +160,10 @@
 HALO = 8
 OWN = slice(HALO, HALO + ZS)
 SCALE = 5040.0
-UNSCALE = 1.0
+UNSCALE = 1.0 / SCALE
 PADX = 4
+EXT_SHAPE = (NXA + 2 * PADX, ZE, 128)
+INNER = slice(PADX, PADX + NXA)
 STEPS = 16
 ROUNDS = STEPS // 2
 MIB = 1 << 20
@@ -240,6 +242,7 @@
     along_z = band(ZE)
     full = np.kron(np.eye(8, dtype=np.float32), along_z)
     own = np.kron(np.eye(8, dtype=np.float32), along_z[OWN])
+    full, own = [np.concatenate([m, m], 1) for m in (full, own)]
     return [jnp.asarray(m, BF16) for m in (along_y, full, own)]
 
 
@@ -339,9 +342,18 @@
                     give[pl.ds(g, 1), f, i] = piece
 
 
-def unpack_small(scal, mine, other, ids_slab, ids_owner, depth, traces):
+def unpack_small(scal, wavelet, mine, other, ids_slab, ids_owner, depth, traces, pulse, pulse_depth, place):
     low = half_lanes((8, 128))
     h = scal[H]
+    x_at = lax.broadcasted_iota(jnp.int32, (NXA, 128), 0)
+    y_at = lax.broadcasted_iota(jnp.int32, (NXA, 128), 1)
+    at_source = (x_at == scal[SX]) & (y_at == scal[SY])
+    for t in range(STEPS):
+        pulse[t] = jnp.where(at_source, wavelet[t], 0.0)
+    pulse_depth[...] = jnp.full((NXA, 128), scal[SZ], jnp.int32)
+    place[0] = jnp.full((8, 128), h, jnp.int32)
+    place[1] = jnp.full((8, 128), jnp.where(is_edge(scal), 1, 0), jnp.int32)
+    place[2] = jnp.full((8, 128), scal[LINE] * ZS - HALO, jnp.int32)
     for ix in range(GX):
         rows = slice(ix * BX, (ix + 1) * BX)
         for ref, is_mine in ((mine, True), (other, False)):
@@ -405,9 +417,9 @@
     sib_at = (ZE - HALO) * (1 - scal[H])
     off_at = (ZE - HALO) * scal[H]
     inside = jnp.where(is_edge(scal), 0.0, 1.0)
-    slow[:, OWN, :] = coefs[:, 0:ZS, :]
-    slow[:, pl.ds(sib_at, HALO), :] = sib[:, 0:HALO, :]
-    slow[:, pl.ds(off_at, HALO), :] = off[:, 0:HALO, :] * inside
+    slow[:, OWN, :] = coefs[:, 0:ZS, :] * UNSCALE
+    slow[:, pl.ds(sib_at, HALO), :] = sib[:, 0:HALO, :] * UNSCALE
+    slow[:, pl.ds(off_at, HALO), :] = off[:, 0:HALO, :] * (inside * UNSCALE)
     aniso[:, OWN, :] = 1.0 + 2.0 * coefs[:, ZS:, :]
     aniso[:, pl.ds(sib_at, HALO), :] = 1.0 + 2.0 * sib[:, HALO:, :]
     aniso[:, pl.ds(off_at, HALO), :] = 1.0 + 2.0 * off[:, HALO:, :]
@@ -479,38 +491,26 @@
             out[part, 8 * group : 8 * group + 8] = jnp.where(at_x < BX, found, -1)
 
 
-def stencil(field, g, along_y, along_z, own):
-    rows = slice(PADX + 8 * g, PADX + 8 * g + 8)
-    zs = OWN if own else slice(0, ZE)
+def bands_of(field, g, along_y, along_z, own):
+    first = PADX + 8 * g
     depth = ZS if own else ZE
-    whole = field[rows].reshape(8 * ZE, 128)
+    whole = field[first : first + 8].reshape(8 * ZE, 128)
     high = whole.astype(BF16)
     rest = (whole - high.astype(F32)).astype(BF16)
-    both = jnp.concatenate([high, rest], axis=1)
-    my = jnp.dot(both, along_y[...], preferred_element_type=F32).reshape(8, ZE, 128)[:, zs]
-    mz = jnp.dot(along_z[...], both, preferred_element_type=F32)
-    mz = (mz[:, :128] + mz[:, 128:]).reshape(8, depth, 128)
-    center = field[rows, zs, :]
-    hor = my * (1.0 / SCALE) + (2.0 * STENCIL[0]) * center
-    for i in range(1, 5):
-        up = field[PADX + 8 * g + i : PADX + 8 * g + 8 + i, zs, :]
-        down = field[PADX + 8 * g - i : PADX + 8 * g + 8 - i, zs, :]
-        hor = hor + STENCIL[i] * (up + down)
-    ver = mz * (1.0 / SCALE) + STENCIL[0] * center
-    return center, hor, ver
-
-
-def round_kernel(kind, r, scal, *refs):
+    my = jnp.dot(jnp.concatenate([high, rest], axis=1), along_y[...], preferred_element_type=F32)
+    mz = jnp.dot(along_z[...], jnp.concatenate([high, rest], axis=0), preferred_element_type=F32)
+    return my.reshape(8, ZE, 128), mz.reshape(8, depth, 128)
+
+
+def round_scratch():
+    return [pltpu.VMEM(EXT_SHAPE, F32)]
+
+
+def round_kernel(kind, r, *refs):
     refs = list(refs)
     take = lambda n: [refs.pop(0) for _ in range(n)]
     first, later, last = r == 0, r >= ROUNDS // 2, r == ROUNDS - 1
-    if kind == "u":
-        (weights,) = take(1)
-    else:
-        traces, depth = take(2)
-    own, sib, off = take(3)
-    (prev,) = take(1)
-    slow, aniso, along_y, along_z, along_z_own = take(5)
+    place, drive, depth, own, sib, off, prev, slow, aniso, along_y, along_z, along_z_own = take(12)
     if later:
         if kind == "u":
             partner_mid, partner_end = take(2)
@@ -525,92 +525,87 @@
         (total,) = take(1)
     elif kind == "u":
         (history,) = take(1)
-    e0, e1 = take(2)
-
-    h = scal[H]
-    sib_at = (ZE - HALO) * (1 - h)
-    off_at = (ZE - HALO) * h
-    edge = is_edge(scal)
+    (e0,) = take(1)
+    e1 = out_mid
+
+    core_0 = place[0] == 0
+    inside = place[1] == 0
     zero = jnp.zeros((PADX, ZE, 128), F32)
     for e in (e0, e1):
         e[0:PADX] = zero
         e[PADX + NXA :] = zero
-    inner = slice(PADX, PADX + NXA)
-    now = 1 if first else 0
-    e0[inner, OWN, :] = own[...]
-    e0[inner, pl.ds(sib_at, HALO), :] = sib[now]
-    e0[inner, pl.ds(off_at, HALO), :] = jnp.where(edge, 0.0, off[now])
+
+    def extend(e, own, n):
+        for x in range(NXA):
+            near, far = sib[n, x], jnp.where(inside, off[n, x], 0.0)
+            e[PADX + x, 0:HALO] = jnp.where(core_0, far, near)
+            e[PADX + x, OWN] = own[x]
+            e[PADX + x, HALO + ZS :] = jnp.where(core_0, near, far)
+
     if first:
-        out_mid[:, OWN, :] = prev[...]
-        out_mid[:, pl.ds(sib_at, HALO), :] = sib[0]
-        out_mid[:, pl.ds(off_at, HALO), :] = jnp.where(edge, 0.0, off[0])
-        prev = out_mid
-    top = scal[LINE] * ZS - HALO
-
-    def source(weight, depth_rows, start):
-        shape = (1, depth_rows, 128)
-        z = lax.broadcasted_iota(jnp.int32, shape, 1) + start
-        y = lax.broadcasted_iota(jnp.int32, shape, 2)
-        return jnp.where((z == scal[SZ]) & (y == scal[SY]), weight, 0.0)
-
-    def receivers(t, g, depth_rows, start):
-        z = lax.broadcasted_iota(jnp.int32, (depth_rows, 128), 0) + start
-        out = []
-        for x in range(8 * g, 8 * g + 8):
-            at = jnp.broadcast_to(depth[x : x + 1, :], (depth_rows, 128))
-            value = jnp.broadcast_to(traces[t, x : x + 1, :], (depth_rows, 128))
-            out.append(jnp.where(z == at, value, 0.0)[None])
-        return jnp.concatenate(out, axis=0)
-
-    for step in range(2):
-        t = 2 * r + step
+        extend(e0, own, 1)
+        extend(e1, prev, 0)
+        prev = e1
+    else:
+        extend(e0, own, 0)
+    base = jnp.concatenate([place[2]] * (ZE // 8), axis=0) + lax.broadcasted_iota(jnp.int32, (ZE, 128), 0)
+
+    def bands(step, g):
+        if step:
+            return bands_of(e1, g, along_y, along_z_own, True)
+        return bands_of(e0, g, along_y, along_z, False)
+
+    items = [(step, g) for step in range(2) for g in range(4)]
+    ahead = bands(*items[0])
+    for k, (step, g) in enumerate(items):
+        my, mz = ahead
+        if k + 1 < len(items):
+            ahead = bands(*items[k + 1])
+        t = 2 * r + step if kind == "u" else STEPS - 1 - (2 * r + step)
         field = e1 if step else e0
-        depth_rows = ZS if step else ZE
-        start = top + HALO if step else top
-        for g in range(4):
-            xs = slice(8 * g, 8 * g + 8)
-            zs = OWN if step else slice(0, ZE)
-            center, hor, ver = stencil(field, g, along_y, along_z_own if step else along_z, step)
-            before = e0[PADX + 8 * g : PADX + 8 * g + 8, OWN, :] if step else prev[xs]
-            lap = aniso[xs, zs, :] * hor + ver
-            following = 2.0 * center - before + slow[xs, zs, :] * lap
-            if kind == "a":
-                following = following + receivers(STEPS - 1 - t, g, depth_rows, start)
+        zs = OWN if step else slice(0, ZE)
+        count = ZS if step else ZE
+        z = base[zs]
+        for n in range(8):
+            x = 8 * g + n
+            at = PADX + x
+            center = field[at, zs, :]
+            hor = my[n, zs] + (2.0 * SCALE * STENCIL[0]) * center
+            for i in range(1, 5):
+                hor = hor + (SCALE * STENCIL[i]) * (field[at + i, zs, :] + field[at - i, zs, :])
+            ver = mz[n] + (SCALE * STENCIL[0]) * center
+            before = e0[at, OWN, :] if step else prev[at]
+            lap = aniso[x, zs, :] * hor + ver
+            following = 2.0 * center - before + slow[x, zs, :] * lap
+            at_z = jnp.broadcast_to(depth[x : x + 1, :], (count, 128))
+            value = jnp.broadcast_to(drive[t, x : x + 1, :], (count, 128))
+            following = following + jnp.where(z == at_z, value, 0.0)
             if step:
-                out_own[xs] = following
+                out_own[x] = following
+                if not last:
+                    low, high = following[:HALO], following[HALO:]
+                    out_sib[0, x] = jnp.where(core_0, high, low)
+                    out_off[0, x] = jnp.where(core_0, low, high)
             else:
-                e1[PADX + 8 * g : PADX + 8 * g + 8] = following
-            if step == 0:
-                hor, ver = hor[:, OWN], ver[:, OWN]
+                e1[at] = following
+                hor, ver = hor[OWN], ver[OWN]
             if kind == "u" and not later:
-                history[2 * step, xs] = hor
-                history[2 * step + 1, xs] = ver
+                history[2 * step, x] = hor
+                history[2 * step + 1, x] = ver
             if later:
                 if kind == "u":
-                    other = partner_mid[xs, OWN, :] if step else partner_end[xs]
-                    hor_part, ver_part = hor, ver
+                    other = partner_mid[at, OWN, :] if step else partner_end[x]
                 else:
-                    other = following if step else following[:, OWN]
-                    hor_part = partner[2 * (1 - step), xs]
-                    ver_part = partner[2 * (1 - step) + 1, xs]
-                sum_h, sum_v = other * hor_part, other * ver_part
+                    other = following if step else following[OWN]
+                    hor = partner[2 * (1 - step), x]
+                    ver = partner[2 * (1 - step) + 1, x]
+                sum_h, sum_v = other * hor, other * ver
                 if step:
-                    sum_h, sum_v = total[0, xs] + sum_h, total[1, xs] + sum_v
+                    sum_h, sum_v = total[0, x] + sum_h, total[1, x] + sum_v
                 elif r > ROUNDS // 2:
-                    sum_h, sum_v = total_in[0, xs] + sum_h, total_in[1, xs] + sum_v
-                total[0, xs] = sum_h
-                total[1, xs] = sum_v
-        if kind == "u":
-            if step:
-                row = out_own[pl.ds(scal[SX], 1)]
-                out_own[pl.ds(scal[SX], 1)] = row + source(weights[t], ZS, start)
-            else:
-                row = e1[pl.ds(PADX + scal[SX], 1)]
-                e1[pl.ds(PADX + scal[SX], 1)] = row + source(weights[t], ZE, start)
-    out_mid[...] = e1[inner]
-    if not last:
-        out_sib[0] = out_own[:, pl.ds(HALO * (1 - h), HALO), :]
-        out_off[0] = out_own[:, pl.ds(HALO * h, HALO), :]
+                    sum_h, sum_v = total_in[0, x] + sum_h, total_in[1, x] + sum_v
+                total[0, x] = sum_h
+                total[1, x] = sum_v
 
 
 def pack_out(scal, u, a, index, total_u, total_a, coefs, *refs):
@@ -742,13 +737,14 @@
     )(scal, forward_prev, forward_now, adjoint_prev, adjoint_now)
     fields = exchange(by_half(h, keep, to_sibling(give)))
 
-    ids_slab, ids_owner, depth, traces = call(
+    plane, drive = ((NXA, 128), jnp.int32), ((STEPS, NXA, 128), F32)
+    ids_slab, ids_owner, depth, traces, pulse, pulse_depth, place_info = call(
         unpack_small,
-        [((NXA, 128), jnp.int32)] * 3 + [((STEPS, NXA, 128), F32)],
-        [SMEM] + vmem(2),
+        [plane] * 3 + [drive, drive, plane, ((3, 8, 128), jnp.int32)],
+        [SMEM] * 2 + vmem(2),
         moved=MIB // 2,
         flops=1 << 20,
-    )(scal, small_mine, small_other)
+    )(scal, wavelet, small_mine, small_other)
     coef_shape = ((NXA, 2 * ZS, 128), F32)
     half_shape = ((NXA, 2 * HALO, 128), F32)
     (coefs,) = call(
@@ -793,16 +789,14 @@
     for r in range(ROUNDS):
         for kind in "ua":
             later, last = r >= ROUNDS // 2, r == ROUNDS - 1
-            drive = [wavelet] if kind == "u" else [traces, depth]
-            specs = [SMEM] + ([SMEM] if kind == "u" else vmem(2))
-            args = state[kind] + [slow, aniso] + bands
+            args = [place_info] + ([pulse, pulse_depth] if kind == "u" else [traces, depth])
+            args += state[kind] + [slow, aniso] + bands
             if later:
                 partner = ROUNDS - 1 - r
                 args += [mids[partner], ends[partner]] if kind == "u" else [history[partner]]
                 if r > ROUNDS // 2:
                     args += [totals[kind]]
-            specs = specs + vmem(len(args))
-            outs = [own_shape, ext_shape] + ([] if last else [halo, halo])
+            outs = [own_shape, (EXT_SHAPE, F32)] + ([] if last else [halo, halo])
             if later:
                 outs.append(((2, NXA, ZS, 128), F32))
             elif kind == "u":
@@ -810,11 +804,11 @@
             res = call(
                 functools.partial(round_kernel, kind, r),
                 outs,
-                specs,
-                [pltpu.VMEM((NXA + 2 * PADX, ZE, 128), F32)] * 2,
+                vmem(len(args)),
+                round_scratch(),
                 moved=4 * MIB,
                 flops=1 << 24,
-            )(scal, *drive, *args)
+            )(*args)
             own, mid = res[0], res[1]
             if later:
                 totals[kind] = res[-1]

time: 172 us -> 169 us (0.983)
  Pallas kernels: 63.3 us -> 57.3 us
  starting transfers between devices: 67.3 us -> 72.1 us
  waiting for transfers between devices: 35 us -> 33 us
    pallas_call x17, Pallas kernels: 30.4 us -> 23.7 us  [the longest x16 22.6 us: slab_body(): call(functools.partial(round_kernel, kind, r), outs, vmem(len(args)), rou...]
    ppermute x17, starting transfers between devices: 13.7 us -> 19.6 us  [to_off_chip(): return lax.ppermute(x, ('gx', 'gy', 'gz'), OFF_PAIRS)]
    ppermute x20, starting transfers between devices: 11.7 us -> 9.68 us  [to_sibling(): return lax.ppermute(x, 'gz', SWAP)]
  transfers between devices with their start and end apart: 48 -> 48, of which waited for: 23 -> 22; matrix products, arithmetic and copies ran while one was open for 1% -> 1% of each run, Pallas kernels for 29% -> 26%
where the time goes in v3:
time: 169 us
  starting transfers between devices  72.1 us (43%)
  Pallas kernels  57.3 us (34%)
  waiting for transfers between devices  33 us (20%)
  local copies, waits for them, and re-layouts  5.22 us (3%)
    ppermute x8, starting transfers between devices, to_blocks(): return lax.ppermute(x, ('gx', 'gy', 'gz'), spread(e))  30.5 us
    pallas_call x16, Pallas kernels, slab_body(): call(functools.partial(round_kernel, kind, r), outs, vmem(len(args)), rou...  22.6 us
    ppermute x17, starting transfers between devices, to_off_chip(): return lax.ppermute(x, ('gx', 'gy', 'gz'), OFF_PAIRS)  19.6 us
    all_to_all x2, waiting for transfers between devices, exchange(): lax.all_to_all(x, ('gx', 'gy'), split_axis=0, concat_axis=0, tiled=True)  11.9 us
    ppermute x8, waiting for transfers between devices, to_blocks(): return lax.ppermute(x, ('gx', 'gy', 'gz'), spread(e))  11.1 us
    all_to_all x2, starting transfers between devices, exchange(): lax.all_to_all(x, ('gx', 'gy'), split_axis=0, concat_axis=0, tiled=True)  11 us
    ppermute x20, starting transfers between devices, to_sibling(): return lax.ppermute(x, 'gz', SWAP)  9.68 us
    pallas_call x1, Pallas kernels, slab_body(): call(functools.partial(gather_half, True), [coef_shape, half_shape, half_...  8.11 us
  transfers between devices with their start and end apart: 48, of which 22 were waited for; matrix products, arithmetic and copies ran while one was open for 1% of the time, Pallas kernels for 26%

profile of v3, /device:TPU:1, one launch (start us, length us, event | category | flops | bytes accessed | tf_op | source)
XLA Modules:
  0.0 168.8 jit_solution(4372047060505384091)
XLA Ops:
  2.7 1.6 shard_map.158
  6.6 1.5 shard_map.160
  8.1 7.0 %all-to-all-start.1 = ((f32[8,168,128]{2,1,0:T(8,128)}), f32[8,168,128]{2,1,0:T(8,128)S(1)}, u32[]{:S(2)}, u32[]{:S(2)}) async-start(f32[8,168,128]{2,1,0:T(8,128)} %shard_map.160), calls=%async_computation.1 | async-start | bytes 1376256 | tf_op jit(solution)/shard_map/all_to_all | solution.py:695
  15.1 2.7 %shard_map.157 = (f32[4,4,4,16,128]{4,3,2,1,0:T(8,128)S(1)}, f32[4,4,4,16,128]{4,3,2,1,0:T(8,128)S(1)}) custom-call(s32[8]{0:T(128)S(1)} %stack.32.scal, f32[8,64,128]{2,1,0:T(8,128)S(1)} %copy-done.5, f32[8,64,128]{2,1,0:T(8,128)S(1)} %copy-done.6, f32[8,64,128]{2,1,0:T(8,128)S(1)} %copy-done.7, f32[8,64,128]{2,1,0:T(8,128)S(1)} %copy-done.8), custom_call_target="tpu_custom_call" | custom-call | flops 1048576 | bytes 2097152 | tf_op jit(solution)/shard_map/pallas_call | solution.py:735
  18.2 1.5 collective-permute-done
  21.0 11.9 %all-to-all-done.1 = f32[8,168,128]{2,1,0:T(8,128)S(1)} async-done(((f32[8,168,128]{2,1,0:T(8,128)}), f32[8,168,128]{2,1,0:T(8,128)S(1)}, u32[]{:S(2)}, u32[]{:S(2)}) %all-to-all-start.1) | async-done | bytes 688160 | tf_op jit(solution)/shard_map/all_to_all | solution.py:695
  32.9 4.0 %all-to-all-start = ((f32[8,4,4,16,128]{4,3,2,1,0:T(8,128)}), f32[8,4,4,16,128]{4,3,2,1,0:T(8,128)S(1)}, u32[]{:S(2)}, u32[]{:S(2)}) async-start(f32[8,4,4,16,128]{4,3,2,1,0:T(8,128)} %bitcast.22), calls=%async_computation | async-start | bytes 2097152 | tf_op jit(solution)/shard_map/all_to_all | solution.py:695
  41.6 7.2 %shard_map.164.refs_0_ = f32[32,32,128]{2,1,0:T(8,128)S(1)} custom-call(s32[8]{0:T(128)S(1)} %stack.32.scal, f32[8,4,32,128]{3,2,1,0:T(8,128)S(1)} %bitcast.18, s32[32,128]{1,0:T(8,128)S(1)} %get-tuple-element.115.ids_slab.ids), custom_call_target="tpu_custom_call" | custom-call | flops 16777216 | bytes 1048576 | tf_op jit(solution)/shard_map/pallas_call | solution.py:750
  49.7 8.1 %shard_map.165 = (f32[32,32,128]{2,1,0:T(8,128)S(1)}, f32[32,16,128]{2,1,0:T(8,128)}, f32[32,16,128]{2,1,0:T(8,128)S(1)}) custom-call(s32[8]{0:T(128)S(1)} %stack.32.scal, f32[8,4,32,128]{3,2,1,0:T(8,128)S(1)} %collective-permute-done.5.table, s32[32,128]{1,0:T(8,128)S(1)} %get-tuple-element.115.ids_slab.ids, f32[32,32,128]{2,1,0:T(8,128)S(1)} %shard_map.164.refs_0_), custom_call_target="tpu_custom_call" | custom-call | flops 16777216 | bytes 2097152 | tf_op jit(solution)/shard_map/pallas_call | solution.py:753
  57.8 1.6 collective-permute-start.6
  59.5 1.8 %shard_map.162.index = s32[2,40,128]{2,1,0:T(8,128)S(1)} custom-call(s32[8]{0:T(128)S(1)} %stack.32.scal, s32[32,128]{1,0:T(8,128)S(1)} %get-tuple-element.115.ids_slab.ids, s32[32,128]{1,0:T(8,128)S(1)} %get-tuple-element.116.ids_owner), custom_call_target="tpu_custom_call" | custom-call | flops 16777216 | bytes 262144 | tf_op jit(solution)/shard_map/pallas_call | solution.py:765
  61.3 1.4 collective-permute-start.7
  68.1 2.6 %collective-permute-done.4.refs_5_ = f32[2,32,8,128]{3,2,1,0:T(8,128)S(1)} collective-permute-done((f32[2,32,8,128]{3,2,1,0:T(8,128)S(1)}, f32[2,32,8,128]{3,2,1,0:T(8,128)S(1)}, u32[]{:S(2)}, u32[]{:S(2)}) %collective-permute-start.4) | collective-permute-done | bytes 262176 | tf_op jit(solution)/shard_map/ppermute | solution.py:204
  94.8 1.6 shard_map.175
  100.9 1.4 shard_map.176
  103.9 1.4 shard_map.180
  107.2 1.4 shard_map.177
  110.2 1.4 shard_map.181
  113.2 1.8 %shard_map.178 = (f32[32,16,128]{2,1,0:T(8,128)S(1)}, f32[40,32,128]{2,1,0:T(8,128)}, f32[2,32,16,128]{3,2,1,0:T(8,128)S(1)}) custom-call(s32[3,8,128]{2,1,0:T(8,128)S(1)} %get-tuple-element.118.refs_0_, f32[16,32,128]{2,1,0:T(8,128)S(1)} %get-tuple-element.119.refs_1_, s32[32,128]{1,0:T(8,128)S(1)} %get-tuple-element.120.refs_2_, ...), custom_call_target="tpu_custom_call" | custom-call | flops 16777216 | bytes 4194304 | tf_op jit(solution)/shard_map/pallas_call | solution.py:804
  116.2 1.8 %shard_map.182 = (f32[32,16,128]{2,1,0:T(8,128)S(1)}, f32[40,32,128]{2,1,0:T(8,128)}, f32[2,32,16,128]{3,2,1,0:T(8,128)S(1)}) custom-call(s32[3,8,128]{2,1,0:T(8,128)S(1)} %get-tuple-element.118.refs_0_, f32[16,32,128]{2,1,0:T(8,128)S(1)} %get-tuple-element.147.refs_1_, s32[32,128]{1,0:T(8,128)S(1)} %get-tuple-element.148.refs_2_, ...), custom_call_target="tpu_custom_call" | custom-call | flops 16777216 | bytes 4194304 | tf_op jit(solution)/shard_map/pallas_call | solution.py:804
  118.1 5.8 %shard_map.183 = (f32[384,128]{1,0:T(8,128)S(1)}, f32[384,128]{1,0:T(8,128)S(1)}, f32[384,128]{1,0:T(8,128)S(1)}, f32[384,128]{1,0:T(8,128)S(1)}, f32[384,128]{1...) custom-call(s32[8]{0:T(128)S(1)} %stack.32.scal, ...), custom_call_target="tpu_custom_call" | custom-call | flops 4194304 | bytes 4194304 | tf_op jit(solution)/shard_map/pallas_call | solution.py:824
  123.9 3.2 %collective-permute-start.38 = (f32[384,128]{1,0:T(8,128)S(1)}, f32[384,128]{1,0:T(8,128)S(1)}, u32[]{:S(2)}, u32[]{:S(2)}) collective-permute-start(f32[384,128]{1,0:T(8,128)S(1)} %get-tuple-element.209), channel_id=1, source_target_pairs={{0,12},{1,14},{2,15},{3,13},{4,8},{5,10},{6,11},{7,9},{8,4},{9,6},... | collective-permute-start | bytes 589832 | tf_op jit(solution)/shard_map/ppermute | solution.py:212
  127.7 1.9 %collective-permute-start.40 = (f32[384,128]{1,0:T(8,128)S(1)}, f32[384,128]{1,0:T(8,128)S(1)}, u32[]{:S(2)}, u32[]{:S(2)}) collective-permute-start(f32[384,128]{1,0:T(8,128)S(1)} %get-tuple-element.211), channel_id=1, source_target_pairs={{0,8},{1,10},{2,11},{3,9},{4,12},{5,14},{6,15},{7,13},{8,0},{9,2},... | collective-permute-start | bytes 589832 | tf_op jit(solution)/shard_map/ppermute | solution.py:212
  129.7 1.6 collective-permute-start.41
  132.8 16.7 %collective-permute-start.43 = (f32[384,128]{1,0:T(8,128)S(1)}, f32[384,128]{1,0:T(8,128)S(1)}, u32[]{:S(2)}, u32[]{:S(2)}) collective-permute-start(f32[384,128]{1,0:T(8,128)S(1)} %get-tuple-element.214), channel_id=1, source_target_pairs={{0,6},{1,4},{2,5},{3,7},{4,2},{5,0},{6,1},{7,3},{8,14},{9,12},{10,... | collective-permute-start | bytes 589832 | tf_op jit(solution)/shard_map/ppermute | solution.py:212
  149.5 2.9 %collective-permute-start.44 = (f32[384,128]{1,0:T(8,128)S(1)}, f32[384,128]{1,0:T(8,128)S(1)}, u32[]{:S(2)}, u32[]{:S(2)}) collective-permute-start(f32[384,128]{1,0:T(8,128)S(1)} %get-tuple-element.215), channel_id=1, source_target_pairs={{0,0},{1,2},{2,3},{3,1},{4,4},{5,6},{6,7},{7,5},{8,8},{9,10},{10,1... | collective-permute-start | bytes 589832 | tf_op jit(solution)/shard_map/ppermute | solution.py:212
  152.4 4.9 %collective-permute-done.40.refs_2_ = f32[384,128]{1,0:T(8,128)S(1)} collective-permute-done((f32[384,128]{1,0:T(8,128)S(1)}, f32[384,128]{1,0:T(8,128)S(1)}, u32[]{:S(2)}, u32[]{:S(2)}) %collective-permute-start.40) | collective-permute-done | bytes 196640 | tf_op jit(solution)/shard_map/ppermute | solution.py:212
  157.3 2.4 %collective-permute-start.45 = (f32[384,128]{1,0:T(8,128)S(1)}, f32[384,128]{1,0:T(8,128)S(1)}, u32[]{:S(2)}, u32[]{:S(2)}) collective-permute-start(f32[384,128]{1,0:T(8,128)S(1)} %get-tuple-element.207), channel_id=1, source_target_pairs={{0,2},{1,0},{2,1},{3,3},{4,6},{5,4},{6,5},{7,7},{8,10},{9,8},{10,9... | collective-permute-start | bytes 589832 | tf_op jit(solution)/shard_map/ppermute | solution.py:212
  160.1 1.8 %collective-permute-done.41.refs_3_ = f32[384,128]{1,0:T(8,128)S(1)} collective-permute-done((f32[384,128]{1,0:T(8,128)S(1)}, f32[384,128]{1,0:T(8,128)S(1)}, u32[]{:S(2)}, u32[]{:S(2)}) %collective-permute-start.41) | collective-permute-done | bytes 196640 | tf_op jit(solution)/shard_map/ppermute | solution.py:212
  161.9 1.9 %collective-permute-done.43.refs_5_ = f32[384,128]{1,0:T(8,128)S(1)} collective-permute-done((f32[384,128]{1,0:T(8,128)S(1)}, f32[384,128]{1,0:T(8,128)S(1)}, u32[]{:S(2)}, u32[]{:S(2)}) %collective-permute-start.43) | collective-permute-done | bytes 196640 | tf_op jit(solution)/shard_map/ppermute | solution.py:212
  163.8 2.0 %collective-permute-done.45.refs_7_ = f32[384,128]{1,0:T(8,128)S(1)} collective-permute-done((f32[384,128]{1,0:T(8,128)S(1)}, f32[384,128]{1,0:T(8,128)S(1)}, u32[]{:S(2)}, u32[]{:S(2)}) %collective-permute-start.45) | collective-permute-done | bytes 196640 | tf_op jit(solution)/shard_map/ppermute | solution.py:212
  165.8 3.0 %shard_map.185 = (f32[8,64,128]{2,1,0:T(8,128)}, f32[8,64,128]{2,1,0:T(8,128)}, f32[2048,128]{1,0:T(8,128)}) custom-call(s32[8]{0:T(128)S(1)} %stack.32.scal, bf16[1024,1024]{1,0:T(8,128)(2,1)S(1)} %shard_map.184.picks, f32[384,128]{1,0:T(8,128)S(1)} %collective-permute-done.38.refs_0_, f32[384,128]{1,0:T(8,128)S(1)} %collective-permute-done.39.refs_1_, ...), custom_call_target="tpu_custom_call" | custom-call | flops 268435456 | bytes 4194304 | tf_op jit(solution)/shard_map/pallas_call | solution.py:835
  (126 shorter events, 55.8 us)
Async XLA Ops:
  8.1 24.8 %all-to-all-start.1 = ((f32[8,168,128]{2,1,0:T(8,128)}), f32[8,168,128]{2,1,0:T(8,128)S(1)}, u32[]{:S(2)}, u32[]{:S(2)}) async-start(f32[8,168,128]{2,1,0:T(8,128)} %shard_map.160), calls=%async_computation.1 | async-start | bytes 1376256 | tf_op jit(solution)/shard_map/all_to_all | solution.py:695
  32.9 29.8 %all-to-all-start = ((f32[8,4,4,16,128]{4,3,2,1,0:T(8,128)}), f32[8,4,4,16,128]{4,3,2,1,0:T(8,128)S(1)}, u32[]{:S(2)}, u32[]{:S(2)}) async-start(f32[8,4,4,16,128]{4,3,2,1,0:T(8,128)} %bitcast.22), calls=%async_computation | async-start | bytes 2097152 | tf_op jit(solution)/shard_map/all_to_all | solution.py:695
  36.9 12.8 %collective-permute-start.5 = (f32[8,4,32,128]{3,2,1,0:T(8,128)S(1)}, f32[8,4,32,128]{3,2,1,0:T(8,128)S(1)}, u32[]{:S(2)}, u32[]{:S(2)}) collective-permute-start(f32[8,4,32,128]{3,2,1,0:T(8,128)S(1)} %bitcast.17), channel_id=1, source_target_pairs={{0,16},{16,0},{1,17},{17,1},{2,18},{18,2},{3,19},{19,3},{4,20},{20... | collective-permute-start | bytes 1572872 | tf_op jit(solution)/shard_map/ppermute | solution.py:732
  57.8 8.3 %collective-permute-start.6 = (f32[32,16,128]{2,1,0:T(8,128)}, f32[32,16,128]{2,1,0:T(8,128)S(1)}, u32[]{:S(2)}, u32[]{:S(2)}) collective-permute-start(f32[32,16,128]{2,1,0:T(8,128)} %get-tuple-element.127), channel_id=1, source_target_pairs={{0,1},{1,0},{2,3},{3,2},{4,5},{5,4},{6,7},{7,6},{8,9},{9,8},{10,11... | collective-permute-start | bytes 786440 | tf_op jit(solution)/shard_map/ppermute | solution.py:200
  61.3 6.2 %collective-permute-start.7 = (f32[32,16,128]{2,1,0:T(8,128)S(1)}, f32[32,16,128]{2,1,0:T(8,128)S(1)}, u32[]{:S(2)}, u32[]{:S(2)}) collective-permute-start(f32[32,16,128]{2,1,0:T(8,128)S(1)} %get-tuple-element.128), channel_id=1, source_target_pairs={{1,4},{4,1},{5,8},{8,5},{9,12},{12,9},{13,14},{14,13},{15,10},{10,... | collective-permute-start | bytes 786440 | tf_op jit(solution)/shard_map/ppermute | solution.py:204
  63.6 4.5 %collective-permute-start.3 = (f32[2,32,8,128]{3,2,1,0:T(8,128)S(1)}, f32[2,32,8,128]{3,2,1,0:T(8,128)S(1)}, u32[]{:S(2)}, u32[]{:S(2)}) collective-permute-start(f32[2,32,8,128]{3,2,1,0:T(8,128)S(1)} %get-tuple-element.123), channel_id=1, source_target_pairs={{0,1},{1,0},{2,3},{3,2},{4,5},{5,4},{6,7},{7,6},{8,9},{9,8},{10,11... | collective-permute-start | bytes 786440 | tf_op jit(solution)/shard_map/ppermute | solution.py:200
  64.6 6.1 %collective-permute-start.4 = (f32[2,32,8,128]{3,2,1,0:T(8,128)S(1)}, f32[2,32,8,128]{3,2,1,0:T(8,128)S(1)}, u32[]{:S(2)}, u32[]{:S(2)}) collective-permute-start(f32[2,32,8,128]{3,2,1,0:T(8,128)S(1)} %get-tuple-element.124), channel_id=1, source_target_pairs={{1,4},{4,1},{5,8},{8,5},{9,12},{12,9},{13,14},{14,13},{15,10},{10,... | collective-permute-start | bytes 786440 | tf_op jit(solution)/shard_map/ppermute | solution.py:204
  65.3 8.2 %collective-permute-start.16 = (f32[2,32,8,128]{3,2,1,0:T(8,128)S(1)}, f32[2,32,8,128]{3,2,1,0:T(8,128)S(1)}, u32[]{:S(2)}, u32[]{:S(2)}) collective-permute-start(f32[2,32,8,128]{3,2,1,0:T(8,128)S(1)} %get-tuple-element.150), channel_id=1, source_target_pairs={{0,1},{1,0},{2,3},{3,2},{4,5},{5,4},{6,7},{7,6},{8,9},{9,8},{10,11... | collective-permute-start | bytes 786440 | tf_op jit(solution)/shard_map/ppermute | solution.py:200
  66.2 7.3 %collective-permute-start.17 = (f32[2,32,8,128]{3,2,1,0:T(8,128)S(1)}, f32[2,32,8,128]{3,2,1,0:T(8,128)S(1)}, u32[]{:S(2)}, u32[]{:S(2)}) collective-permute-start(f32[2,32,8,128]{3,2,1,0:T(8,128)S(1)} %get-tuple-element.151), channel_id=1, source_target_pairs={{1,4},{4,1},{5,8},{8,5},{9,12},{12,9},{13,14},{14,13},{15,10},{10,... | collective-permute-start | bytes 786440 | tf_op jit(solution)/shard_map/ppermute | solution.py:204
  72.0 4.4 %collective-permute-start.8 = (f32[1,32,8,128]{3,2,1,0:T(8,128)S(1)}, f32[1,32,8,128]{3,2,1,0:T(8,128)S(1)}, u32[]{:S(2)}, u32[]{:S(2)}) collective-permute-start(f32[1,32,8,128]{3,2,1,0:T(8,128)S(1)} %get-tuple-element.132), channel_id=1, source_target_pairs={{0,1},{1,0},{2,3},{3,2},{4,5},{5,4},{6,7},{7,6},{8,9},{9,8},{10,11... | collective-permute-start | bytes 393224 | tf_op jit(solution)/shard_map/ppermute | solution.py:200
  72.1 4.5 %collective-permute-start.9 = (f32[1,32,8,128]{3,2,1,0:T(8,128)S(1)}, f32[1,32,8,128]{3,2,1,0:T(8,128)S(1)}, u32[]{:S(2)}, u32[]{:S(2)}) collective-permute-start(f32[1,32,8,128]{3,2,1,0:T(8,128)S(1)} %get-tuple-element.133), channel_id=1, source_target_pairs={{1,4},{4,1},{5,8},{8,5},{9,12},{12,9},{13,14},{14,13},{15,10},{10,... | collective-permute-start | bytes 393224 | tf_op jit(solution)/shard_map/ppermute | solution.py:204
  74.8 4.6 %collective-permute-start.18 = (f32[1,32,8,128]{3,2,1,0:T(8,128)S(1)}, f32[1,32,8,128]{3,2,1,0:T(8,128)S(1)}, u32[]{:S(2)}, u32[]{:S(2)}) collective-permute-start(f32[1,32,8,128]{3,2,1,0:T(8,128)S(1)} %get-tuple-element.154), channel_id=1, source_target_pairs={{0,1},{1,0},{2,3},{3,2},{4,5},{5,4},{6,7},{7,6},{8,9},{9,8},{10,11... | collective-permute-start | bytes 393224 | tf_op jit(solution)/shard_map/ppermute | solution.py:200
  77.9 4.4 %collective-permute-start.10 = (f32[1,32,8,128]{3,2,1,0:T(8,128)S(1)}, f32[1,32,8,128]{3,2,1,0:T(8,128)S(1)}, u32[]{:S(2)}, u32[]{:S(2)}) collective-permute-start(f32[1,32,8,128]{3,2,1,0:T(8,128)S(1)} %get-tuple-element.136), channel_id=1, source_target_pairs={{0,1},{1,0},{2,3},{3,2},{4,5},{5,4},{6,7},{7,6},{8,9},{9,8},{10,11... | collective-permute-start | bytes 393224 | tf_op jit(solution)/shard_map/ppermute | solution.py:200
  80.7 4.8 %collective-permute-start.20 = (f32[1,32,8,128]{3,2,1,0:T(8,128)S(1)}, f32[1,32,8,128]{3,2,1,0:T(8,128)S(1)}, u32[]{:S(2)}, u32[]{:S(2)}) collective-permute-start(f32[1,32,8,128]{3,2,1,0:T(8,128)S(1)} %get-tuple-element.158), channel_id=1, source_target_pairs={{0,1},{1,0},{2,3},{3,2},{4,5},{5,4},{6,7},{7,6},{8,9},{9,8},{10,11... | collective-permute-start | bytes 393224 | tf_op jit(solution)/shard_map/ppermute | solution.py:200
  84.2 4.4 %collective-permute-start.13 = (f32[1,32,8,128]{3,2,1,0:T(8,128)S(1)}, f32[1,32,8,128]{3,2,1,0:T(8,128)S(1)}, u32[]{:S(2)}, u32[]{:S(2)}) collective-permute-start(f32[1,32,8,128]{3,2,1,0:T(8,128)S(1)} %get-tuple-element.141), channel_id=1, source_target_pairs={{1,4},{4,1},{5,8},{8,5},{9,12},{12,9},{13,14},{14,13},{15,10},{10,... | collective-permute-start | bytes 393224 | tf_op jit(solution)/shard_map/ppermute | solution.py:204
  86.9 4.5 %collective-permute-start.22 = (f32[1,32,8,128]{3,2,1,0:T(8,128)S(1)}, f32[1,32,8,128]{3,2,1,0:T(8,128)S(1)}, u32[]{:S(2)}, u32[]{:S(2)}) collective-permute-start(f32[1,32,8,128]{3,2,1,0:T(8,128)S(1)} %get-tuple-element.162), channel_id=1, source_target_pairs={{0,1},{1,0},{2,3},{3,2},{4,5},{5,4},{6,7},{7,6},{8,9},{9,8},{10,11... | collective-permute-start | bytes 393224 | tf_op jit(solution)/shard_map/ppermute | solution.py:200
  92.8 5.0 %collective-permute-start.30 = (f32[1,32,8,128]{3,2,1,0:T(8,128)S(1)}, f32[1,32,8,128]{3,2,1,0:T(8,128)S(1)}, u32[]{:S(2)}, u32[]{:S(2)}) collective-permute-start(f32[1,32,8,128]{3,2,1,0:T(8,128)S(1)} %get-tuple-element.183), channel_id=1, source_target_pairs={{0,1},{1,0},{2,3},{3,2},{4,5},{5,4},{6,7},{7,6},{8,9},{9,8},{10,11... | collective-permute-start | bytes 393224 | tf_op jit(solution)/shard_map/ppermute | solution.py:200
  93.2 4.6 %collective-permute-start.31 = (f32[1,32,8,128]{3,2,1,0:T(8,128)S(1)}, f32[1,32,8,128]{3,2,1,0:T(8,128)S(1)}, u32[]{:S(2)}, u32[]{:S(2)}) collective-permute-start(f32[1,32,8,128]{3,2,1,0:T(8,128)S(1)} %get-tuple-element.184), channel_id=1, source_target_pairs={{1,4},{4,1},{5,8},{8,5},{9,12},{12,9},{13,14},{14,13},{15,10},{10,... | collective-permute-start | bytes 393224 | tf_op jit(solution)/shard_map/ppermute | solution.py:204
  96.3 4.5 %collective-permute-start.24 = (f32[1,32,8,128]{3,2,1,0:T(8,128)S(1)}, f32[1,32,8,128]{3,2,1,0:T(8,128)S(1)}, u32[]{:S(2)}, u32[]{:S(2)}) collective-permute-start(f32[1,32,8,128]{3,2,1,0:T(8,128)S(1)} %get-tuple-element.168), channel_id=1, source_target_pairs={{0,1},{1,0},{2,3},{3,2},{4,5},{5,4},{6,7},{7,6},{8,9},{9,8},{10,11... | collective-permute-start | bytes 393224 | tf_op jit(solution)/shard_map/ppermute | solution.py:200
  99.2 4.7 %collective-permute-start.32 = (f32[1,32,8,128]{3,2,1,0:T(8,128)S(1)}, f32[1,32,8,128]{3,2,1,0:T(8,128)S(1)}, u32[]{:S(2)}, u32[]{:S(2)}) collective-permute-start(f32[1,32,8,128]{3,2,1,0:T(8,128)S(1)} %get-tuple-element.187), channel_id=1, source_target_pairs={{0,1},{1,0},{2,3},{3,2},{4,5},{5,4},{6,7},{7,6},{8,9},{9,8},{10,11... | collective-permute-start | bytes 393224 | tf_op jit(solution)/shard_map/ppermute | solution.py:200
  102.3 4.7 %collective-permute-start.26 = (f32[1,32,8,128]{3,2,1,0:T(8,128)S(1)}, f32[1,32,8,128]{3,2,1,0:T(8,128)S(1)}, u32[]{:S(2)}, u32[]{:S(2)}) collective-permute-start(f32[1,32,8,128]{3,2,1,0:T(8,128)S(1)} %get-tuple-element.173), channel_id=1, source_target_pairs={{0,1},{1,0},{2,3},{3,2},{4,5},{5,4},{6,7},{7,6},{8,9},{9,8},{10,11... | collective-permute-start | bytes 393224 | tf_op jit(solution)/shard_map/ppermute | solution.py:200
  105.4 4.7 %collective-permute-start.34 = (f32[1,32,8,128]{3,2,1,0:T(8,128)S(1)}, f32[1,32,8,128]{3,2,1,0:T(8,128)S(1)}, u32[]{:S(2)}, u32[]{:S(2)}) collective-permute-start(f32[1,32,8,128]{3,2,1,0:T(8,128)S(1)} %get-tuple-element.193), channel_id=1, source_target_pairs={{0,1},{1,0},{2,3},{3,2},{4,5},{5,4},{6,7},{7,6},{8,9},{9,8},{10,11... | collective-permute-start | bytes 393224 | tf_op jit(solution)/shard_map/ppermute | solution.py:200
  108.6 4.5 %collective-permute-start.28 = (f32[1,32,8,128]{3,2,1,0:T(8,128)S(1)}, f32[1,32,8,128]{3,2,1,0:T(8,128)S(1)}, u32[]{:S(2)}, u32[]{:S(2)}) collective-permute-start(f32[1,32,8,128]{3,2,1,0:T(8,128)S(1)} %get-tuple-element.178), channel_id=1, source_target_pairs={{0,1},{1,0},{2,3},{3,2},{4,5},{5,4},{6,7},{7,6},{8,9},{9,8},{10,11... | collective-permute-start | bytes 393224 | tf_op jit(solution)/shard_map/ppermute | solution.py:200
  108.8 4.4 %collective-permute-start.29 = (f32[1,32,8,128]{3,2,1,0:T(8,128)S(1)}, f32[1,32,8,128]{3,2,1,0:T(8,128)S(1)}, u32[]{:S(2)}, u32[]{:S(2)}) collective-permute-start(f32[1,32,8,128]{3,2,1,0:T(8,128)S(1)} %get-tuple-element.179), channel_id=1, source_target_pairs={{1,4},{4,1},{5,8},{8,5},{9,12},{12,9},{13,14},{14,13},{15,10},{10,... | collective-permute-start | bytes 393224 | tf_op jit(solution)/shard_map/ppermute | solution.py:204
  123.9 9.0 %collective-permute-start.38 = (f32[384,128]{1,0:T(8,128)S(1)}, f32[384,128]{1,0:T(8,128)S(1)}, u32[]{:S(2)}, u32[]{:S(2)}) collective-permute-start(f32[384,128]{1,0:T(8,128)S(1)} %get-tuple-element.209), channel_id=1, source_target_pairs={{0,12},{1,14},{2,15},{3,13},{4,8},{5,10},{6,11},{7,9},{8,4},{9,6},... | collective-permute-start | bytes 589832 | tf_op jit(solution)/shard_map/ppermute | solution.py:212
  127.1 22.4 %collective-permute-start.39 = (f32[384,128]{1,0:T(8,128)S(1)}, f32[384,128]{1,0:T(8,128)S(1)}, u32[]{:S(2)}, u32[]{:S(2)}) collective-permute-start(f32[384,128]{1,0:T(8,128)S(1)} %get-tuple-element.210), channel_id=1, source_target_pairs={{0,14},{1,12},{2,13},{3,15},{4,10},{5,8},{6,9},{7,11},{8,6},{9,4},... | collective-permute-start | bytes 589832 | tf_op jit(solution)/shard_map/ppermute | solution.py:212
  127.7 29.6 %collective-permute-start.40 = (f32[384,128]{1,0:T(8,128)S(1)}, f32[384,128]{1,0:T(8,128)S(1)}, u32[]{:S(2)}, u32[]{:S(2)}) collective-permute-start(f32[384,128]{1,0:T(8,128)S(1)} %get-tuple-element.211), channel_id=1, source_target_pairs={{0,8},{1,10},{2,11},{3,9},{4,12},{5,14},{6,15},{7,13},{8,0},{9,2},... | collective-permute-start | bytes 589832 | tf_op jit(solution)/shard_map/ppermute | solution.py:212
  129.7 32.2 %collective-permute-start.41 = (f32[384,128]{1,0:T(8,128)S(1)}, f32[384,128]{1,0:T(8,128)S(1)}, u32[]{:S(2)}, u32[]{:S(2)}) collective-permute-start(f32[384,128]{1,0:T(8,128)S(1)} %get-tuple-element.212), channel_id=1, source_target_pairs={{0,10},{1,8},{2,9},{3,11},{4,14},{5,12},{6,13},{7,15},{8,2},{9,0},... | collective-permute-start | bytes 589832 | tf_op jit(solution)/shard_map/ppermute | solution.py:212
  131.3 30.6 %collective-permute-start.42 = (f32[384,128]{1,0:T(8,128)S(1)}, f32[384,128]{1,0:T(8,128)S(1)}, u32[]{:S(2)}, u32[]{:S(2)}) collective-permute-start(f32[384,128]{1,0:T(8,128)S(1)} %get-tuple-element.213), channel_id=1, source_target_pairs={{0,4},{1,6},{2,7},{3,5},{4,0},{5,2},{6,3},{7,1},{8,12},{9,14},{10,... | collective-permute-start | bytes 589832 | tf_op jit(solution)/shard_map/ppermute | solution.py:212
  132.8 31.0 %collective-permute-start.43 = (f32[384,128]{1,0:T(8,128)S(1)}, f32[384,128]{1,0:T(8,128)S(1)}, u32[]{:S(2)}, u32[]{:S(2)}) collective-permute-start(f32[384,128]{1,0:T(8,128)S(1)} %get-tuple-element.214), channel_id=1, source_target_pairs={{0,6},{1,4},{2,5},{3,7},{4,2},{5,0},{6,1},{7,3},{8,14},{9,12},{10,... | collective-permute-start | bytes 589832 | tf_op jit(solution)/shard_map/ppermute | solution.py:212
  149.5 14.3 %collective-permute-start.44 = (f32[384,128]{1,0:T(8,128)S(1)}, f32[384,128]{1,0:T(8,128)S(1)}, u32[]{:S(2)}, u32[]{:S(2)}) collective-permute-start(f32[384,128]{1,0:T(8,128)S(1)} %get-tuple-element.215), channel_id=1, source_target_pairs={{0,0},{1,2},{2,3},{3,1},{4,4},{5,6},{6,7},{7,5},{8,8},{9,10},{10,1... | collective-permute-start | bytes 589832 | tf_op jit(solution)/shard_map/ppermute | solution.py:212
  157.3 8.5 %collective-permute-start.45 = (f32[384,128]{1,0:T(8,128)S(1)}, f32[384,128]{1,0:T(8,128)S(1)}, u32[]{:S(2)}, u32[]{:S(2)}) collective-permute-start(f32[384,128]{1,0:T(8,128)S(1)} %get-tuple-element.207), channel_id=1, source_target_pairs={{0,2},{1,0},{2,1},{3,3},{4,6},{5,4},{6,5},{7,7},{8,10},{9,8},{10,9... | collective-permute-start | bytes 589832 | tf_op jit(solution)/shard_map/ppermute | solution.py:212
  (29 other events, 225.9 us)

commit v4 on v3

--- a/solution.py
+++ b/solution.py
@@ -296,10 +296,9 @@
 
 
 def pack_table(scal, table, keep, give):
-    first = scal[SHOT] * 1024
     for q in range(4):
         for comp in range(2):
-            turned = table[pl.ds(first + q * 256 + comp, 128, stride=2), :].T
+            turned = table[pl.ds(q * 256 + comp, 128, stride=2), :].T
             at = q * 32 + comp * ZS
             for chunk in range(8):
                 mine, g = place(scal, chunk)
@@ -608,14 +607,7 @@
                 total[1, x] = sum_v
 
 
-def pack_out(scal, u, a, index, total_u, total_a, coefs, *refs):
-    outs, grads = refs[:8], refs[8]
-    for x in range(NXA):
-        gh = (total_u[0, x] + total_a[0, x]) * UNSCALE
-        gv = (total_u[1, x] + total_a[1, x]) * UNSCALE
-        slow, aniso = coefs[x, 0:ZS, :], coefs[x, ZS:, :]
-        grads[x, 0:ZS, :] = (1.0 + 2.0 * aniso) * gh + gv
-        grads[x, ZS:, :] = (2.0 * slow) * gh
+def pack_final(scal, u, a, *outs):
     low = half_lanes((ZS, 128))
     for n, out in enumerate(outs):
         block = block_of(scal, FAR_FIRST[n])
@@ -626,8 +618,19 @@
                 x1 = field[pl.ds(x + 1, 1)].reshape(ZS, 128)
                 piece = jnp.where(low, x0, roll_half(x1))
                 upper = jnp.where(low, roll_half(x0), x1)
-                at = 256 + (f * 4 + i) * ZS
-                out[at : at + ZS, :] = jnp.where((block & 1) == 0, piece, upper)
+                out[f, i] = jnp.where((block & 1) == 0, piece, upper)
+
+
+def pack_grads(scal, index, total_u, total_a, coefs, *refs):
+    outs, grads = refs[:8], refs[8]
+    for x in range(NXA):
+        gh = (total_u[0, x] + total_a[0, x]) * UNSCALE
+        gv = (total_u[1, x] + total_a[1, x]) * UNSCALE
+        slow, aniso = coefs[x, 0:ZS, :], coefs[x, ZS:, :]
+        grads[x, 0:ZS, :] = (1.0 + 2.0 * aniso) * gh + gv
+        grads[x, ZS:, :] = (2.0 * slow) * gh
+    for n, out in enumerate(outs):
+        block = block_of(scal, FAR_FIRST[n])
 
         def stripe(ix, carry, out=out, block=block):
             for part in range(2):
@@ -643,8 +646,7 @@
                         )
                         totals[t] = jnp.where(hit, value, totals[t])
                 for t in range(4):
-                    at = pl.multiple_of((ix * 2 + part) * 32 + 8 * t, 8)
-                    out[pl.ds(at, 8), :] = totals[t]
+                    out[ix * 2 + part, 8 * t : 8 * t + 8, :] = totals[t]
             return carry
 
         lax.fori_loop(0, GX, stripe, 0)
@@ -658,28 +660,29 @@
         picks[block * 256 : (block + 1) * 256, :] = pick.astype(F32).astype(BF16)
 
 
-def finish(scal, picks, *refs):
-    gots, (u_out, a_out, model, turned, columns) = refs[:8], refs[8:]
+def finish_fields(scal, *refs):
+    gots, (u_out, a_out, turned) = refs[:8], refs[8:]
     for f, out in enumerate((u_out, a_out)):
         for i in range(4):
             for n, e in enumerate(FAR_FIRST):
-                at = 256 + (f * 4 + i) * ZS
-                turned[pl.ds(slab_of(scal, e), ZS), :] = gots[n][at : at + ZS, :]
-            out[2 * i : 2 * i + 2] = turned[...].T.reshape(2, BY, 128)
+                turned[f * 4 + i, pl.ds(slab_of(scal, e), ZS), :] = gots[n][f, i]
+            out[2 * i : 2 * i + 2] = turned[f * 4 + i].T.reshape(2, BY, 128)
+
+
+def finish_model(scal, picks, *refs):
+    gots, (model, columns) = refs[:8], refs[8:]
     for n, e in enumerate(FAR_FIRST):
-        for m in range(8):
-            for comp in range(2):
-                rows = pl.ds(pl.multiple_of(comp * 128 + slab_of(scal, e), ZS), ZS)
-                at = m * 32 + comp * ZS
-                columns[rows, m * 128 : (m + 1) * 128] = gots[n][at : at + ZS, :]
-    values = columns[...]
+        for comp in range(2):
+            rows = pl.ds(pl.multiple_of(comp * 128 + slab_of(scal, e), ZS), ZS)
+            for m in range(8):
+                columns[rows, m * 128 : (m + 1) * 128] = gots[n][m, comp * ZS : (comp + 1) * ZS, :]
+    values = columns[...].T
     high = values.astype(BF16)
     rest = (values - high.astype(F32)).astype(BF16)
+    both = jnp.concatenate([high, rest], axis=1)
     for block in range(4):
-        pick = picks[block * 256 : (block + 1) * 256, :]
-        dims = (((1,), (1,)), ((), ()))
-        sums = lax.dot_general(pick, high, dims, preferred_element_type=F32)
-        sums = sums + lax.dot_general(pick, rest, dims, preferred_element_type=F32)
+        sums = jnp.dot(picks[block * 256 : (block + 1) * 256, :], both, preferred_element_type=F32)
+        sums = sums[:, :256] + sums[:, 256:]
         for comp in range(2):
             model[pl.ds(block * 512 + comp, 256, stride=2), :] = sums[:, comp * 128 : (comp + 1) * 128]
 
@@ -722,7 +725,7 @@
     )
     keep, give = call(
         pack_table, [((GX, 128, 128), F32)] * 2, [SMEM] + vmem(1), moved=2 * MIB, flops=1 << 20
-    )(scal, model_table.reshape(2048, 128))
+    )(scal, lax.dynamic_slice_in_dim(model_table.reshape(2048, 128), lax.axis_index("shots") * 1024, 1024, axis=0))
     (sent,) = call(assemble, [((GX * GY, 168, 128), F32)], [SMEM] + vmem(3), moved=2 * MIB, flops=1 << 20)(
         scal, keep, to_sibling(give), small
     )
@@ -821,25 +824,37 @@
             else:
                 state[kind] = [own, to_sibling(res[2]), to_off_chip(res[3]), mid]
 
-    packed = call(
-        pack_out,
-        [((384, 128), F32)] * 8,
-        [SMEM] + vmem(6),
+    final = call(
+        pack_final, [((2, 4, ZS, 128), F32)] * 8, [SMEM] + vmem(2), moved=MIB, flops=1 << 20
+    )(scal, state["u"][0], state["a"][0])
+    final = [to_blocks(x, e) for x, e in zip(final, FAR_FIRST)]
+    columns = call(
+        pack_grads,
+        [((8, 2 * ZS, 128), F32)] * 8,
+        [SMEM] + vmem(4),
         [pltpu.VMEM((NXA, 2 * ZS, 128), F32)],
-        moved=4 * MIB,
+        moved=16 * MIB,
         flops=1 << 22,
-    )(scal, state["u"][0], state["a"][0], index, totals["u"], totals["a"], coefs)
-    index, _ = lax.optimization_barrier((index, packed[7]))
+    )(scal, index, totals["u"], totals["a"], coefs)
+    index, _ = lax.optimization_barrier((index, columns[7]))
     (picks,) = call(name_slots, [((1024, 1024), BF16)], vmem(1), moved=4 * MIB, flops=1 << 22)(index)
-    arrived = [to_blocks(x, e) for x, e in zip(packed, FAR_FIRST)]
-    u, a, model = call(
-        finish,
-        [((BX, BY, BZ), F32)] * 2 + [((2048, 128), F32)],
+    columns = [to_blocks(x, e) for x, e in zip(columns, FAR_FIRST)]
+    u, a = call(
+        finish_fields,
+        [((BX, BY, BZ), F32)] * 2,
+        [SMEM] + vmem(8),
+        [pltpu.VMEM((8, 128, 128), F32)],
+        moved=MIB,
+        flops=1 << 20,
+    )(scal, *final)
+    (model,) = call(
+        finish_model,
+        [((2048, 128), F32)],
         [SMEM] + vmem(9),
-        [pltpu.VMEM((128, 128), F32), pltpu.VMEM((256, 1024), F32)],
+        [pltpu.VMEM((256, 1024), F32)],
         moved=4 * MIB,
         flops=1 << 28,
-    )(scal, picks, *arrived)
+    )(scal, picks, *columns)
     return (u, a, model.reshape(1, 1024, 2, 128))
 
 

time: 169 us -> 170 us (level)
  waiting for transfers between devices: 33 us -> 22 us
  local copies, waits for them, and re-layouts: 5.22 us -> 10.6 us
  starting transfers between devices: 72.1 us -> 77.3 us
    ppermute x8 -> x16, waiting for transfers between devices: 11.1 us -> 6.09 us  [to_blocks(): return lax.ppermute(x, ('gx', 'gy', 'gz'), spread(e))]
    ppermute x17, starting transfers between devices: 19.6 us -> 23.9 us  [to_off_chip(): return lax.ppermute(x, ('gx', 'gy', 'gz'), OFF_PAIRS)]
    ppermute x17, waiting for transfers between devices: 6.53 us -> 3.06 us  [to_off_chip(): return lax.ppermute(x, ('gx', 'gy', 'gz'), OFF_PAIRS)]
    unnamed x26 -> x32, local copies, waits for them, and re-layouts: 3.32 us -> 5.91 us
    pallas_call x16, Pallas kernels: 22.6 us -> 20 us  [slab_body(): call(functools.partial(round_kernel, kind, r), outs, vmem(len(args)), rou...]
    ppermute x8 -> x16, starting transfers between devices: 30.5 us -> 32.6 us  [to_blocks(): return lax.ppermute(x, ('gx', 'gy', 'gz'), spread(e))]
    pallas_call x2 -> x4, Pallas kernels: 8.78 us -> 10.5 us  [the longest x1 5.2 us: slab_body(): call(pack_grads, [((8, 2 * ZS, 128), F32)] * 8, [SMEM] + vmem(4), [pltpu....]
  transfers between devices with their start and end apart: 48 -> 56, of which waited for: 22 -> 13; matrix products, arithmetic and copies ran while one was open for 1% -> 3% of each run, Pallas kernels for 26% -> 29%
where the time goes in v4:
time: 170 us; the launch traced here: 169 us
  starting transfers between devices  77.3 us (45%)
  Pallas kernels  57 us (34%)
  waiting for transfers between devices  22 us (13%)
  local copies, waits for them, and re-layouts  10.6 us (6%)
    ppermute x16, starting transfers between devices, to_blocks(): return lax.ppermute(x, ('gx', 'gy', 'gz'), spread(e))  32.6 us
    ppermute x17, starting transfers between devices, to_off_chip(): return lax.ppermute(x, ('gx', 'gy', 'gz'), OFF_PAIRS)  23.9 us
    pallas_call x16, Pallas kernels, slab_body(): call(functools.partial(round_kernel, kind, r), outs, vmem(len(args)), rou...  20 us
    all_to_all x2, starting transfers between devices, exchange(): lax.all_to_all(x, ('gx', 'gy'), split_axis=0, concat_axis=0, tiled=True)  11 us
    all_to_all x2, waiting for transfers between devices, exchange(): lax.all_to_all(x, ('gx', 'gy'), split_axis=0, concat_axis=0, tiled=True)  10.2 us
    ppermute x20, starting transfers between devices, to_sibling(): return lax.ppermute(x, 'gz', SWAP)  8.47 us
    pallas_call x1, Pallas kernels, slab_body(): call(functools.partial(gather_half, True), [coef_shape, half_shape, half_...  8.2 us
    pallas_call x1, Pallas kernels, slab_body(): call(functools.partial(gather_half, False), [coef_shape], [SMEM] + vmem(2...  7.2 us
  transfers between devices with their start and end apart: 56, of which 13 were waited for; matrix products, arithmetic and copies ran while one was open for 3% of the time, Pallas kernels for 29%

profile of v4, /device:TPU:1, one launch (start us, length us, event | category | flops | bytes accessed | tf_op | source)
XLA Modules:
  0.0 169.1 jit_solution(14381679901598753569)
XLA Ops:
  2.7 1.6 shard_map.157
  8.8 7.0 %all-to-all-start = ((f32[8,168,128]{2,1,0:T(8,128)}), f32[8,168,128]{2,1,0:T(8,128)}, u32[]{:S(2)}, u32[]{:S(2)}) async-start(f32[8,168,128]{2,1,0:T(8,128)} %shard_map.159), calls=%async_computation | async-start | bytes 1376256 | tf_op jit(solution)/shard_map/all_to_all | solution.py:698
  15.8 2.7 %shard_map.161 = (f32[4,4,4,16,128]{4,3,2,1,0:T(8,128)S(1)}, f32[4,4,4,16,128]{4,3,2,1,0:T(8,128)S(1)}) custom-call(s32[8]{0:T(128)S(1)} %stack.32.scal, f32[8,64,128]{2,1,0:T(8,128)S(1)} %copy-done.7, f32[8,64,128]{2,1,0:T(8,128)S(1)} %copy-done.8, f32[8,64,128]{2,1,0:T(8,128)S(1)} %copy-done.9, f32[8,64,128]{2,1,0:T(8,128)S(1)} %copy-done.10), custom_call_target="tpu_custom_call" | custom-call | flops 1048576 | bytes 2097152 | tf_op jit(solution)/shard_map/pallas_call | solution.py:738
  19.0 1.5 collective-permute-done.2
  23.6 10.2 %all-to-all-done = f32[8,168,128]{2,1,0:T(8,128)} async-done(((f32[8,168,128]{2,1,0:T(8,128)}), f32[8,168,128]{2,1,0:T(8,128)}, u32[]{:S(2)}, u32[]{:S(2)}) %all-to-all-start) | async-done | bytes 688160 | tf_op jit(solution)/shard_map/all_to_all | solution.py:698
  33.8 4.0 %all-to-all-start.1 = ((f32[8,4,4,16,128]{4,3,2,1,0:T(8,128)}), f32[8,4,4,16,128]{4,3,2,1,0:T(8,128)S(1)}, u32[]{:S(2)}, u32[]{:S(2)}) async-start(f32[8,4,4,16,128]{4,3,2,1,0:T(8,128)} %bitcast.11), calls=%async_computation.1 | async-start | bytes 2097152 | tf_op jit(solution)/shard_map/all_to_all | solution.py:698
  44.4 7.2 %shard_map.164.refs_0_ = f32[32,32,128]{2,1,0:T(8,128)S(1)} custom-call(s32[8]{0:T(128)S(1)} %stack.32.scal, f32[8,4,32,128]{3,2,1,0:T(8,128)S(1)} %bitcast.19, s32[32,128]{1,0:T(8,128)S(1)} %get-tuple-element.125.ids_slab.ids), custom_call_target="tpu_custom_call" | custom-call | flops 16777216 | bytes 1048576 | tf_op jit(solution)/shard_map/pallas_call | solution.py:753
  51.7 8.2 %shard_map.165 = (f32[32,32,128]{2,1,0:T(8,128)S(1)}, f32[32,16,128]{2,1,0:T(8,128)}, f32[32,16,128]{2,1,0:T(8,128)}) custom-call(s32[8]{0:T(128)S(1)} %stack.32.scal, f32[8,4,32,128]{3,2,1,0:T(8,128)S(1)} %collective-permute-done.5.table, s32[32,128]{1,0:T(8,128)S(1)} %get-tuple-element.125.ids_slab.ids, f32[32,32,128]{2,1,0:T(8,128)S(1)} %shard_map.164.refs_0_), custom_call_target="tpu_custom_call" | custom-call | flops 16777216 | bytes 2097152 | tf_op jit(solution)/shard_map/pallas_call | solution.py:756
  60.6 1.6 collective-permute-start.6
  62.3 1.8 %shard_map.162.index = s32[2,40,128]{2,1,0:T(8,128)S(1)} custom-call(s32[8]{0:T(128)S(1)} %stack.32.scal, s32[32,128]{1,0:T(8,128)S(1)} %get-tuple-element.125.ids_slab.ids, s32[32,128]{1,0:T(8,128)S(1)} %get-tuple-element.126.ids_owner), custom_call_target="tpu_custom_call" | custom-call | flops 16777216 | bytes 262144 | tf_op jit(solution)/shard_map/pallas_call | solution.py:768
  74.5 1.8 %collective-permute-start.9 = (f32[1,32,8,128]{3,2,1,0:T(8,128)S(1)}, f32[1,32,8,128]{3,2,1,0:T(8,128)S(1)}, u32[]{:S(2)}, u32[]{:S(2)}) collective-permute-start(f32[1,32,8,128]{3,2,1,0:T(8,128)S(1)} %get-tuple-element.139), channel_id=1, source_target_pairs={{1,4},{4,1},{5,8},{8,5},{9,12},{12,9},{13,14},{14,13},{15,10},{10,... | collective-permute-start | bytes 393224 | tf_op jit(solution)/shard_map/ppermute | solution.py:204
  77.7 1.5 collective-permute-start.19
  86.5 1.6 collective-permute-start.13
  98.5 1.6 collective-permute-start.25
  101.5 1.5 collective-permute-start.33
  110.5 1.5 collective-permute-start.29
  114.9 1.7 %shard_map.178 = (f32[32,16,128]{2,1,0:T(8,128)S(1)}, f32[40,32,128]{2,1,0:T(8,128)}, f32[2,32,16,128]{3,2,1,0:T(8,128)S(1)}) custom-call(s32[3,8,128]{2,1,0:T(8,128)S(1)} %get-tuple-element.120.refs_0_, f32[16,32,128]{2,1,0:T(8,128)S(1)} %get-tuple-element.121.refs_1_, s32[32,128]{1,0:T(8,128)S(1)} %get-tuple-element.122.refs_2_, ...), custom_call_target="tpu_custom_call" | custom-call | flops 16777216 | bytes 4194304 | tf_op jit(solution)/shard_map/pallas_call | solution.py:807
  117.8 1.7 %shard_map.182 = (f32[32,16,128]{2,1,0:T(8,128)S(1)}, f32[40,32,128]{2,1,0:T(8,128)}, f32[2,32,16,128]{3,2,1,0:T(8,128)S(1)}) custom-call(s32[3,8,128]{2,1,0:T(8,128)S(1)} %get-tuple-element.120.refs_0_, f32[16,32,128]{2,1,0:T(8,128)S(1)} %get-tuple-element.153.refs_1_, s32[32,128]{1,0:T(8,128)S(1)} %get-tuple-element.154.refs_2_, ...), custom_call_target="tpu_custom_call" | custom-call | flops 16777216 | bytes 4194304 | tf_op jit(solution)/shard_map/pallas_call | solution.py:807
  120.4 3.5 %collective-permute-start.38 = (f32[2,4,16,128]{3,2,1,0:T(8,128)S(1)}, f32[2,4,16,128]{3,2,1,0:T(8,128)S(1)}, u32[]{:S(2)}, u32[]{:S(2)}) collective-permute-start(f32[2,4,16,128]{3,2,1,0:T(8,128)S(1)} %get-tuple-element.211), channel_id=1, source_target_pairs={{0,12},{1,14},{2,15},{3,13},{4,8},{5,10},{6,11},{7,9},{8,4},{9,6},... | collective-permute-start | bytes 196616 | tf_op jit(solution)/shard_map/ppermute | solution.py:212
  124.3 2.1 %collective-permute-start.40 = (f32[2,4,16,128]{3,2,1,0:T(8,128)S(1)}, f32[2,4,16,128]{3,2,1,0:T(8,128)S(1)}, u32[]{:S(2)}, u32[]{:S(2)}) collective-permute-start(f32[2,4,16,128]{3,2,1,0:T(8,128)S(1)} %get-tuple-element.213), channel_id=1, source_target_pairs={{0,8},{1,10},{2,11},{3,9},{4,12},{5,14},{6,15},{7,13},{8,0},{9,2},... | collective-permute-start | bytes 196616 | tf_op jit(solution)/shard_map/ppermute | solution.py:212
  129.3 5.2 %shard_map.185 = (f32[8,32,128]{2,1,0:T(8,128)S(1)}, f32[8,32,128]{2,1,0:T(8,128)S(1)}, f32[8,32,128]{2,1,0:T(8,128)S(1)}, f32[8,32,128]{2,1,0:T(8,128)S(1)}, f3...) custom-call(s32[8]{0:T(128)S(1)} %stack.32.scal, ...), custom_call_target="tpu_custom_call" | custom-call | flops 4194304 | bytes 16777216 | tf_op jit(solution)/shard_map/pallas_call | solution.py:831
  134.5 5.3 %collective-permute-start.46 = (f32[8,32,128]{2,1,0:T(8,128)S(1)}, f32[8,32,128]{2,1,0:T(8,128)S(1)}, u32[]{:S(2)}, u32[]{:S(2)}) collective-permute-start(f32[8,32,128]{2,1,0:T(8,128)S(1)} %get-tuple-element.226), channel_id=1, source_target_pairs={{0,12},{1,14},{2,15},{3,13},{4,8},{5,10},{6,11},{7,9},{8,4},{9,6},... | collective-permute-start | bytes 393224 | tf_op jit(solution)/shard_map/ppermute | solution.py:212
  139.8 1.7 collective-permute-start.47
  142.4 1.9 %collective-permute-start.44 = (f32[2,4,16,128]{3,2,1,0:T(8,128)S(1)}, f32[2,4,16,128]{3,2,1,0:T(8,128)S(1)}, u32[]{:S(2)}, u32[]{:S(2)}) collective-permute-start(f32[2,4,16,128]{3,2,1,0:T(8,128)S(1)} %get-tuple-element.217), channel_id=1, source_target_pairs={{0,0},{1,2},{2,3},{3,1},{4,4},{5,6},{6,7},{7,5},{8,8},{9,10},{10,1... | collective-permute-start | bytes 196616 | tf_op jit(solution)/shard_map/ppermute | solution.py:212
  144.3 1.9 %collective-permute-start.45 = (f32[2,4,16,128]{3,2,1,0:T(8,128)S(1)}, f32[2,4,16,128]{3,2,1,0:T(8,128)S(1)}, u32[]{:S(2)}, u32[]{:S(2)}) collective-permute-start(f32[2,4,16,128]{3,2,1,0:T(8,128)S(1)} %get-tuple-element.218), channel_id=1, source_target_pairs={{0,2},{1,0},{2,1},{3,3},{4,6},{5,4},{6,5},{7,7},{8,10},{9,8},{10,9... | collective-permute-start | bytes 196616 | tf_op jit(solution)/shard_map/ppermute | solution.py:212
  146.2 2.3 %collective-permute-done.44.refs_6_ = f32[2,4,16,128]{3,2,1,0:T(8,128)S(1)} collective-permute-done((f32[2,4,16,128]{3,2,1,0:T(8,128)S(1)}, f32[2,4,16,128]{3,2,1,0:T(8,128)S(1)}, u32[]{:S(2)}, u32[]{:S(2)}) %collective-permute-start.44) | collective-permute-done | bytes 65568 | tf_op jit(solution)/shard_map/ppermute | solution.py:212
  149.9 5.2 %collective-permute-start.50 = (f32[8,32,128]{2,1,0:T(8,128)S(1)}, f32[8,32,128]{2,1,0:T(8,128)S(1)}, u32[]{:S(2)}, u32[]{:S(2)}) collective-permute-start(f32[8,32,128]{2,1,0:T(8,128)S(1)} %get-tuple-element.230), channel_id=1, source_target_pairs={{0,4},{1,6},{2,7},{3,5},{4,0},{5,2},{6,3},{7,1},{8,12},{9,14},{10,... | collective-permute-start | bytes 393224 | tf_op jit(solution)/shard_map/ppermute | solution.py:212
  155.1 1.9 %collective-permute-start.52 = (f32[8,32,128]{2,1,0:T(8,128)S(1)}, f32[8,32,128]{2,1,0:T(8,128)S(1)}, u32[]{:S(2)}, u32[]{:S(2)}) collective-permute-start(f32[8,32,128]{2,1,0:T(8,128)S(1)} %get-tuple-element.232), channel_id=1, source_target_pairs={{0,0},{1,2},{2,3},{3,1},{4,4},{5,6},{6,7},{7,5},{8,8},{9,10},{10,1... | collective-permute-start | bytes 393224 | tf_op jit(solution)/shard_map/ppermute | solution.py:212
  158.0 3.7 %collective-permute-start.53 = (f32[8,32,128]{2,1,0:T(8,128)S(1)}, f32[8,32,128]{2,1,0:T(8,128)S(1)}, u32[]{:S(2)}, u32[]{:S(2)}) collective-permute-start(f32[8,32,128]{2,1,0:T(8,128)S(1)} %get-tuple-element.224), channel_id=1, source_target_pairs={{0,2},{1,0},{2,1},{3,3},{4,6},{5,4},{6,5},{7,7},{8,10},{9,8},{10,9... | collective-permute-start | bytes 393224 | tf_op jit(solution)/shard_map/ppermute | solution.py:212
  162.1 1.5 shard_map.184
  163.6 1.8 %collective-permute-done.51.refs_5_ = f32[8,32,128]{2,1,0:T(8,128)S(1)} collective-permute-done((f32[8,32,128]{2,1,0:T(8,128)S(1)}, f32[8,32,128]{2,1,0:T(8,128)S(1)}, u32[]{:S(2)}, u32[]{:S(2)}) %collective-permute-start.51) | collective-permute-done | bytes 131104 | tf_op jit(solution)/shard_map/ppermute | solution.py:212
  166.2 2.9 %shard_map.187 = f32[2048,128]{1,0:T(8,128)} custom-call(s32[8]{0:T(128)S(1)} %stack.32.scal, bf16[1024,1024]{1,0:T(8,128)(2,1)S(1)} %shard_map.186.picks, f32[8,32,128]{2,1,0:T(8,128)S(1)} %collective-permute-done.46.refs_0_, f32[8,32,128]{2,1,0:T(8,128)S(1)} %collective-permute-done.47.refs_1_, f32[8,32,128]{2,1,0:T(8,128)S(1)} %collective-permute-done.48.refs_2_, ...), custom_call_target="tpu_custom_call" | custom-call | flops 268435456 | bytes 4194304 | tf_op jit(solution)/shard_map/pallas_call | solution.py:850
  (151 shorter events, 68.4 us)
Async XLA Ops:
  8.8 25.0 %all-to-all-start = ((f32[8,168,128]{2,1,0:T(8,128)}), f32[8,168,128]{2,1,0:T(8,128)}, u32[]{:S(2)}, u32[]{:S(2)}) async-start(f32[8,168,128]{2,1,0:T(8,128)} %shard_map.159), calls=%async_computation | async-start | bytes 1376256 | tf_op jit(solution)/shard_map/all_to_all | solution.py:698
  33.8 31.7 %all-to-all-start.1 = ((f32[8,4,4,16,128]{4,3,2,1,0:T(8,128)}), f32[8,4,4,16,128]{4,3,2,1,0:T(8,128)S(1)}, u32[]{:S(2)}, u32[]{:S(2)}) async-start(f32[8,4,4,16,128]{4,3,2,1,0:T(8,128)} %bitcast.11), calls=%async_computation.1 | async-start | bytes 2097152 | tf_op jit(solution)/shard_map/all_to_all | solution.py:698
  38.9 12.8 %collective-permute-start.5 = (f32[8,4,32,128]{3,2,1,0:T(8,128)S(1)}, f32[8,4,32,128]{3,2,1,0:T(8,128)S(1)}, u32[]{:S(2)}, u32[]{:S(2)}) collective-permute-start(f32[8,4,32,128]{3,2,1,0:T(8,128)S(1)} %bitcast.18), channel_id=1, source_target_pairs={{0,16},{16,0},{1,17},{17,1},{2,18},{18,2},{3,19},{19,3},{4,20},{20... | collective-permute-start | bytes 1572872 | tf_op jit(solution)/shard_map/ppermute | solution.py:735
  60.6 7.9 %collective-permute-start.6 = (f32[32,16,128]{2,1,0:T(8,128)}, f32[32,16,128]{2,1,0:T(8,128)S(1)}, u32[]{:S(2)}, u32[]{:S(2)}) collective-permute-start(f32[32,16,128]{2,1,0:T(8,128)} %get-tuple-element.133), channel_id=1, source_target_pairs={{0,1},{1,0},{2,3},{3,2},{4,5},{5,4},{6,7},{7,6},{8,9},{9,8},{10,11... | collective-permute-start | bytes 786440 | tf_op jit(solution)/shard_map/ppermute | solution.py:200
  64.1 6.4 %collective-permute-start.7 = (f32[32,16,128]{2,1,0:T(8,128)}, f32[32,16,128]{2,1,0:T(8,128)}, u32[]{:S(2)}, u32[]{:S(2)}) collective-permute-start(f32[32,16,128]{2,1,0:T(8,128)} %get-tuple-element.134), channel_id=1, source_target_pairs={{1,4},{4,1},{5,8},{8,5},{9,12},{12,9},{13,14},{14,13},{15,10},{10,... | collective-permute-start | bytes 786440 | tf_op jit(solution)/shard_map/ppermute | solution.py:204
  66.4 6.1 %collective-permute-start.3 = (f32[2,32,8,128]{3,2,1,0:T(8,128)S(1)}, f32[2,32,8,128]{3,2,1,0:T(8,128)S(1)}, u32[]{:S(2)}, u32[]{:S(2)}) collective-permute-start(f32[2,32,8,128]{3,2,1,0:T(8,128)S(1)} %get-tuple-element.129), channel_id=1, source_target_pairs={{0,1},{1,0},{2,3},{3,2},{4,5},{5,4},{6,7},{7,6},{8,9},{9,8},{10,11... | collective-permute-start | bytes 786440 | tf_op jit(solution)/shard_map/ppermute | solution.py:200
  67.0 6.3 %collective-permute-start.4 = (f32[2,32,8,128]{3,2,1,0:T(8,128)S(1)}, f32[2,32,8,128]{3,2,1,0:T(8,128)S(1)}, u32[]{:S(2)}, u32[]{:S(2)}) collective-permute-start(f32[2,32,8,128]{3,2,1,0:T(8,128)S(1)} %get-tuple-element.130), channel_id=1, source_target_pairs={{1,4},{4,1},{5,8},{8,5},{9,12},{12,9},{13,14},{14,13},{15,10},{10,... | collective-permute-start | bytes 786440 | tf_op jit(solution)/shard_map/ppermute | solution.py:204
  68.1 8.3 %collective-permute-start.16 = (f32[2,32,8,128]{3,2,1,0:T(8,128)S(1)}, f32[2,32,8,128]{3,2,1,0:T(8,128)S(1)}, u32[]{:S(2)}, u32[]{:S(2)}) collective-permute-start(f32[2,32,8,128]{3,2,1,0:T(8,128)S(1)} %get-tuple-element.156), channel_id=1, source_target_pairs={{0,1},{1,0},{2,3},{3,2},{4,5},{5,4},{6,7},{7,6},{8,9},{9,8},{10,11... | collective-permute-start | bytes 786440 | tf_op jit(solution)/shard_map/ppermute | solution.py:200
  68.6 7.8 %collective-permute-start.17 = (f32[2,32,8,128]{3,2,1,0:T(8,128)S(1)}, f32[2,32,8,128]{3,2,1,0:T(8,128)S(1)}, u32[]{:S(2)}, u32[]{:S(2)}) collective-permute-start(f32[2,32,8,128]{3,2,1,0:T(8,128)S(1)} %get-tuple-element.157), channel_id=1, source_target_pairs={{1,4},{4,1},{5,8},{8,5},{9,12},{12,9},{13,14},{14,13},{15,10},{10,... | collective-permute-start | bytes 786440 | tf_op jit(solution)/shard_map/ppermute | solution.py:204
  74.4 4.7 %collective-permute-start.8 = (f32[1,32,8,128]{3,2,1,0:T(8,128)S(1)}, f32[1,32,8,128]{3,2,1,0:T(8,128)S(1)}, u32[]{:S(2)}, u32[]{:S(2)}) collective-permute-start(f32[1,32,8,128]{3,2,1,0:T(8,128)S(1)} %get-tuple-element.138), channel_id=1, source_target_pairs={{0,1},{1,0},{2,3},{3,2},{4,5},{5,4},{6,7},{7,6},{8,9},{9,8},{10,11... | collective-permute-start | bytes 393224 | tf_op jit(solution)/shard_map/ppermute | solution.py:200
  83.2 4.8 %collective-permute-start.20 = (f32[1,32,8,128]{3,2,1,0:T(8,128)S(1)}, f32[1,32,8,128]{3,2,1,0:T(8,128)S(1)}, u32[]{:S(2)}, u32[]{:S(2)}) collective-permute-start(f32[1,32,8,128]{3,2,1,0:T(8,128)S(1)} %get-tuple-element.164), channel_id=1, source_target_pairs={{0,1},{1,0},{2,3},{3,2},{4,5},{5,4},{6,7},{7,6},{8,9},{9,8},{10,11... | collective-permute-start | bytes 393224 | tf_op jit(solution)/shard_map/ppermute | solution.py:200
  86.1 4.7 %collective-permute-start.12 = (f32[1,32,8,128]{3,2,1,0:T(8,128)S(1)}, f32[1,32,8,128]{3,2,1,0:T(8,128)S(1)}, u32[]{:S(2)}, u32[]{:S(2)}) collective-permute-start(f32[1,32,8,128]{3,2,1,0:T(8,128)S(1)} %get-tuple-element.146), channel_id=1, source_target_pairs={{0,1},{1,0},{2,3},{3,2},{4,5},{5,4},{6,7},{7,6},{8,9},{9,8},{10,11... | collective-permute-start | bytes 393224 | tf_op jit(solution)/shard_map/ppermute | solution.py:200
  94.9 5.2 %collective-permute-start.30 = (f32[1,32,8,128]{3,2,1,0:T(8,128)S(1)}, f32[1,32,8,128]{3,2,1,0:T(8,128)S(1)}, u32[]{:S(2)}, u32[]{:S(2)}) collective-permute-start(f32[1,32,8,128]{3,2,1,0:T(8,128)S(1)} %get-tuple-element.189), channel_id=1, source_target_pairs={{0,1},{1,0},{2,3},{3,2},{4,5},{5,4},{6,7},{7,6},{8,9},{9,8},{10,11... | collective-permute-start | bytes 393224 | tf_op jit(solution)/shard_map/ppermute | solution.py:200
  98.2 4.8 %collective-permute-start.24 = (f32[1,32,8,128]{3,2,1,0:T(8,128)S(1)}, f32[1,32,8,128]{3,2,1,0:T(8,128)S(1)}, u32[]{:S(2)}, u32[]{:S(2)}) collective-permute-start(f32[1,32,8,128]{3,2,1,0:T(8,128)S(1)} %get-tuple-element.174), channel_id=1, source_target_pairs={{0,1},{1,0},{2,3},{3,2},{4,5},{5,4},{6,7},{7,6},{8,9},{9,8},{10,11... | collective-permute-start | bytes 393224 | tf_op jit(solution)/shard_map/ppermute | solution.py:200
  107.1 4.9 %collective-permute-start.34 = (f32[1,32,8,128]{3,2,1,0:T(8,128)S(1)}, f32[1,32,8,128]{3,2,1,0:T(8,128)S(1)}, u32[]{:S(2)}, u32[]{:S(2)}) collective-permute-start(f32[1,32,8,128]{3,2,1,0:T(8,128)S(1)} %get-tuple-element.199), channel_id=1, source_target_pairs={{0,1},{1,0},{2,3},{3,2},{4,5},{5,4},{6,7},{7,6},{8,9},{9,8},{10,11... | collective-permute-start | bytes 393224 | tf_op jit(solution)/shard_map/ppermute | solution.py:200
  110.1 4.8 %collective-permute-start.28 = (f32[1,32,8,128]{3,2,1,0:T(8,128)S(1)}, f32[1,32,8,128]{3,2,1,0:T(8,128)S(1)}, u32[]{:S(2)}, u32[]{:S(2)}) collective-permute-start(f32[1,32,8,128]{3,2,1,0:T(8,128)S(1)} %get-tuple-element.184), channel_id=1, source_target_pairs={{0,1},{1,0},{2,3},{3,2},{4,5},{5,4},{6,7},{7,6},{8,9},{9,8},{10,11... | collective-permute-start | bytes 393224 | tf_op jit(solution)/shard_map/ppermute | solution.py:200
  120.4 8.6 %collective-permute-start.38 = (f32[2,4,16,128]{3,2,1,0:T(8,128)S(1)}, f32[2,4,16,128]{3,2,1,0:T(8,128)S(1)}, u32[]{:S(2)}, u32[]{:S(2)}) collective-permute-start(f32[2,4,16,128]{3,2,1,0:T(8,128)S(1)} %get-tuple-element.211), channel_id=1, source_target_pairs={{0,12},{1,14},{2,15},{3,13},{4,8},{5,10},{6,11},{7,9},{8,4},{9,6},... | collective-permute-start | bytes 196616 | tf_op jit(solution)/shard_map/ppermute | solution.py:212
  123.9 10.6 %collective-permute-start.39 = (f32[2,4,16,128]{3,2,1,0:T(8,128)S(1)}, f32[2,4,16,128]{3,2,1,0:T(8,128)S(1)}, u32[]{:S(2)}, u32[]{:S(2)}) collective-permute-start(f32[2,4,16,128]{3,2,1,0:T(8,128)S(1)} %get-tuple-element.212), channel_id=1, source_target_pairs={{0,14},{1,12},{2,13},{3,15},{4,10},{5,8},{6,9},{7,11},{8,6},{9,4},... | collective-permute-start | bytes 196616 | tf_op jit(solution)/shard_map/ppermute | solution.py:212
  124.3 15.6 %collective-permute-start.40 = (f32[2,4,16,128]{3,2,1,0:T(8,128)S(1)}, f32[2,4,16,128]{3,2,1,0:T(8,128)S(1)}, u32[]{:S(2)}, u32[]{:S(2)}) collective-permute-start(f32[2,4,16,128]{3,2,1,0:T(8,128)S(1)} %get-tuple-element.213), channel_id=1, source_target_pairs={{0,8},{1,10},{2,11},{3,9},{4,12},{5,14},{6,15},{7,13},{8,0},{9,2},... | collective-permute-start | bytes 196616 | tf_op jit(solution)/shard_map/ppermute | solution.py:212
  126.3 15.2 %collective-permute-start.41 = (f32[2,4,16,128]{3,2,1,0:T(8,128)S(1)}, f32[2,4,16,128]{3,2,1,0:T(8,128)S(1)}, u32[]{:S(2)}, u32[]{:S(2)}) collective-permute-start(f32[2,4,16,128]{3,2,1,0:T(8,128)S(1)} %get-tuple-element.214), channel_id=1, source_target_pairs={{0,10},{1,8},{2,9},{3,11},{4,14},{5,12},{6,13},{7,15},{8,2},{9,0},... | collective-permute-start | bytes 196616 | tf_op jit(solution)/shard_map/ppermute | solution.py:212
  127.8 14.6 %collective-permute-start.42 = (f32[2,4,16,128]{3,2,1,0:T(8,128)S(1)}, f32[2,4,16,128]{3,2,1,0:T(8,128)S(1)}, u32[]{:S(2)}, u32[]{:S(2)}) collective-permute-start(f32[2,4,16,128]{3,2,1,0:T(8,128)S(1)} %get-tuple-element.215), channel_id=1, source_target_pairs={{0,4},{1,6},{2,7},{3,5},{4,0},{5,2},{6,3},{7,1},{8,12},{9,14},{10,... | collective-permute-start | bytes 196616 | tf_op jit(solution)/shard_map/ppermute | solution.py:212
  129.0 15.3 %collective-permute-start.43 = (f32[2,4,16,128]{3,2,1,0:T(8,128)S(1)}, f32[2,4,16,128]{3,2,1,0:T(8,128)S(1)}, u32[]{:S(2)}, u32[]{:S(2)}) collective-permute-start(f32[2,4,16,128]{3,2,1,0:T(8,128)S(1)} %get-tuple-element.216), channel_id=1, source_target_pairs={{0,6},{1,4},{2,5},{3,7},{4,2},{5,0},{6,1},{7,3},{8,14},{9,12},{10,... | collective-permute-start | bytes 196616 | tf_op jit(solution)/shard_map/ppermute | solution.py:212
  134.5 20.6 %collective-permute-start.46 = (f32[8,32,128]{2,1,0:T(8,128)S(1)}, f32[8,32,128]{2,1,0:T(8,128)S(1)}, u32[]{:S(2)}, u32[]{:S(2)}) collective-permute-start(f32[8,32,128]{2,1,0:T(8,128)S(1)} %get-tuple-element.226), channel_id=1, source_target_pairs={{0,12},{1,14},{2,15},{3,13},{4,8},{5,10},{6,11},{7,9},{8,4},{9,6},... | collective-permute-start | bytes 393224 | tf_op jit(solution)/shard_map/ppermute | solution.py:212
  139.8 15.2 %collective-permute-start.47 = (f32[8,32,128]{2,1,0:T(8,128)S(1)}, f32[8,32,128]{2,1,0:T(8,128)S(1)}, u32[]{:S(2)}, u32[]{:S(2)}) collective-permute-start(f32[8,32,128]{2,1,0:T(8,128)S(1)} %get-tuple-element.227), channel_id=1, source_target_pairs={{0,14},{1,12},{2,13},{3,15},{4,10},{5,8},{6,9},{7,11},{8,6},{9,4},... | collective-permute-start | bytes 393224 | tf_op jit(solution)/shard_map/ppermute | solution.py:212
  141.5 16.5 %collective-permute-start.48 = (f32[8,32,128]{2,1,0:T(8,128)S(1)}, f32[8,32,128]{2,1,0:T(8,128)S(1)}, u32[]{:S(2)}, u32[]{:S(2)}) collective-permute-start(f32[8,32,128]{2,1,0:T(8,128)S(1)} %get-tuple-element.228), channel_id=1, source_target_pairs={{0,8},{1,10},{2,11},{3,9},{4,12},{5,14},{6,15},{7,13},{8,0},{9,2},... | collective-permute-start | bytes 393224 | tf_op jit(solution)/shard_map/ppermute | solution.py:212
  142.4 6.1 %collective-permute-start.44 = (f32[2,4,16,128]{3,2,1,0:T(8,128)S(1)}, f32[2,4,16,128]{3,2,1,0:T(8,128)S(1)}, u32[]{:S(2)}, u32[]{:S(2)}) collective-permute-start(f32[2,4,16,128]{3,2,1,0:T(8,128)S(1)} %get-tuple-element.217), channel_id=1, source_target_pairs={{0,0},{1,2},{2,3},{3,1},{4,4},{5,6},{6,7},{7,5},{8,8},{9,10},{10,1... | collective-permute-start | bytes 196616 | tf_op jit(solution)/shard_map/ppermute | solution.py:212
  144.3 5.6 %collective-permute-start.45 = (f32[2,4,16,128]{3,2,1,0:T(8,128)S(1)}, f32[2,4,16,128]{3,2,1,0:T(8,128)S(1)}, u32[]{:S(2)}, u32[]{:S(2)}) collective-permute-start(f32[2,4,16,128]{3,2,1,0:T(8,128)S(1)} %get-tuple-element.218), channel_id=1, source_target_pairs={{0,2},{1,0},{2,1},{3,3},{4,6},{5,4},{6,5},{7,7},{8,10},{9,8},{10,9... | collective-permute-start | bytes 196616 | tf_op jit(solution)/shard_map/ppermute | solution.py:212
  148.5 15.1 %collective-permute-start.49 = (f32[8,32,128]{2,1,0:T(8,128)S(1)}, f32[8,32,128]{2,1,0:T(8,128)S(1)}, u32[]{:S(2)}, u32[]{:S(2)}) collective-permute-start(f32[8,32,128]{2,1,0:T(8,128)S(1)} %get-tuple-element.229), channel_id=1, source_target_pairs={{0,10},{1,8},{2,9},{3,11},{4,14},{5,12},{6,13},{7,15},{8,2},{9,0},... | collective-permute-start | bytes 393224 | tf_op jit(solution)/shard_map/ppermute | solution.py:212
  149.9 13.7 %collective-permute-start.50 = (f32[8,32,128]{2,1,0:T(8,128)S(1)}, f32[8,32,128]{2,1,0:T(8,128)S(1)}, u32[]{:S(2)}, u32[]{:S(2)}) collective-permute-start(f32[8,32,128]{2,1,0:T(8,128)S(1)} %get-tuple-element.230), channel_id=1, source_target_pairs={{0,4},{1,6},{2,7},{3,5},{4,0},{5,2},{6,3},{7,1},{8,12},{9,14},{10,... | collective-permute-start | bytes 393224 | tf_op jit(solution)/shard_map/ppermute | solution.py:212
  155.1 10.3 %collective-permute-start.51 = (f32[8,32,128]{2,1,0:T(8,128)S(1)}, f32[8,32,128]{2,1,0:T(8,128)S(1)}, u32[]{:S(2)}, u32[]{:S(2)}) collective-permute-start(f32[8,32,128]{2,1,0:T(8,128)S(1)} %get-tuple-element.231), channel_id=1, source_target_pairs={{0,6},{1,4},{2,5},{3,7},{4,2},{5,0},{6,1},{7,3},{8,14},{9,12},{10,... | collective-permute-start | bytes 393224 | tf_op jit(solution)/shard_map/ppermute | solution.py:212
  155.1 10.3 %collective-permute-start.52 = (f32[8,32,128]{2,1,0:T(8,128)S(1)}, f32[8,32,128]{2,1,0:T(8,128)S(1)}, u32[]{:S(2)}, u32[]{:S(2)}) collective-permute-start(f32[8,32,128]{2,1,0:T(8,128)S(1)} %get-tuple-element.232), channel_id=1, source_target_pairs={{0,0},{1,2},{2,3},{3,1},{4,4},{5,6},{6,7},{7,5},{8,8},{9,10},{10,1... | collective-permute-start | bytes 393224 | tf_op jit(solution)/shard_map/ppermute | solution.py:212
  158.0 8.2 %collective-permute-start.53 = (f32[8,32,128]{2,1,0:T(8,128)S(1)}, f32[8,32,128]{2,1,0:T(8,128)S(1)}, u32[]{:S(2)}, u32[]{:S(2)}) collective-permute-start(f32[8,32,128]{2,1,0:T(8,128)S(1)} %get-tuple-element.224), channel_id=1, source_target_pairs={{0,2},{1,0},{2,1},{3,3},{4,6},{5,4},{6,5},{7,7},{8,10},{9,8},{10,9... | collective-permute-start | bytes 393224 | tf_op jit(solution)/shard_map/ppermute | solution.py:212
  (40 other events, 279.6 us)

commit v5 on v4

--- a/solution.py
+++ b/solution.py
@@ -274,6 +274,10 @@
     return pltpu.roll(x, BY, x.ndim - 1)
 
 
+def roll_tile(x):
+    return pltpu.roll(x, HALO // 2, 0)
+
+
 def place(scal, chunk):
     chip, core = divmod(chunk, 2)
     mine = core == scal[H]
@@ -296,9 +300,10 @@
 
 
 def pack_table(scal, table, keep, give):
+    first = scal[SHOT] * 1024
     for q in range(4):
         for comp in range(2):
-            turned = table[pl.ds(q * 256 + comp, 128, stride=2), :].T
+            turned = table[pl.ds(first + q * 256 + comp, 128, stride=2), :].T
             at = q * 32 + comp * ZS
             for chunk in range(8):
                 mine, g = place(scal, chunk)
@@ -437,8 +442,15 @@
                     x = ix * BX + 2 * i
                     own[x] = jnp.where(low, a, roll_half(b))
                     own[x + 1] = jnp.where(low, roll_half(a), b)
-            sib[step] = own[:, pl.ds(HALO * (1 - h), HALO), :]
-            off[step] = own[:, pl.ds(HALO * h, HALO), :]
+        sib[0:NXA] = now[:, pl.ds(HALO * (1 - h), HALO), :]
+        off[0:NXA] = now[:, pl.ds(HALO * h, HALO), :]
+        upper = lax.broadcasted_iota(jnp.int32, (HALO, 128), 0) < HALO // 2
+        for x in range(NXA // 2):
+            one, two = prev[x], prev[x + NXA // 2]
+            start = jnp.where(upper, one[:HALO], roll_tile(two[:HALO]))
+            end = jnp.where(upper, roll_tile(one[HALO:]), two[HALO:])
+            sib[NXA + x] = jnp.where(h == 0, end, start)
+            off[NXA + x] = jnp.where(h == 0, start, end)
 
 
 def index_kernel(scal, ids_slab, ids_owner, out):
@@ -534,19 +546,23 @@
         e[0:PADX] = zero
         e[PADX + NXA :] = zero
 
-    def extend(e, own, n):
+    def extend(e, own, shared):
         for x in range(NXA):
-            near, far = sib[n, x], jnp.where(inside, off[n, x], 0.0)
-            e[PADX + x, 0:HALO] = jnp.where(core_0, far, near)
+            at = NXA + x % (NXA // 2) if shared else x
+            near, far = sib[at], jnp.where(inside, off[at], 0.0)
+            low, high = jnp.where(core_0, far, near), jnp.where(core_0, near, far)
+            if shared and x < NXA // 2:
+                low = roll_tile(low)
+            elif shared:
+                high = roll_tile(high)
+            e[PADX + x, 0:HALO] = low
             e[PADX + x, OWN] = own[x]
-            e[PADX + x, HALO + ZS :] = jnp.where(core_0, near, far)
-
+            e[PADX + x, HALO + ZS :] = high
+
+    extend(e0, own, False)
     if first:
-        extend(e0, own, 1)
-        extend(e1, prev, 0)
+        extend(e1, prev, True)
         prev = e1
-    else:
-        extend(e0, own, 0)
     base = jnp.concatenate([place[2]] * (ZE // 8), axis=0) + lax.broadcasted_iota(jnp.int32, (ZE, 128), 0)
 
     def bands(step, g):
@@ -583,8 +599,8 @@
                 out_own[x] = following
                 if not last:
                     low, high = following[:HALO], following[HALO:]
-                    out_sib[0, x] = jnp.where(core_0, high, low)
-                    out_off[0, x] = jnp.where(core_0, low, high)
+                    out_sib[x] = jnp.where(core_0, high, low)
+                    out_off[x] = jnp.where(core_0, low, high)
             else:
                 e1[at] = following
                 hor, ver = hor[OWN], ver[OWN]
@@ -670,7 +686,7 @@
 
 
 def finish_model(scal, picks, *refs):
-    gots, (model, columns) = refs[:8], refs[8:]
+    gots, (out, columns, model, sems) = refs[:8], refs[8:]
     for n, e in enumerate(FAR_FIRST):
         for comp in range(2):
             rows = pl.ds(pl.multiple_of(comp * 128 + slab_of(scal, e), ZS), ZS)
@@ -680,11 +696,17 @@
     high = values.astype(BF16)
     rest = (values - high.astype(F32)).astype(BF16)
     both = jnp.concatenate([high, rest], axis=1)
+    copies = []
     for block in range(4):
         sums = jnp.dot(picks[block * 256 : (block + 1) * 256, :], both, preferred_element_type=F32)
         sums = sums[:, :256] + sums[:, 256:]
         for comp in range(2):
             model[pl.ds(block * 512 + comp, 256, stride=2), :] = sums[:, comp * 128 : (comp + 1) * 128]
+        rows = pl.ds(block * 512, 512)
+        copies.append(pltpu.make_async_copy(model.at[rows], out.at[rows], sems.at[block]))
+        copies[-1].start()
+    for copy in copies:
+        copy.wait()
 
 
 def by_half(h, mine, other):
@@ -725,7 +747,7 @@
     )
     keep, give = call(
         pack_table, [((GX, 128, 128), F32)] * 2, [SMEM] + vmem(1), moved=2 * MIB, flops=1 << 20
-    )(scal, lax.dynamic_slice_in_dim(model_table.reshape(2048, 128), lax.axis_index("shots") * 1024, 1024, axis=0))
+    )(scal, model_table.reshape(2048, 128))
     (sent,) = call(assemble, [((GX * GY, 168, 128), F32)], [SMEM] + vmem(3), moved=2 * MIB, flops=1 << 20)(
         scal, keep, to_sibling(give), small
     )
@@ -774,7 +796,7 @@
     )(scal, ids_slab, ids_owner)
 
     fields, index = lax.optimization_barrier((fields, index))
-    first_halo = ((2, NXA, HALO, 128), F32)
+    first_halo = ((NXA + NXA // 2, HALO, 128), F32)
     unpacked = call(
         unpack_fields,
         [own_shape, own_shape, first_halo, first_halo] * 2,
@@ -783,7 +805,7 @@
         flops=1 << 20,
     )(scal, fields)
     bands = matrices()
-    halo = ((1, NXA, HALO, 128), F32)
+    halo = ((NXA, HALO, 128), F32)
     state = {}
     for n, kind in enumerate("ua"):
         prev, now, sib, off = unpacked[4 * n : 4 * n + 4]
@@ -847,13 +869,18 @@
         moved=MIB,
         flops=1 << 20,
     )(scal, *final)
-    (model,) = call(
+    model = pl.pallas_call(
         finish_model,
-        [((2048, 128), F32)],
-        [SMEM] + vmem(9),
-        [pltpu.VMEM((256, 1024), F32)],
-        moved=4 * MIB,
-        flops=1 << 28,
+        out_shape=jax.ShapeDtypeStruct((2048, 128), F32),
+        in_specs=[SMEM] + vmem(9),
+        out_specs=pl.BlockSpec(memory_space=pl.ANY),
+        scratch_shapes=[
+            pltpu.VMEM((256, 1024), F32),
+            pltpu.VMEM((2048, 128), F32),
+            pltpu.SemaphoreType.DMA((4,)),
+        ],
+        compiler_params=pltpu.CompilerParams(vmem_limit_bytes=24 * MIB),
+        cost_estimate=pl.CostEstimate(flops=1 << 28, bytes_accessed=4 * MIB, transcendentals=0),
     )(scal, picks, *columns)
     return (u, a, model.reshape(1, 1024, 2, 128))
 

time: 170 us -> 166 us (0.976)
  waiting for transfers between devices: 22 us -> 36.9 us
  starting transfers between devices: 77.3 us -> 63.8 us
  local copies, waits for them, and re-layouts: 10.6 us -> 5.19 us
    ppermute x17, starting transfers between devices: 23.9 us -> 8.25 us  [to_off_chip(): return lax.ppermute(x, ('gx', 'gy', 'gz'), OFF_PAIRS)]
    ppermute x17, waiting for transfers between devices: 3.06 us -> 16.1 us  [to_off_chip(): return lax.ppermute(x, ('gx', 'gy', 'gz'), OFF_PAIRS)]
    unnamed x32 -> x26, local copies, waits for them, and re-layouts: 5.91 us -> 3.32 us
    ppermute x20, starting transfers between devices: 8.47 us -> 11 us  [to_sibling(): return lax.ppermute(x, 'gz', SWAP)]
    pallas_call x16, Pallas kernels: 20 us -> 22.2 us  [slab_body(): call(functools.partial(round_kernel, kind, r), outs, vmem(len(args)), rou...]
  transfers between devices with their start and end apart: 56 -> 56, of which waited for: 13 -> 23; matrix products, arithmetic and copies ran while one was open for 3% -> 1% of each run, Pallas kernels for 29% -> 30%
where the time goes in v5:
time: 166 us
  starting transfers between devices  63.8 us (38%)
  Pallas kernels  58.6 us (35%)
  waiting for transfers between devices  36.9 us (22%)
  local copies, waits for them, and re-layouts  5.19 us (3%)
    ppermute x16, starting transfers between devices, to_blocks(): return lax.ppermute(x, ('gx', 'gy', 'gz'), spread(e))  32.2 us
    pallas_call x16, Pallas kernels, slab_body(): call(functools.partial(round_kernel, kind, r), outs, vmem(len(args)), rou...  22.2 us
    ppermute x17, waiting for transfers between devices, to_off_chip(): return lax.ppermute(x, ('gx', 'gy', 'gz'), OFF_PAIRS)  16.1 us
    all_to_all x2, waiting for transfers between devices, exchange(): lax.all_to_all(x, ('gx', 'gy'), split_axis=0, concat_axis=0, tiled=True)  11.9 us
    ppermute x20, starting transfers between devices, to_sibling(): return lax.ppermute(x, 'gz', SWAP)  11 us
    all_to_all x2, starting transfers between devices, exchange(): lax.all_to_all(x, ('gx', 'gy'), split_axis=0, concat_axis=0, tiled=True)  11 us
    ppermute x17, starting transfers between devices, to_off_chip(): return lax.ppermute(x, ('gx', 'gy', 'gz'), OFF_PAIRS)  8.25 us
    pallas_call x1, Pallas kernels, slab_body(): call(functools.partial(gather_half, True), [coef_shape, half_shape, half_...  8.11 us
  transfers between devices with their start and end apart: 56, of which 23 were waited for; matrix products, arithmetic and copies ran while one was open for 1% of the time, Pallas kernels for 30%

profile of v5, /device:TPU:1, one launch (start us, length us, event | category | flops | bytes accessed | tf_op | source)
XLA Modules:
  0.0 165.9 jit_solution(9135215116521074264)
XLA Ops:
  2.7 1.6 shard_map.157
  6.6 1.4 shard_map.159
  8.0 7.0 %all-to-all-start = ((f32[8,168,128]{2,1,0:T(8,128)}), f32[8,168,128]{2,1,0:T(8,128)S(1)}, u32[]{:S(2)}, u32[]{:S(2)}) async-start(f32[8,168,128]{2,1,0:T(8,128)} %shard_map.159), calls=%async_computation | async-start | bytes 1376256 | tf_op jit(solution)/shard_map/all_to_all | solution.py:720
  15.0 2.7 %shard_map.161 = (f32[4,4,4,16,128]{4,3,2,1,0:T(8,128)S(1)}, f32[4,4,4,16,128]{4,3,2,1,0:T(8,128)S(1)}) custom-call(s32[8]{0:T(128)S(1)} %stack.32.scal, f32[8,64,128]{2,1,0:T(8,128)S(1)} %copy-done.5, f32[8,64,128]{2,1,0:T(8,128)S(1)} %copy-done.6, f32[8,64,128]{2,1,0:T(8,128)S(1)} %copy-done.7, f32[8,64,128]{2,1,0:T(8,128)S(1)} %copy-done.8), custom_call_target="tpu_custom_call" | custom-call | flops 1048576 | bytes 2097152 | tf_op jit(solution)/shard_map/pallas_call | solution.py:760
  18.2 1.5 collective-permute-done.2
  21.0 11.9 %all-to-all-done = f32[8,168,128]{2,1,0:T(8,128)S(1)} async-done(((f32[8,168,128]{2,1,0:T(8,128)}), f32[8,168,128]{2,1,0:T(8,128)S(1)}, u32[]{:S(2)}, u32[]{:S(2)}) %all-to-all-start) | async-done | bytes 688160 | tf_op jit(solution)/shard_map/all_to_all | solution.py:720
  32.9 4.0 %all-to-all-start.1 = ((f32[8,4,4,16,128]{4,3,2,1,0:T(8,128)}), f32[8,4,4,16,128]{4,3,2,1,0:T(8,128)S(1)}, u32[]{:S(2)}, u32[]{:S(2)}) async-start(f32[8,4,4,16,128]{4,3,2,1,0:T(8,128)} %bitcast.11), calls=%async_computation.1 | async-start | bytes 2097152 | tf_op jit(solution)/shard_map/all_to_all | solution.py:720
  41.6 7.2 %shard_map.164.refs_0_ = f32[32,32,128]{2,1,0:T(8,128)S(1)} custom-call(s32[8]{0:T(128)S(1)} %stack.32.scal, f32[8,4,32,128]{3,2,1,0:T(8,128)S(1)} %bitcast.18, s32[32,128]{1,0:T(8,128)S(1)} %get-tuple-element.125.ids_slab.ids), custom_call_target="tpu_custom_call" | custom-call | flops 16777216 | bytes 1048576 | tf_op jit(solution)/shard_map/pallas_call | solution.py:775
  49.7 8.1 %shard_map.165 = (f32[32,32,128]{2,1,0:T(8,128)S(1)}, f32[32,16,128]{2,1,0:T(8,128)}, f32[32,16,128]{2,1,0:T(8,128)S(1)}) custom-call(s32[8]{0:T(128)S(1)} %stack.32.scal, f32[8,4,32,128]{3,2,1,0:T(8,128)S(1)} %collective-permute-done.5.table, s32[32,128]{1,0:T(8,128)S(1)} %get-tuple-element.125.ids_slab.ids, f32[32,32,128]{2,1,0:T(8,128)S(1)} %shard_map.164.refs_0_), custom_call_target="tpu_custom_call" | custom-call | flops 16777216 | bytes 2097152 | tf_op jit(solution)/shard_map/pallas_call | solution.py:778
  57.8 1.6 collective-permute-start.6
  60.8 1.8 %shard_map.162.index = s32[2,40,128]{2,1,0:T(8,128)S(1)} custom-call(s32[8]{0:T(128)S(1)} %stack.32.scal, s32[32,128]{1,0:T(8,128)S(1)} %get-tuple-element.125.ids_slab.ids, s32[32,128]{1,0:T(8,128)S(1)} %get-tuple-element.126.ids_owner), custom_call_target="tpu_custom_call" | custom-call | flops 16777216 | bytes 262144 | tf_op jit(solution)/shard_map/pallas_call | solution.py:790
  67.4 2.6 %collective-permute-done.4.refs_5_ = f32[48,8,128]{2,1,0:T(8,128)S(1)} collective-permute-done((f32[48,8,128]{2,1,0:T(8,128)S(1)}, f32[48,8,128]{2,1,0:T(8,128)S(1)}, u32[]{:S(2)}, u32[]{:S(2)}) %collective-permute-start.4) | collective-permute-done | bytes 196640 | tf_op jit(solution)/shard_map/ppermute | solution.py:204
  94.0 1.6 shard_map.175
  100.1 1.4 shard_map.176
  103.2 1.4 shard_map.180
  106.4 1.4 shard_map.177
  112.4 1.8 %shard_map.178 = (f32[32,16,128]{2,1,0:T(8,128)S(1)}, f32[40,32,128]{2,1,0:T(8,128)}, f32[2,32,16,128]{3,2,1,0:T(8,128)S(1)}) custom-call(s32[3,8,128]{2,1,0:T(8,128)S(1)} %get-tuple-element.120.refs_0_, f32[16,32,128]{2,1,0:T(8,128)S(1)} %get-tuple-element.121.refs_1_, s32[32,128]{1,0:T(8,128)S(1)} %get-tuple-element.122.refs_2_, ...), custom_call_target="tpu_custom_call" | custom-call | flops 16777216 | bytes 4194304 | tf_op jit(solution)/shard_map/pallas_call | solution.py:829
  115.4 1.8 %shard_map.182 = (f32[32,16,128]{2,1,0:T(8,128)S(1)}, f32[40,32,128]{2,1,0:T(8,128)}, f32[2,32,16,128]{3,2,1,0:T(8,128)S(1)}) custom-call(s32[3,8,128]{2,1,0:T(8,128)S(1)} %get-tuple-element.120.refs_0_, f32[16,32,128]{2,1,0:T(8,128)S(1)} %get-tuple-element.153.refs_1_, s32[32,128]{1,0:T(8,128)S(1)} %get-tuple-element.154.refs_2_, ...), custom_call_target="tpu_custom_call" | custom-call | flops 16777216 | bytes 4194304 | tf_op jit(solution)/shard_map/pallas_call | solution.py:829
  118.2 3.4 %collective-permute-start.38 = (f32[2,4,16,128]{3,2,1,0:T(8,128)S(1)}, f32[2,4,16,128]{3,2,1,0:T(8,128)S(1)}, u32[]{:S(2)}, u32[]{:S(2)}) collective-permute-start(f32[2,4,16,128]{3,2,1,0:T(8,128)S(1)} %get-tuple-element.211), channel_id=1, source_target_pairs={{0,12},{1,14},{2,15},{3,13},{4,8},{5,10},{6,11},{7,9},{8,4},{9,6},... | collective-permute-start | bytes 196616 | tf_op jit(solution)/shard_map/ppermute | solution.py:212
  123.0 2.1 %collective-permute-start.41 = (f32[2,4,16,128]{3,2,1,0:T(8,128)S(1)}, f32[2,4,16,128]{3,2,1,0:T(8,128)S(1)}, u32[]{:S(2)}, u32[]{:S(2)}) collective-permute-start(f32[2,4,16,128]{3,2,1,0:T(8,128)S(1)} %get-tuple-element.214), channel_id=1, source_target_pairs={{0,10},{1,8},{2,9},{3,11},{4,14},{5,12},{6,13},{7,15},{8,2},{9,0},... | collective-permute-start | bytes 196616 | tf_op jit(solution)/shard_map/ppermute | solution.py:212
  125.1 1.5 collective-permute-start.42
  127.1 5.2 %shard_map.185 = (f32[8,32,128]{2,1,0:T(8,128)S(1)}, f32[8,32,128]{2,1,0:T(8,128)S(1)}, f32[8,32,128]{2,1,0:T(8,128)S(1)}, f32[8,32,128]{2,1,0:T(8,128)S(1)}, f3...) custom-call(s32[8]{0:T(128)S(1)} %stack.32.scal, ...), custom_call_target="tpu_custom_call" | custom-call | flops 4194304 | bytes 16777216 | tf_op jit(solution)/shard_map/pallas_call | solution.py:853
  132.3 5.2 %collective-permute-start.46 = (f32[8,32,128]{2,1,0:T(8,128)S(1)}, f32[8,32,128]{2,1,0:T(8,128)S(1)}, u32[]{:S(2)}, u32[]{:S(2)}) collective-permute-start(f32[8,32,128]{2,1,0:T(8,128)S(1)} %get-tuple-element.226), channel_id=1, source_target_pairs={{0,12},{1,14},{2,15},{3,13},{4,8},{5,10},{6,11},{7,9},{8,4},{9,6},... | collective-permute-start | bytes 393224 | tf_op jit(solution)/shard_map/ppermute | solution.py:212
  137.8 3.6 %collective-permute-start.44 = (f32[2,4,16,128]{3,2,1,0:T(8,128)S(1)}, f32[2,4,16,128]{3,2,1,0:T(8,128)S(1)}, u32[]{:S(2)}, u32[]{:S(2)}) collective-permute-start(f32[2,4,16,128]{3,2,1,0:T(8,128)S(1)} %get-tuple-element.217), channel_id=1, source_target_pairs={{0,0},{1,2},{2,3},{3,1},{4,4},{5,6},{6,7},{7,5},{8,8},{9,10},{10,1... | collective-permute-start | bytes 196616 | tf_op jit(solution)/shard_map/ppermute | solution.py:212
  141.4 1.9 %collective-permute-start.45 = (f32[2,4,16,128]{3,2,1,0:T(8,128)S(1)}, f32[2,4,16,128]{3,2,1,0:T(8,128)S(1)}, u32[]{:S(2)}, u32[]{:S(2)}) collective-permute-start(f32[2,4,16,128]{3,2,1,0:T(8,128)S(1)} %get-tuple-element.218), channel_id=1, source_target_pairs={{0,2},{1,0},{2,1},{3,3},{4,6},{5,4},{6,5},{7,7},{8,10},{9,8},{10,9... | collective-permute-start | bytes 196616 | tf_op jit(solution)/shard_map/ppermute | solution.py:212
  143.4 2.5 %collective-permute-start.49 = (f32[8,32,128]{2,1,0:T(8,128)S(1)}, f32[8,32,128]{2,1,0:T(8,128)S(1)}, u32[]{:S(2)}, u32[]{:S(2)}) collective-permute-start(f32[8,32,128]{2,1,0:T(8,128)S(1)} %get-tuple-element.229), channel_id=1, source_target_pairs={{0,10},{1,8},{2,9},{3,11},{4,14},{5,12},{6,13},{7,15},{8,2},{9,0},... | collective-permute-start | bytes 393224 | tf_op jit(solution)/shard_map/ppermute | solution.py:212
  147.0 2.8 %collective-permute-start.50 = (f32[8,32,128]{2,1,0:T(8,128)S(1)}, f32[8,32,128]{2,1,0:T(8,128)S(1)}, u32[]{:S(2)}, u32[]{:S(2)}) collective-permute-start(f32[8,32,128]{2,1,0:T(8,128)S(1)} %get-tuple-element.230), channel_id=1, source_target_pairs={{0,4},{1,6},{2,7},{3,5},{4,0},{5,2},{6,3},{7,1},{8,12},{9,14},{10,... | collective-permute-start | bytes 393224 | tf_op jit(solution)/shard_map/ppermute | solution.py:212
  150.1 3.9 %collective-permute-start.52 = (f32[8,32,128]{2,1,0:T(8,128)S(1)}, f32[8,32,128]{2,1,0:T(8,128)S(1)}, u32[]{:S(2)}, u32[]{:S(2)}) collective-permute-start(f32[8,32,128]{2,1,0:T(8,128)S(1)} %get-tuple-element.232), channel_id=1, source_target_pairs={{0,0},{1,2},{2,3},{3,1},{4,4},{5,6},{6,7},{7,5},{8,8},{9,10},{10,1... | collective-permute-start | bytes 393224 | tf_op jit(solution)/shard_map/ppermute | solution.py:212
  154.1 2.2 %collective-permute-done.48.refs_2_ = f32[8,32,128]{2,1,0:T(8,128)S(1)} collective-permute-done((f32[8,32,128]{2,1,0:T(8,128)S(1)}, f32[8,32,128]{2,1,0:T(8,128)S(1)}, u32[]{:S(2)}, u32[]{:S(2)}) %collective-permute-start.48) | collective-permute-done | bytes 131104 | tf_op jit(solution)/shard_map/ppermute | solution.py:212
  156.3 2.7 %collective-permute-start.53 = (f32[8,32,128]{2,1,0:T(8,128)S(1)}, f32[8,32,128]{2,1,0:T(8,128)S(1)}, u32[]{:S(2)}, u32[]{:S(2)}) collective-permute-start(f32[8,32,128]{2,1,0:T(8,128)S(1)} %get-tuple-element.224), channel_id=1, source_target_pairs={{0,2},{1,0},{2,1},{3,3},{4,6},{5,4},{6,5},{7,7},{8,10},{9,8},{10,9... | collective-permute-start | bytes 393224 | tf_op jit(solution)/shard_map/ppermute | solution.py:212
  159.4 1.5 shard_map.184
  162.9 2.8 %shard_map.187 = f32[2048,128]{1,0:T(8,128)} custom-call(s32[8]{0:T(128)S(1)} %stack.32.scal, bf16[1024,1024]{1,0:T(8,128)(2,1)S(1)} %shard_map.186.picks, f32[8,32,128]{2,1,0:T(8,128)S(1)} %collective-permute-done.46.refs_0_, f32[8,32,128]{2,1,0:T(8,128)S(1)} %collective-permute-done.47.refs_1_, f32[8,32,128]{2,1,0:T(8,128)S(1)} %collective-permute-done.48.refs_2_, ...), custom_call_target="tpu_custom_call" | custom-call | flops 268435456 | bytes 4194304 | tf_op jit(solution)/shard_map/pallas_call | solution.py:872
  (144 shorter events, 62.4 us)
Async XLA Ops:
  8.0 24.8 %all-to-all-start = ((f32[8,168,128]{2,1,0:T(8,128)}), f32[8,168,128]{2,1,0:T(8,128)S(1)}, u32[]{:S(2)}, u32[]{:S(2)}) async-start(f32[8,168,128]{2,1,0:T(8,128)} %shard_map.159), calls=%async_computation | async-start | bytes 1376256 | tf_op jit(solution)/shard_map/all_to_all | solution.py:720
  32.9 29.8 %all-to-all-start.1 = ((f32[8,4,4,16,128]{4,3,2,1,0:T(8,128)}), f32[8,4,4,16,128]{4,3,2,1,0:T(8,128)S(1)}, u32[]{:S(2)}, u32[]{:S(2)}) async-start(f32[8,4,4,16,128]{4,3,2,1,0:T(8,128)} %bitcast.11), calls=%async_computation.1 | async-start | bytes 2097152 | tf_op jit(solution)/shard_map/all_to_all | solution.py:720
  36.9 12.8 %collective-permute-start.5 = (f32[8,4,32,128]{3,2,1,0:T(8,128)S(1)}, f32[8,4,32,128]{3,2,1,0:T(8,128)S(1)}, u32[]{:S(2)}, u32[]{:S(2)}) collective-permute-start(f32[8,4,32,128]{3,2,1,0:T(8,128)S(1)} %bitcast.17), channel_id=1, source_target_pairs={{0,16},{16,0},{1,17},{17,1},{2,18},{18,2},{3,19},{19,3},{4,20},{20... | collective-permute-start | bytes 1572872 | tf_op jit(solution)/shard_map/ppermute | solution.py:757
  57.8 8.4 %collective-permute-start.6 = (f32[32,16,128]{2,1,0:T(8,128)}, f32[32,16,128]{2,1,0:T(8,128)S(1)}, u32[]{:S(2)}, u32[]{:S(2)}) collective-permute-start(f32[32,16,128]{2,1,0:T(8,128)} %get-tuple-element.133), channel_id=1, source_target_pairs={{0,1},{1,0},{2,3},{3,2},{4,5},{5,4},{6,7},{7,6},{8,9},{9,8},{10,11... | collective-permute-start | bytes 786440 | tf_op jit(solution)/shard_map/ppermute | solution.py:200
  59.4 7.3 %collective-permute-start.7 = (f32[32,16,128]{2,1,0:T(8,128)S(1)}, f32[32,16,128]{2,1,0:T(8,128)S(1)}, u32[]{:S(2)}, u32[]{:S(2)}) collective-permute-start(f32[32,16,128]{2,1,0:T(8,128)S(1)} %get-tuple-element.134), channel_id=1, source_target_pairs={{1,4},{4,1},{5,8},{8,5},{9,12},{12,9},{13,14},{14,13},{15,10},{10,... | collective-permute-start | bytes 786440 | tf_op jit(solution)/shard_map/ppermute | solution.py:204
  64.6 5.4 %collective-permute-start.4 = (f32[48,8,128]{2,1,0:T(8,128)S(1)}, f32[48,8,128]{2,1,0:T(8,128)S(1)}, u32[]{:S(2)}, u32[]{:S(2)}) collective-permute-start(f32[48,8,128]{2,1,0:T(8,128)S(1)} %get-tuple-element.130), channel_id=1, source_target_pairs={{1,4},{4,1},{5,8},{8,5},{9,12},{12,9},{13,14},{14,13},{15,10},{10,... | collective-permute-start | bytes 589832 | tf_op jit(solution)/shard_map/ppermute | solution.py:204
  65.2 6.8 %collective-permute-start.16 = (f32[48,8,128]{2,1,0:T(8,128)S(1)}, f32[48,8,128]{2,1,0:T(8,128)S(1)}, u32[]{:S(2)}, u32[]{:S(2)}) collective-permute-start(f32[48,8,128]{2,1,0:T(8,128)S(1)} %get-tuple-element.156), channel_id=1, source_target_pairs={{0,1},{1,0},{2,3},{3,2},{4,5},{5,4},{6,7},{7,6},{8,9},{9,8},{10,11... | collective-permute-start | bytes 589832 | tf_op jit(solution)/shard_map/ppermute | solution.py:200
  66.2 5.8 %collective-permute-start.17 = (f32[48,8,128]{2,1,0:T(8,128)S(1)}, f32[48,8,128]{2,1,0:T(8,128)S(1)}, u32[]{:S(2)}, u32[]{:S(2)}) collective-permute-start(f32[48,8,128]{2,1,0:T(8,128)S(1)} %get-tuple-element.157), channel_id=1, source_target_pairs={{1,4},{4,1},{5,8},{8,5},{9,12},{12,9},{13,14},{14,13},{15,10},{10,... | collective-permute-start | bytes 589832 | tf_op jit(solution)/shard_map/ppermute | solution.py:204
  71.4 4.5 %collective-permute-start.9 = (f32[32,8,128]{2,1,0:T(8,128)S(1)}, f32[32,8,128]{2,1,0:T(8,128)S(1)}, u32[]{:S(2)}, u32[]{:S(2)}) collective-permute-start(f32[32,8,128]{2,1,0:T(8,128)S(1)} %get-tuple-element.139), channel_id=1, source_target_pairs={{1,4},{4,1},{5,8},{8,5},{9,12},{12,9},{13,14},{14,13},{15,10},{10,... | collective-permute-start | bytes 393224 | tf_op jit(solution)/shard_map/ppermute | solution.py:204
  73.3 4.6 %collective-permute-start.18 = (f32[32,8,128]{2,1,0:T(8,128)S(1)}, f32[32,8,128]{2,1,0:T(8,128)S(1)}, u32[]{:S(2)}, u32[]{:S(2)}) collective-permute-start(f32[32,8,128]{2,1,0:T(8,128)S(1)} %get-tuple-element.160), channel_id=1, source_target_pairs={{0,1},{1,0},{2,3},{3,2},{4,5},{5,4},{6,7},{7,6},{8,9},{9,8},{10,11... | collective-permute-start | bytes 393224 | tf_op jit(solution)/shard_map/ppermute | solution.py:200
  74.4 4.4 %collective-permute-start.19 = (f32[32,8,128]{2,1,0:T(8,128)S(1)}, f32[32,8,128]{2,1,0:T(8,128)S(1)}, u32[]{:S(2)}, u32[]{:S(2)}) collective-permute-start(f32[32,8,128]{2,1,0:T(8,128)S(1)} %get-tuple-element.161), channel_id=1, source_target_pairs={{1,4},{4,1},{5,8},{8,5},{9,12},{12,9},{13,14},{14,13},{15,10},{10,... | collective-permute-start | bytes 393224 | tf_op jit(solution)/shard_map/ppermute | solution.py:204
  77.6 4.4 %collective-permute-start.11 = (f32[32,8,128]{2,1,0:T(8,128)S(1)}, f32[32,8,128]{2,1,0:T(8,128)S(1)}, u32[]{:S(2)}, u32[]{:S(2)}) collective-permute-start(f32[32,8,128]{2,1,0:T(8,128)S(1)} %get-tuple-element.143), channel_id=1, source_target_pairs={{1,4},{4,1},{5,8},{8,5},{9,12},{12,9},{13,14},{14,13},{15,10},{10,... | collective-permute-start | bytes 393224 | tf_op jit(solution)/shard_map/ppermute | solution.py:204
  80.4 4.4 %collective-permute-start.21 = (f32[32,8,128]{2,1,0:T(8,128)S(1)}, f32[32,8,128]{2,1,0:T(8,128)S(1)}, u32[]{:S(2)}, u32[]{:S(2)}) collective-permute-start(f32[32,8,128]{2,1,0:T(8,128)S(1)} %get-tuple-element.165), channel_id=1, source_target_pairs={{1,4},{4,1},{5,8},{8,5},{9,12},{12,9},{13,14},{14,13},{15,10},{10,... | collective-permute-start | bytes 393224 | tf_op jit(solution)/shard_map/ppermute | solution.py:204
  83.5 4.4 %collective-permute-start.13 = (f32[32,8,128]{2,1,0:T(8,128)S(1)}, f32[32,8,128]{2,1,0:T(8,128)S(1)}, u32[]{:S(2)}, u32[]{:S(2)}) collective-permute-start(f32[32,8,128]{2,1,0:T(8,128)S(1)} %get-tuple-element.147), channel_id=1, source_target_pairs={{1,4},{4,1},{5,8},{8,5},{9,12},{12,9},{13,14},{14,13},{15,10},{10,... | collective-permute-start | bytes 393224 | tf_op jit(solution)/shard_map/ppermute | solution.py:204
  86.3 4.4 %collective-permute-start.23 = (f32[32,8,128]{2,1,0:T(8,128)S(1)}, f32[32,8,128]{2,1,0:T(8,128)S(1)}, u32[]{:S(2)}, u32[]{:S(2)}) collective-permute-start(f32[32,8,128]{2,1,0:T(8,128)S(1)} %get-tuple-element.169), channel_id=1, source_target_pairs={{1,4},{4,1},{5,8},{8,5},{9,12},{12,9},{13,14},{14,13},{15,10},{10,... | collective-permute-start | bytes 393224 | tf_op jit(solution)/shard_map/ppermute | solution.py:204
  89.6 4.4 %collective-permute-start.15 = (f32[32,8,128]{2,1,0:T(8,128)S(1)}, f32[32,8,128]{2,1,0:T(8,128)S(1)}, u32[]{:S(2)}, u32[]{:S(2)}) collective-permute-start(f32[32,8,128]{2,1,0:T(8,128)S(1)} %get-tuple-element.151), channel_id=1, source_target_pairs={{1,4},{4,1},{5,8},{8,5},{9,12},{12,9},{13,14},{14,13},{15,10},{10,... | collective-permute-start | bytes 393224 | tf_op jit(solution)/shard_map/ppermute | solution.py:204
  118.2 8.4 %collective-permute-start.38 = (f32[2,4,16,128]{3,2,1,0:T(8,128)S(1)}, f32[2,4,16,128]{3,2,1,0:T(8,128)S(1)}, u32[]{:S(2)}, u32[]{:S(2)}) collective-permute-start(f32[2,4,16,128]{3,2,1,0:T(8,128)S(1)} %get-tuple-element.211), channel_id=1, source_target_pairs={{0,12},{1,14},{2,15},{3,13},{4,8},{5,10},{6,11},{7,9},{8,4},{9,6},... | collective-permute-start | bytes 196616 | tf_op jit(solution)/shard_map/ppermute | solution.py:212
  121.5 10.8 %collective-permute-start.39 = (f32[2,4,16,128]{3,2,1,0:T(8,128)S(1)}, f32[2,4,16,128]{3,2,1,0:T(8,128)S(1)}, u32[]{:S(2)}, u32[]{:S(2)}) collective-permute-start(f32[2,4,16,128]{3,2,1,0:T(8,128)S(1)} %get-tuple-element.212), channel_id=1, source_target_pairs={{0,14},{1,12},{2,13},{3,15},{4,10},{5,8},{6,9},{7,11},{8,6},{9,4},... | collective-permute-start | bytes 196616 | tf_op jit(solution)/shard_map/ppermute | solution.py:212
  122.0 15.4 %collective-permute-start.40 = (f32[2,4,16,128]{3,2,1,0:T(8,128)S(1)}, f32[2,4,16,128]{3,2,1,0:T(8,128)S(1)}, u32[]{:S(2)}, u32[]{:S(2)}) collective-permute-start(f32[2,4,16,128]{3,2,1,0:T(8,128)S(1)} %get-tuple-element.213), channel_id=1, source_target_pairs={{0,8},{1,10},{2,11},{3,9},{4,12},{5,14},{6,15},{7,13},{8,0},{9,2},... | collective-permute-start | bytes 196616 | tf_op jit(solution)/shard_map/ppermute | solution.py:212
  123.0 14.5 %collective-permute-start.41 = (f32[2,4,16,128]{3,2,1,0:T(8,128)S(1)}, f32[2,4,16,128]{3,2,1,0:T(8,128)S(1)}, u32[]{:S(2)}, u32[]{:S(2)}) collective-permute-start(f32[2,4,16,128]{3,2,1,0:T(8,128)S(1)} %get-tuple-element.214), channel_id=1, source_target_pairs={{0,10},{1,8},{2,9},{3,11},{4,14},{5,12},{6,13},{7,15},{8,2},{9,0},... | collective-permute-start | bytes 196616 | tf_op jit(solution)/shard_map/ppermute | solution.py:212
  125.1 12.7 %collective-permute-start.42 = (f32[2,4,16,128]{3,2,1,0:T(8,128)S(1)}, f32[2,4,16,128]{3,2,1,0:T(8,128)S(1)}, u32[]{:S(2)}, u32[]{:S(2)}) collective-permute-start(f32[2,4,16,128]{3,2,1,0:T(8,128)S(1)} %get-tuple-element.215), channel_id=1, source_target_pairs={{0,4},{1,6},{2,7},{3,5},{4,0},{5,2},{6,3},{7,1},{8,12},{9,14},{10,... | collective-permute-start | bytes 196616 | tf_op jit(solution)/shard_map/ppermute | solution.py:212
  126.5 14.9 %collective-permute-start.43 = (f32[2,4,16,128]{3,2,1,0:T(8,128)S(1)}, f32[2,4,16,128]{3,2,1,0:T(8,128)S(1)}, u32[]{:S(2)}, u32[]{:S(2)}) collective-permute-start(f32[2,4,16,128]{3,2,1,0:T(8,128)S(1)} %get-tuple-element.216), channel_id=1, source_target_pairs={{0,6},{1,4},{2,5},{3,7},{4,2},{5,0},{6,1},{7,3},{8,14},{9,12},{10,... | collective-permute-start | bytes 196616 | tf_op jit(solution)/shard_map/ppermute | solution.py:212
  132.3 17.5 %collective-permute-start.46 = (f32[8,32,128]{2,1,0:T(8,128)S(1)}, f32[8,32,128]{2,1,0:T(8,128)S(1)}, u32[]{:S(2)}, u32[]{:S(2)}) collective-permute-start(f32[8,32,128]{2,1,0:T(8,128)S(1)} %get-tuple-element.226), channel_id=1, source_target_pairs={{0,12},{1,14},{2,15},{3,13},{4,8},{5,10},{6,11},{7,9},{8,4},{9,6},... | collective-permute-start | bytes 393224 | tf_op jit(solution)/shard_map/ppermute | solution.py:212
  137.5 12.7 %collective-permute-start.47 = (f32[8,32,128]{2,1,0:T(8,128)S(1)}, f32[8,32,128]{2,1,0:T(8,128)S(1)}, u32[]{:S(2)}, u32[]{:S(2)}) collective-permute-start(f32[8,32,128]{2,1,0:T(8,128)S(1)} %get-tuple-element.227), channel_id=1, source_target_pairs={{0,14},{1,12},{2,13},{3,15},{4,10},{5,8},{6,9},{7,11},{8,6},{9,4},... | collective-permute-start | bytes 393224 | tf_op jit(solution)/shard_map/ppermute | solution.py:212
  137.5 18.8 %collective-permute-start.48 = (f32[8,32,128]{2,1,0:T(8,128)S(1)}, f32[8,32,128]{2,1,0:T(8,128)S(1)}, u32[]{:S(2)}, u32[]{:S(2)}) collective-permute-start(f32[8,32,128]{2,1,0:T(8,128)S(1)} %get-tuple-element.228), channel_id=1, source_target_pairs={{0,8},{1,10},{2,11},{3,9},{4,12},{5,14},{6,15},{7,13},{8,0},{9,2},... | collective-permute-start | bytes 393224 | tf_op jit(solution)/shard_map/ppermute | solution.py:212
  137.8 5.6 %collective-permute-start.44 = (f32[2,4,16,128]{3,2,1,0:T(8,128)S(1)}, f32[2,4,16,128]{3,2,1,0:T(8,128)S(1)}, u32[]{:S(2)}, u32[]{:S(2)}) collective-permute-start(f32[2,4,16,128]{3,2,1,0:T(8,128)S(1)} %get-tuple-element.217), channel_id=1, source_target_pairs={{0,0},{1,2},{2,3},{3,1},{4,4},{5,6},{6,7},{7,5},{8,8},{9,10},{10,1... | collective-permute-start | bytes 196616 | tf_op jit(solution)/shard_map/ppermute | solution.py:212
  141.4 5.6 %collective-permute-start.45 = (f32[2,4,16,128]{3,2,1,0:T(8,128)S(1)}, f32[2,4,16,128]{3,2,1,0:T(8,128)S(1)}, u32[]{:S(2)}, u32[]{:S(2)}) collective-permute-start(f32[2,4,16,128]{3,2,1,0:T(8,128)S(1)} %get-tuple-element.218), channel_id=1, source_target_pairs={{0,2},{1,0},{2,1},{3,3},{4,6},{5,4},{6,5},{7,7},{8,10},{9,8},{10,9... | collective-permute-start | bytes 196616 | tf_op jit(solution)/shard_map/ppermute | solution.py:212
  143.4 17.5 %collective-permute-start.49 = (f32[8,32,128]{2,1,0:T(8,128)S(1)}, f32[8,32,128]{2,1,0:T(8,128)S(1)}, u32[]{:S(2)}, u32[]{:S(2)}) collective-permute-start(f32[8,32,128]{2,1,0:T(8,128)S(1)} %get-tuple-element.229), channel_id=1, source_target_pairs={{0,10},{1,8},{2,9},{3,11},{4,14},{5,12},{6,13},{7,15},{8,2},{9,0},... | collective-permute-start | bytes 393224 | tf_op jit(solution)/shard_map/ppermute | solution.py:212
  147.0 13.8 %collective-permute-start.50 = (f32[8,32,128]{2,1,0:T(8,128)S(1)}, f32[8,32,128]{2,1,0:T(8,128)S(1)}, u32[]{:S(2)}, u32[]{:S(2)}) collective-permute-start(f32[8,32,128]{2,1,0:T(8,128)S(1)} %get-tuple-element.230), channel_id=1, source_target_pairs={{0,4},{1,6},{2,7},{3,5},{4,0},{5,2},{6,3},{7,1},{8,12},{9,14},{10,... | collective-permute-start | bytes 393224 | tf_op jit(solution)/shard_map/ppermute | solution.py:212
  149.8 11.8 %collective-permute-start.51 = (f32[8,32,128]{2,1,0:T(8,128)S(1)}, f32[8,32,128]{2,1,0:T(8,128)S(1)}, u32[]{:S(2)}, u32[]{:S(2)}) collective-permute-start(f32[8,32,128]{2,1,0:T(8,128)S(1)} %get-tuple-element.231), channel_id=1, source_target_pairs={{0,6},{1,4},{2,5},{3,7},{4,2},{5,0},{6,1},{7,3},{8,14},{9,12},{10,... | collective-permute-start | bytes 393224 | tf_op jit(solution)/shard_map/ppermute | solution.py:212
  150.1 11.4 %collective-permute-start.52 = (f32[8,32,128]{2,1,0:T(8,128)S(1)}, f32[8,32,128]{2,1,0:T(8,128)S(1)}, u32[]{:S(2)}, u32[]{:S(2)}) collective-permute-start(f32[8,32,128]{2,1,0:T(8,128)S(1)} %get-tuple-element.232), channel_id=1, source_target_pairs={{0,0},{1,2},{2,3},{3,1},{4,4},{5,6},{6,7},{7,5},{8,8},{9,10},{10,1... | collective-permute-start | bytes 393224 | tf_op jit(solution)/shard_map/ppermute | solution.py:212
  156.3 6.6 %collective-permute-start.53 = (f32[8,32,128]{2,1,0:T(8,128)S(1)}, f32[8,32,128]{2,1,0:T(8,128)S(1)}, u32[]{:S(2)}, u32[]{:S(2)}) collective-permute-start(f32[8,32,128]{2,1,0:T(8,128)S(1)} %get-tuple-element.224), channel_id=1, source_target_pairs={{0,2},{1,0},{2,1},{3,3},{4,6},{5,4},{6,5},{7,7},{8,10},{9,8},{10,9... | collective-permute-start | bytes 393224 | tf_op jit(solution)/shard_map/ppermute | solution.py:212
  (37 other events, 251.6 us)

commit v6 on v5

--- a/solution.py
+++ b/solution.py
@@ -404,7 +404,7 @@
             out[x, 8 * t : 8 * t + 8, :] = totals[t]
         return carry
 
-    lax.fori_loop(0, NXA, column, 0)
+    lax.fori_loop(0, NXA, column, 0, unroll=4)
     if second:
         h = scal[H]
         for comp in range(2):
@@ -665,7 +665,7 @@
                     out[ix * 2 + part, 8 * t : 8 * t + 8, :] = totals[t]
             return carry
 
-        lax.fori_loop(0, GX, stripe, 0)
+        lax.fori_loop(0, GX, stripe, 0, unroll=4)
 
 
 def name_slots(index, picks):

time: 166 us -> 166 us (level)
  Pallas kernels: 58.6 us -> 53.2 us
  waiting for transfers between devices: 36.9 us -> 42.3 us
    ppermute x20, starting transfers between devices: 11 us -> 15.8 us  [to_sibling(): return lax.ppermute(x, 'gz', SWAP)]
    ppermute x17, starting transfers between devices: 8.25 us -> 4.81 us  [to_off_chip(): return lax.ppermute(x, ('gx', 'gy', 'gz'), OFF_PAIRS)]
    pallas_call x1, Pallas kernels: 5.21 us -> 2.98 us  [slab_body(): call(pack_grads, [((8, 2 * ZS, 128), F32)] * 8, [SMEM] + vmem(4), [pltpu....]
    ppermute x16, waiting for transfers between devices: 5.35 us -> 7.16 us  [to_blocks(): return lax.ppermute(x, ('gx', 'gy', 'gz'), spread(e))]
  transfers between devices with their start and end apart: 56 -> 56, of which waited for: 23 -> 25; matrix products, arithmetic and copies ran while one was open for 1% -> 1% of each run, Pallas kernels for 30% -> 27%
where the time goes in v6:
time: 166 us
  starting transfers between devices  63.5 us (38%)
  Pallas kernels  53.2 us (32%)
  waiting for transfers between devices  42.3 us (25%)
  local copies, waits for them, and re-layouts  5.19 us (3%)
    ppermute x16, starting transfers between devices, to_blocks(): return lax.ppermute(x, ('gx', 'gy', 'gz'), spread(e))  30.6 us
    pallas_call x16, Pallas kernels, slab_body(): call(functools.partial(round_kernel, kind, r), outs, vmem(len(args)), rou...  22.2 us
    ppermute x17, waiting for transfers between devices, to_off_chip(): return lax.ppermute(x, ('gx', 'gy', 'gz'), OFF_PAIRS)  17.1 us
    ppermute x20, starting transfers between devices, to_sibling(): return lax.ppermute(x, 'gz', SWAP)  15.8 us
    all_to_all x2, waiting for transfers between devices, exchange(): lax.all_to_all(x, ('gx', 'gy'), split_axis=0, concat_axis=0, tiled=True)  12.8 us
    all_to_all x2, starting transfers between devices, exchange(): lax.all_to_all(x, ('gx', 'gy'), split_axis=0, concat_axis=0, tiled=True)  11 us
    ppermute x16, waiting for transfers between devices, to_blocks(): return lax.ppermute(x, ('gx', 'gy', 'gz'), spread(e))  7.16 us
    pallas_call x1, Pallas kernels, slab_body(): call(functools.partial(gather_half, True), [coef_shape, half_shape, half_...  6.56 us
  transfers between devices with their start and end apart: 56, of which 25 were waited for; matrix products, arithmetic and copies ran while one was open for 1% of the time, Pallas kernels for 27%

profile of v6, /device:TPU:1, one launch (start us, length us, event | category | flops | bytes accessed | tf_op | source)
XLA Modules:
  0.0 165.6 jit_solution(14394317314687127195)
XLA Ops:
  2.7 1.6 shard_map.157
  8.0 7.0 %all-to-all-start = ((f32[8,168,128]{2,1,0:T(8,128)}), f32[8,168,128]{2,1,0:T(8,128)S(1)}, u32[]{:S(2)}, u32[]{:S(2)}) async-start(f32[8,168,128]{2,1,0:T(8,128)} %shard_map.159), calls=%async_computation | async-start | bytes 1376256 | tf_op jit(solution)/shard_map/all_to_all | solution.py:720
  15.0 2.7 %shard_map.161 = (f32[4,4,4,16,128]{4,3,2,1,0:T(8,128)S(1)}, f32[4,4,4,16,128]{4,3,2,1,0:T(8,128)S(1)}) custom-call(s32[8]{0:T(128)S(1)} %stack.32.scal, f32[8,64,128]{2,1,0:T(8,128)S(1)} %copy-done.5, f32[8,64,128]{2,1,0:T(8,128)S(1)} %copy-done.6, f32[8,64,128]{2,1,0:T(8,128)S(1)} %copy-done.7, f32[8,64,128]{2,1,0:T(8,128)S(1)} %copy-done.8), custom_call_target="tpu_custom_call" | custom-call | flops 1048576 | bytes 2097152 | tf_op jit(solution)/shard_map/pallas_call | solution.py:760
  21.0 11.9 %all-to-all-done = f32[8,168,128]{2,1,0:T(8,128)S(1)} async-done(((f32[8,168,128]{2,1,0:T(8,128)}), f32[8,168,128]{2,1,0:T(8,128)S(1)}, u32[]{:S(2)}, u32[]{:S(2)}) %all-to-all-start) | async-done | bytes 688160 | tf_op jit(solution)/shard_map/all_to_all | solution.py:720
  32.9 4.0 %all-to-all-start.1 = ((f32[8,4,4,16,128]{4,3,2,1,0:T(8,128)}), f32[8,4,4,16,128]{4,3,2,1,0:T(8,128)S(1)}, u32[]{:S(2)}, u32[]{:S(2)}) async-start(f32[8,4,4,16,128]{4,3,2,1,0:T(8,128)} %bitcast.11), calls=%async_computation.1 | async-start | bytes 2097152 | tf_op jit(solution)/shard_map/all_to_all | solution.py:720
  41.6 5.6 %shard_map.164.refs_0_ = f32[32,32,128]{2,1,0:T(8,128)S(1)} custom-call(s32[8]{0:T(128)S(1)} %stack.32.scal, f32[8,4,32,128]{3,2,1,0:T(8,128)S(1)} %bitcast.18, s32[32,128]{1,0:T(8,128)S(1)} %get-tuple-element.125.ids_slab.ids), custom_call_target="tpu_custom_call" | custom-call | flops 16777216 | bytes 1048576 | tf_op jit(solution)/shard_map/pallas_call | solution.py:775
  47.2 2.5 %collective-permute-done.5.table = f32[8,4,32,128]{3,2,1,0:T(8,128)S(1)} collective-permute-done((f32[8,4,32,128]{3,2,1,0:T(8,128)S(1)}, f32[8,4,32,128]{3,2,1,0:T(8,128)S(1)}, u32[]{:S(2)}, u32[]{:S(2)}) %collective-permute-start.5) | collective-permute-done | bytes 524320 | tf_op jit(solution)/shard_map/ppermute | solution.py:757
  49.7 6.6 %shard_map.165 = (f32[32,32,128]{2,1,0:T(8,128)S(1)}, f32[32,16,128]{2,1,0:T(8,128)}, f32[32,16,128]{2,1,0:T(8,128)S(1)}) custom-call(s32[8]{0:T(128)S(1)} %stack.32.scal, f32[8,4,32,128]{3,2,1,0:T(8,128)S(1)} %collective-permute-done.5.table, s32[32,128]{1,0:T(8,128)S(1)} %get-tuple-element.125.ids_slab.ids, f32[32,32,128]{2,1,0:T(8,128)S(1)} %shard_map.164.refs_0_), custom_call_target="tpu_custom_call" | custom-call | flops 16777216 | bytes 2097152 | tf_op jit(solution)/shard_map/pallas_call | solution.py:778
  56.3 1.6 collective-permute-start.6
  59.2 1.8 %shard_map.162.index = s32[2,40,128]{2,1,0:T(8,128)S(1)} custom-call(s32[8]{0:T(128)S(1)} %stack.32.scal, s32[32,128]{1,0:T(8,128)S(1)} %get-tuple-element.125.ids_slab.ids, s32[32,128]{1,0:T(8,128)S(1)} %get-tuple-element.126.ids_owner), custom_call_target="tpu_custom_call" | custom-call | flops 16777216 | bytes 262144 | tf_op jit(solution)/shard_map/pallas_call | solution.py:790
  62.9 1.8 %collective-permute-start.3 = (f32[48,8,128]{2,1,0:T(8,128)S(1)}, f32[48,8,128]{2,1,0:T(8,128)S(1)}, u32[]{:S(2)}, u32[]{:S(2)}) collective-permute-start(f32[48,8,128]{2,1,0:T(8,128)S(1)} %get-tuple-element.129), channel_id=1, source_target_pairs={{0,1},{1,0},{2,3},{3,2},{4,5},{5,4},{6,7},{7,6},{8,9},{9,8},{10,11... | collective-permute-start | bytes 589832 | tf_op jit(solution)/shard_map/ppermute | solution.py:200
  64.7 2.5 %collective-permute-start.16 = (f32[48,8,128]{2,1,0:T(8,128)S(1)}, f32[48,8,128]{2,1,0:T(8,128)S(1)}, u32[]{:S(2)}, u32[]{:S(2)}) collective-permute-start(f32[48,8,128]{2,1,0:T(8,128)S(1)} %get-tuple-element.156), channel_id=1, source_target_pairs={{0,1},{1,0},{2,3},{3,2},{4,5},{5,4},{6,7},{7,6},{8,9},{9,8},{10,11... | collective-permute-start | bytes 589832 | tf_op jit(solution)/shard_map/ppermute | solution.py:200
  67.8 2.3 %collective-permute-done.4.refs_5_ = f32[48,8,128]{2,1,0:T(8,128)S(1)} collective-permute-done((f32[48,8,128]{2,1,0:T(8,128)S(1)}, f32[48,8,128]{2,1,0:T(8,128)S(1)}, u32[]{:S(2)}, u32[]{:S(2)}) %collective-permute-start.4) | collective-permute-done | bytes 196640 | tf_op jit(solution)/shard_map/ppermute | solution.py:204
  73.6 1.8 %collective-permute-start.18 = (f32[32,8,128]{2,1,0:T(8,128)S(1)}, f32[32,8,128]{2,1,0:T(8,128)S(1)}, u32[]{:S(2)}, u32[]{:S(2)}) collective-permute-start(f32[32,8,128]{2,1,0:T(8,128)S(1)} %get-tuple-element.160), channel_id=1, source_target_pairs={{0,1},{1,0},{2,3},{3,2},{4,5},{5,4},{6,7},{7,6},{8,9},{9,8},{10,11... | collective-permute-start | bytes 393224 | tf_op jit(solution)/shard_map/ppermute | solution.py:200
  94.6 1.6 shard_map.175
  113.6 1.8 %shard_map.178 = (f32[32,16,128]{2,1,0:T(8,128)S(1)}, f32[40,32,128]{2,1,0:T(8,128)}, f32[2,32,16,128]{3,2,1,0:T(8,128)S(1)}) custom-call(s32[3,8,128]{2,1,0:T(8,128)S(1)} %get-tuple-element.120.refs_0_, f32[16,32,128]{2,1,0:T(8,128)S(1)} %get-tuple-element.121.refs_1_, s32[32,128]{1,0:T(8,128)S(1)} %get-tuple-element.122.refs_2_, ...), custom_call_target="tpu_custom_call" | custom-call | flops 16777216 | bytes 4194304 | tf_op jit(solution)/shard_map/pallas_call | solution.py:829
  115.4 1.8 %collective-permute-done.37.refs_5_ = f32[32,8,128]{2,1,0:T(8,128)S(1)} collective-permute-done((f32[32,8,128]{2,1,0:T(8,128)S(1)}, f32[32,8,128]{2,1,0:T(8,128)S(1)}, u32[]{:S(2)}, u32[]{:S(2)}) %collective-permute-start.37) | collective-permute-done | bytes 131104 | tf_op jit(solution)/shard_map/ppermute | solution.py:204
  117.2 1.8 %shard_map.182 = (f32[32,16,128]{2,1,0:T(8,128)S(1)}, f32[40,32,128]{2,1,0:T(8,128)}, f32[2,32,16,128]{3,2,1,0:T(8,128)S(1)}) custom-call(s32[3,8,128]{2,1,0:T(8,128)S(1)} %get-tuple-element.120.refs_0_, f32[16,32,128]{2,1,0:T(8,128)S(1)} %get-tuple-element.153.refs_1_, s32[32,128]{1,0:T(8,128)S(1)} %get-tuple-element.154.refs_2_, ...), custom_call_target="tpu_custom_call" | custom-call | flops 16777216 | bytes 4194304 | tf_op jit(solution)/shard_map/pallas_call | solution.py:829
  121.3 2.2 %collective-permute-start.39 = (f32[2,4,16,128]{3,2,1,0:T(8,128)S(1)}, f32[2,4,16,128]{3,2,1,0:T(8,128)S(1)}, u32[]{:S(2)}, u32[]{:S(2)}) collective-permute-start(f32[2,4,16,128]{3,2,1,0:T(8,128)S(1)} %get-tuple-element.212), channel_id=1, source_target_pairs={{0,14},{1,12},{2,13},{3,15},{4,10},{5,8},{6,9},{7,11},{8,6},{9,4},... | collective-permute-start | bytes 196616 | tf_op jit(solution)/shard_map/ppermute | solution.py:212
  123.5 2.9 %collective-permute-start.41 = (f32[2,4,16,128]{3,2,1,0:T(8,128)S(1)}, f32[2,4,16,128]{3,2,1,0:T(8,128)S(1)}, u32[]{:S(2)}, u32[]{:S(2)}) collective-permute-start(f32[2,4,16,128]{3,2,1,0:T(8,128)S(1)} %get-tuple-element.214), channel_id=1, source_target_pairs={{0,10},{1,8},{2,9},{3,11},{4,14},{5,12},{6,13},{7,15},{8,2},{9,0},... | collective-permute-start | bytes 196616 | tf_op jit(solution)/shard_map/ppermute | solution.py:212
  128.8 3.0 %shard_map.185 = (f32[8,32,128]{2,1,0:T(8,128)S(1)}, f32[8,32,128]{2,1,0:T(8,128)S(1)}, f32[8,32,128]{2,1,0:T(8,128)S(1)}, f32[8,32,128]{2,1,0:T(8,128)S(1)}, f3...) custom-call(s32[8]{0:T(128)S(1)} %stack.32.scal, ...), custom_call_target="tpu_custom_call" | custom-call | flops 4194304 | bytes 16777216 | tf_op jit(solution)/shard_map/pallas_call | solution.py:853
  131.8 3.2 %collective-permute-start.46 = (f32[8,32,128]{2,1,0:T(8,128)S(1)}, f32[8,32,128]{2,1,0:T(8,128)S(1)}, u32[]{:S(2)}, u32[]{:S(2)}) collective-permute-start(f32[8,32,128]{2,1,0:T(8,128)S(1)} %get-tuple-element.226), channel_id=1, source_target_pairs={{0,12},{1,14},{2,15},{3,13},{4,8},{5,10},{6,11},{7,9},{8,4},{9,6},... | collective-permute-start | bytes 393224 | tf_op jit(solution)/shard_map/ppermute | solution.py:212
  135.0 3.8 %collective-permute-start.47 = (f32[8,32,128]{2,1,0:T(8,128)S(1)}, f32[8,32,128]{2,1,0:T(8,128)S(1)}, u32[]{:S(2)}, u32[]{:S(2)}) collective-permute-start(f32[8,32,128]{2,1,0:T(8,128)S(1)} %get-tuple-element.227), channel_id=1, source_target_pairs={{0,14},{1,12},{2,13},{3,15},{4,10},{5,8},{6,9},{7,11},{8,6},{9,4},... | collective-permute-start | bytes 393224 | tf_op jit(solution)/shard_map/ppermute | solution.py:212
  138.8 1.9 %collective-permute-start.44 = (f32[2,4,16,128]{3,2,1,0:T(8,128)S(1)}, f32[2,4,16,128]{3,2,1,0:T(8,128)S(1)}, u32[]{:S(2)}, u32[]{:S(2)}) collective-permute-start(f32[2,4,16,128]{3,2,1,0:T(8,128)S(1)} %get-tuple-element.217), channel_id=1, source_target_pairs={{0,0},{1,2},{2,3},{3,1},{4,4},{5,6},{6,7},{7,5},{8,8},{9,10},{10,1... | collective-permute-start | bytes 196616 | tf_op jit(solution)/shard_map/ppermute | solution.py:212
  140.7 1.9 %collective-permute-start.45 = (f32[2,4,16,128]{3,2,1,0:T(8,128)S(1)}, f32[2,4,16,128]{3,2,1,0:T(8,128)S(1)}, u32[]{:S(2)}, u32[]{:S(2)}) collective-permute-start(f32[2,4,16,128]{3,2,1,0:T(8,128)S(1)} %get-tuple-element.218), channel_id=1, source_target_pairs={{0,2},{1,0},{2,1},{3,3},{4,6},{5,4},{6,5},{7,7},{8,10},{9,8},{10,9... | collective-permute-start | bytes 196616 | tf_op jit(solution)/shard_map/ppermute | solution.py:212
  142.6 1.6 collective-permute-done.44.refs_6_
  144.2 2.7 %collective-permute-start.49 = (f32[8,32,128]{2,1,0:T(8,128)S(1)}, f32[8,32,128]{2,1,0:T(8,128)S(1)}, u32[]{:S(2)}, u32[]{:S(2)}) collective-permute-start(f32[8,32,128]{2,1,0:T(8,128)S(1)} %get-tuple-element.229), channel_id=1, source_target_pairs={{0,10},{1,8},{2,9},{3,11},{4,14},{5,12},{6,13},{7,15},{8,2},{9,0},... | collective-permute-start | bytes 393224 | tf_op jit(solution)/shard_map/ppermute | solution.py:212
  148.4 4.3 %collective-permute-start.52 = (f32[8,32,128]{2,1,0:T(8,128)S(1)}, f32[8,32,128]{2,1,0:T(8,128)S(1)}, u32[]{:S(2)}, u32[]{:S(2)}) collective-permute-start(f32[8,32,128]{2,1,0:T(8,128)S(1)} %get-tuple-element.232), channel_id=1, source_target_pairs={{0,0},{1,2},{2,3},{3,1},{4,4},{5,6},{6,7},{7,5},{8,8},{9,10},{10,1... | collective-permute-start | bytes 393224 | tf_op jit(solution)/shard_map/ppermute | solution.py:212
  152.7 2.1 %collective-permute-done.48.refs_2_ = f32[8,32,128]{2,1,0:T(8,128)S(1)} collective-permute-done((f32[8,32,128]{2,1,0:T(8,128)S(1)}, f32[8,32,128]{2,1,0:T(8,128)S(1)}, u32[]{:S(2)}, u32[]{:S(2)}) %collective-permute-start.48) | collective-permute-done | bytes 131104 | tf_op jit(solution)/shard_map/ppermute | solution.py:212
  154.8 2.5 %collective-permute-start.53 = (f32[8,32,128]{2,1,0:T(8,128)S(1)}, f32[8,32,128]{2,1,0:T(8,128)S(1)}, u32[]{:S(2)}, u32[]{:S(2)}) collective-permute-start(f32[8,32,128]{2,1,0:T(8,128)S(1)} %get-tuple-element.224), channel_id=1, source_target_pairs={{0,2},{1,0},{2,1},{3,3},{4,6},{5,4},{6,5},{7,7},{8,10},{9,8},{10,9... | collective-permute-start | bytes 393224 | tf_op jit(solution)/shard_map/ppermute | solution.py:212
  160.5 2.1 %collective-permute-done.53.refs_7_ = f32[8,32,128]{2,1,0:T(8,128)S(1)} collective-permute-done((f32[8,32,128]{2,1,0:T(8,128)S(1)}, f32[8,32,128]{2,1,0:T(8,128)S(1)}, u32[]{:S(2)}, u32[]{:S(2)}) %collective-permute-start.53) | collective-permute-done | bytes 131104 | tf_op jit(solution)/shard_map/ppermute | solution.py:212
  162.6 2.8 %shard_map.187 = f32[2048,128]{1,0:T(8,128)} custom-call(s32[8]{0:T(128)S(1)} %stack.32.scal, bf16[1024,1024]{1,0:T(8,128)(2,1)S(1)} %shard_map.186.picks, f32[8,32,128]{2,1,0:T(8,128)S(1)} %collective-permute-done.46.refs_0_, f32[8,32,128]{2,1,0:T(8,128)S(1)} %collective-permute-done.47.refs_1_, f32[8,32,128]{2,1,0:T(8,128)S(1)} %collective-permute-done.48.refs_2_, ...), custom_call_target="tpu_custom_call" | custom-call | flops 268435456 | bytes 4194304 | tf_op jit(solution)/shard_map/pallas_call | solution.py:872
  (144 shorter events, 67.0 us)
Async XLA Ops:
  8.0 24.8 %all-to-all-start = ((f32[8,168,128]{2,1,0:T(8,128)}), f32[8,168,128]{2,1,0:T(8,128)S(1)}, u32[]{:S(2)}, u32[]{:S(2)}) async-start(f32[8,168,128]{2,1,0:T(8,128)} %shard_map.159), calls=%async_computation | async-start | bytes 1376256 | tf_op jit(solution)/shard_map/all_to_all | solution.py:720
  32.9 29.2 %all-to-all-start.1 = ((f32[8,4,4,16,128]{4,3,2,1,0:T(8,128)}), f32[8,4,4,16,128]{4,3,2,1,0:T(8,128)S(1)}, u32[]{:S(2)}, u32[]{:S(2)}) async-start(f32[8,4,4,16,128]{4,3,2,1,0:T(8,128)} %bitcast.11), calls=%async_computation.1 | async-start | bytes 2097152 | tf_op jit(solution)/shard_map/all_to_all | solution.py:720
  36.9 12.8 %collective-permute-start.5 = (f32[8,4,32,128]{3,2,1,0:T(8,128)S(1)}, f32[8,4,32,128]{3,2,1,0:T(8,128)S(1)}, u32[]{:S(2)}, u32[]{:S(2)}) collective-permute-start(f32[8,4,32,128]{3,2,1,0:T(8,128)S(1)} %bitcast.17), channel_id=1, source_target_pairs={{0,16},{16,0},{1,17},{17,1},{2,18},{18,2},{3,19},{19,3},{4,20},{20... | collective-permute-start | bytes 1572872 | tf_op jit(solution)/shard_map/ppermute | solution.py:757
  56.3 10.9 %collective-permute-start.6 = (f32[32,16,128]{2,1,0:T(8,128)}, f32[32,16,128]{2,1,0:T(8,128)S(1)}, u32[]{:S(2)}, u32[]{:S(2)}) collective-permute-start(f32[32,16,128]{2,1,0:T(8,128)} %get-tuple-element.133), channel_id=1, source_target_pairs={{0,1},{1,0},{2,3},{3,2},{4,5},{5,4},{6,7},{7,6},{8,9},{9,8},{10,11... | collective-permute-start | bytes 786440 | tf_op jit(solution)/shard_map/ppermute | solution.py:200
  57.9 9.3 %collective-permute-start.7 = (f32[32,16,128]{2,1,0:T(8,128)S(1)}, f32[32,16,128]{2,1,0:T(8,128)S(1)}, u32[]{:S(2)}, u32[]{:S(2)}) collective-permute-start(f32[32,16,128]{2,1,0:T(8,128)S(1)} %get-tuple-element.134), channel_id=1, source_target_pairs={{1,4},{4,1},{5,8},{8,5},{9,12},{12,9},{13,14},{14,13},{15,10},{10,... | collective-permute-start | bytes 786440 | tf_op jit(solution)/shard_map/ppermute | solution.py:204
  62.9 4.9 %collective-permute-start.3 = (f32[48,8,128]{2,1,0:T(8,128)S(1)}, f32[48,8,128]{2,1,0:T(8,128)S(1)}, u32[]{:S(2)}, u32[]{:S(2)}) collective-permute-start(f32[48,8,128]{2,1,0:T(8,128)S(1)} %get-tuple-element.129), channel_id=1, source_target_pairs={{0,1},{1,0},{2,3},{3,2},{4,5},{5,4},{6,7},{7,6},{8,9},{9,8},{10,11... | collective-permute-start | bytes 589832 | tf_op jit(solution)/shard_map/ppermute | solution.py:200
  64.7 5.4 %collective-permute-start.4 = (f32[48,8,128]{2,1,0:T(8,128)S(1)}, f32[48,8,128]{2,1,0:T(8,128)S(1)}, u32[]{:S(2)}, u32[]{:S(2)}) collective-permute-start(f32[48,8,128]{2,1,0:T(8,128)S(1)} %get-tuple-element.130), channel_id=1, source_target_pairs={{1,4},{4,1},{5,8},{8,5},{9,12},{12,9},{13,14},{14,13},{15,10},{10,... | collective-permute-start | bytes 589832 | tf_op jit(solution)/shard_map/ppermute | solution.py:204
  64.7 7.1 %collective-permute-start.16 = (f32[48,8,128]{2,1,0:T(8,128)S(1)}, f32[48,8,128]{2,1,0:T(8,128)S(1)}, u32[]{:S(2)}, u32[]{:S(2)}) collective-permute-start(f32[48,8,128]{2,1,0:T(8,128)S(1)} %get-tuple-element.156), channel_id=1, source_target_pairs={{0,1},{1,0},{2,3},{3,2},{4,5},{5,4},{6,7},{7,6},{8,9},{9,8},{10,11... | collective-permute-start | bytes 589832 | tf_op jit(solution)/shard_map/ppermute | solution.py:200
  67.2 5.1 %collective-permute-start.17 = (f32[48,8,128]{2,1,0:T(8,128)S(1)}, f32[48,8,128]{2,1,0:T(8,128)S(1)}, u32[]{:S(2)}, u32[]{:S(2)}) collective-permute-start(f32[48,8,128]{2,1,0:T(8,128)S(1)} %get-tuple-element.157), channel_id=1, source_target_pairs={{1,4},{4,1},{5,8},{8,5},{9,12},{12,9},{13,14},{14,13},{15,10},{10,... | collective-permute-start | bytes 589832 | tf_op jit(solution)/shard_map/ppermute | solution.py:204
  71.8 4.4 %collective-permute-start.9 = (f32[32,8,128]{2,1,0:T(8,128)S(1)}, f32[32,8,128]{2,1,0:T(8,128)S(1)}, u32[]{:S(2)}, u32[]{:S(2)}) collective-permute-start(f32[32,8,128]{2,1,0:T(8,128)S(1)} %get-tuple-element.139), channel_id=1, source_target_pairs={{1,4},{4,1},{5,8},{8,5},{9,12},{12,9},{13,14},{14,13},{15,10},{10,... | collective-permute-start | bytes 393224 | tf_op jit(solution)/shard_map/ppermute | solution.py:204
  73.6 4.9 %collective-permute-start.18 = (f32[32,8,128]{2,1,0:T(8,128)S(1)}, f32[32,8,128]{2,1,0:T(8,128)S(1)}, u32[]{:S(2)}, u32[]{:S(2)}) collective-permute-start(f32[32,8,128]{2,1,0:T(8,128)S(1)} %get-tuple-element.160), channel_id=1, source_target_pairs={{0,1},{1,0},{2,3},{3,2},{4,5},{5,4},{6,7},{7,6},{8,9},{9,8},{10,11... | collective-permute-start | bytes 393224 | tf_op jit(solution)/shard_map/ppermute | solution.py:200
  75.3 4.4 %collective-permute-start.19 = (f32[32,8,128]{2,1,0:T(8,128)S(1)}, f32[32,8,128]{2,1,0:T(8,128)S(1)}, u32[]{:S(2)}, u32[]{:S(2)}) collective-permute-start(f32[32,8,128]{2,1,0:T(8,128)S(1)} %get-tuple-element.161), channel_id=1, source_target_pairs={{1,4},{4,1},{5,8},{8,5},{9,12},{12,9},{13,14},{14,13},{15,10},{10,... | collective-permute-start | bytes 393224 | tf_op jit(solution)/shard_map/ppermute | solution.py:204
  77.9 4.4 %collective-permute-start.11 = (f32[32,8,128]{2,1,0:T(8,128)S(1)}, f32[32,8,128]{2,1,0:T(8,128)S(1)}, u32[]{:S(2)}, u32[]{:S(2)}) collective-permute-start(f32[32,8,128]{2,1,0:T(8,128)S(1)} %get-tuple-element.143), channel_id=1, source_target_pairs={{1,4},{4,1},{5,8},{8,5},{9,12},{12,9},{13,14},{14,13},{15,10},{10,... | collective-permute-start | bytes 393224 | tf_op jit(solution)/shard_map/ppermute | solution.py:204
  81.4 4.4 %collective-permute-start.21 = (f32[32,8,128]{2,1,0:T(8,128)S(1)}, f32[32,8,128]{2,1,0:T(8,128)S(1)}, u32[]{:S(2)}, u32[]{:S(2)}) collective-permute-start(f32[32,8,128]{2,1,0:T(8,128)S(1)} %get-tuple-element.165), channel_id=1, source_target_pairs={{1,4},{4,1},{5,8},{8,5},{9,12},{12,9},{13,14},{14,13},{15,10},{10,... | collective-permute-start | bytes 393224 | tf_op jit(solution)/shard_map/ppermute | solution.py:204
  90.2 4.4 %collective-permute-start.15 = (f32[32,8,128]{2,1,0:T(8,128)S(1)}, f32[32,8,128]{2,1,0:T(8,128)S(1)}, u32[]{:S(2)}, u32[]{:S(2)}) collective-permute-start(f32[32,8,128]{2,1,0:T(8,128)S(1)} %get-tuple-element.151), channel_id=1, source_target_pairs={{1,4},{4,1},{5,8},{8,5},{9,12},{12,9},{13,14},{14,13},{15,10},{10,... | collective-permute-start | bytes 393224 | tf_op jit(solution)/shard_map/ppermute | solution.py:204
  102.9 4.4 %collective-permute-start.27 = (f32[32,8,128]{2,1,0:T(8,128)S(1)}, f32[32,8,128]{2,1,0:T(8,128)S(1)}, u32[]{:S(2)}, u32[]{:S(2)}) collective-permute-start(f32[32,8,128]{2,1,0:T(8,128)S(1)} %get-tuple-element.180), channel_id=1, source_target_pairs={{1,4},{4,1},{5,8},{8,5},{9,12},{12,9},{13,14},{14,13},{15,10},{10,... | collective-permute-start | bytes 393224 | tf_op jit(solution)/shard_map/ppermute | solution.py:204
  119.9 7.7 %collective-permute-start.38 = (f32[2,4,16,128]{3,2,1,0:T(8,128)S(1)}, f32[2,4,16,128]{3,2,1,0:T(8,128)S(1)}, u32[]{:S(2)}, u32[]{:S(2)}) collective-permute-start(f32[2,4,16,128]{3,2,1,0:T(8,128)S(1)} %get-tuple-element.211), channel_id=1, source_target_pairs={{0,12},{1,14},{2,15},{3,13},{4,8},{5,10},{6,11},{7,9},{8,4},{9,6},... | collective-permute-start | bytes 196616 | tf_op jit(solution)/shard_map/ppermute | solution.py:212
  121.3 10.5 %collective-permute-start.39 = (f32[2,4,16,128]{3,2,1,0:T(8,128)S(1)}, f32[2,4,16,128]{3,2,1,0:T(8,128)S(1)}, u32[]{:S(2)}, u32[]{:S(2)}) collective-permute-start(f32[2,4,16,128]{3,2,1,0:T(8,128)S(1)} %get-tuple-element.212), channel_id=1, source_target_pairs={{0,14},{1,12},{2,13},{3,15},{4,10},{5,8},{6,9},{7,11},{8,6},{9,4},... | collective-permute-start | bytes 196616 | tf_op jit(solution)/shard_map/ppermute | solution.py:212
  123.5 11.5 %collective-permute-start.40 = (f32[2,4,16,128]{3,2,1,0:T(8,128)S(1)}, f32[2,4,16,128]{3,2,1,0:T(8,128)S(1)}, u32[]{:S(2)}, u32[]{:S(2)}) collective-permute-start(f32[2,4,16,128]{3,2,1,0:T(8,128)S(1)} %get-tuple-element.213), channel_id=1, source_target_pairs={{0,8},{1,10},{2,11},{3,9},{4,12},{5,14},{6,15},{7,13},{8,0},{9,2},... | collective-permute-start | bytes 196616 | tf_op jit(solution)/shard_map/ppermute | solution.py:212
  123.5 15.2 %collective-permute-start.41 = (f32[2,4,16,128]{3,2,1,0:T(8,128)S(1)}, f32[2,4,16,128]{3,2,1,0:T(8,128)S(1)}, u32[]{:S(2)}, u32[]{:S(2)}) collective-permute-start(f32[2,4,16,128]{3,2,1,0:T(8,128)S(1)} %get-tuple-element.214), channel_id=1, source_target_pairs={{0,10},{1,8},{2,9},{3,11},{4,14},{5,12},{6,13},{7,15},{8,2},{9,0},... | collective-permute-start | bytes 196616 | tf_op jit(solution)/shard_map/ppermute | solution.py:212
  126.4 12.3 %collective-permute-start.42 = (f32[2,4,16,128]{3,2,1,0:T(8,128)S(1)}, f32[2,4,16,128]{3,2,1,0:T(8,128)S(1)}, u32[]{:S(2)}, u32[]{:S(2)}) collective-permute-start(f32[2,4,16,128]{3,2,1,0:T(8,128)S(1)} %get-tuple-element.215), channel_id=1, source_target_pairs={{0,4},{1,6},{2,7},{3,5},{4,0},{5,2},{6,3},{7,1},{8,12},{9,14},{10,... | collective-permute-start | bytes 196616 | tf_op jit(solution)/shard_map/ppermute | solution.py:212
  127.7 13.0 %collective-permute-start.43 = (f32[2,4,16,128]{3,2,1,0:T(8,128)S(1)}, f32[2,4,16,128]{3,2,1,0:T(8,128)S(1)}, u32[]{:S(2)}, u32[]{:S(2)}) collective-permute-start(f32[2,4,16,128]{3,2,1,0:T(8,128)S(1)} %get-tuple-element.216), channel_id=1, source_target_pairs={{0,6},{1,4},{2,5},{3,7},{4,2},{5,0},{6,1},{7,3},{8,14},{9,12},{10,... | collective-permute-start | bytes 196616 | tf_op jit(solution)/shard_map/ppermute | solution.py:212
  131.8 16.4 %collective-permute-start.46 = (f32[8,32,128]{2,1,0:T(8,128)S(1)}, f32[8,32,128]{2,1,0:T(8,128)S(1)}, u32[]{:S(2)}, u32[]{:S(2)}) collective-permute-start(f32[8,32,128]{2,1,0:T(8,128)S(1)} %get-tuple-element.226), channel_id=1, source_target_pairs={{0,12},{1,14},{2,15},{3,13},{4,8},{5,10},{6,11},{7,9},{8,4},{9,6},... | collective-permute-start | bytes 393224 | tf_op jit(solution)/shard_map/ppermute | solution.py:212
  135.0 13.4 %collective-permute-start.47 = (f32[8,32,128]{2,1,0:T(8,128)S(1)}, f32[8,32,128]{2,1,0:T(8,128)S(1)}, u32[]{:S(2)}, u32[]{:S(2)}) collective-permute-start(f32[8,32,128]{2,1,0:T(8,128)S(1)} %get-tuple-element.227), channel_id=1, source_target_pairs={{0,14},{1,12},{2,13},{3,15},{4,10},{5,8},{6,9},{7,11},{8,6},{9,4},... | collective-permute-start | bytes 393224 | tf_op jit(solution)/shard_map/ppermute | solution.py:212
  138.8 16.0 %collective-permute-start.48 = (f32[8,32,128]{2,1,0:T(8,128)S(1)}, f32[8,32,128]{2,1,0:T(8,128)S(1)}, u32[]{:S(2)}, u32[]{:S(2)}) collective-permute-start(f32[8,32,128]{2,1,0:T(8,128)S(1)} %get-tuple-element.228), channel_id=1, source_target_pairs={{0,8},{1,10},{2,11},{3,9},{4,12},{5,14},{6,15},{7,13},{8,0},{9,2},... | collective-permute-start | bytes 393224 | tf_op jit(solution)/shard_map/ppermute | solution.py:212
  138.8 5.4 %collective-permute-start.44 = (f32[2,4,16,128]{3,2,1,0:T(8,128)S(1)}, f32[2,4,16,128]{3,2,1,0:T(8,128)S(1)}, u32[]{:S(2)}, u32[]{:S(2)}) collective-permute-start(f32[2,4,16,128]{3,2,1,0:T(8,128)S(1)} %get-tuple-element.217), channel_id=1, source_target_pairs={{0,0},{1,2},{2,3},{3,1},{4,4},{5,6},{6,7},{7,5},{8,8},{9,10},{10,1... | collective-permute-start | bytes 196616 | tf_op jit(solution)/shard_map/ppermute | solution.py:212
  140.7 6.2 %collective-permute-start.45 = (f32[2,4,16,128]{3,2,1,0:T(8,128)S(1)}, f32[2,4,16,128]{3,2,1,0:T(8,128)S(1)}, u32[]{:S(2)}, u32[]{:S(2)}) collective-permute-start(f32[2,4,16,128]{3,2,1,0:T(8,128)S(1)} %get-tuple-element.218), channel_id=1, source_target_pairs={{0,2},{1,0},{2,1},{3,3},{4,6},{5,4},{6,5},{7,7},{8,10},{9,8},{10,9... | collective-permute-start | bytes 196616 | tf_op jit(solution)/shard_map/ppermute | solution.py:212
  144.2 14.9 %collective-permute-start.49 = (f32[8,32,128]{2,1,0:T(8,128)S(1)}, f32[8,32,128]{2,1,0:T(8,128)S(1)}, u32[]{:S(2)}, u32[]{:S(2)}) collective-permute-start(f32[8,32,128]{2,1,0:T(8,128)S(1)} %get-tuple-element.229), channel_id=1, source_target_pairs={{0,10},{1,8},{2,9},{3,11},{4,14},{5,12},{6,13},{7,15},{8,2},{9,0},... | collective-permute-start | bytes 393224 | tf_op jit(solution)/shard_map/ppermute | solution.py:212
  146.9 12.2 %collective-permute-start.50 = (f32[8,32,128]{2,1,0:T(8,128)S(1)}, f32[8,32,128]{2,1,0:T(8,128)S(1)}, u32[]{:S(2)}, u32[]{:S(2)}) collective-permute-start(f32[8,32,128]{2,1,0:T(8,128)S(1)} %get-tuple-element.230), channel_id=1, source_target_pairs={{0,4},{1,6},{2,7},{3,5},{4,0},{5,2},{6,3},{7,1},{8,12},{9,14},{10,... | collective-permute-start | bytes 393224 | tf_op jit(solution)/shard_map/ppermute | solution.py:212
  148.2 12.2 %collective-permute-start.51 = (f32[8,32,128]{2,1,0:T(8,128)S(1)}, f32[8,32,128]{2,1,0:T(8,128)S(1)}, u32[]{:S(2)}, u32[]{:S(2)}) collective-permute-start(f32[8,32,128]{2,1,0:T(8,128)S(1)} %get-tuple-element.231), channel_id=1, source_target_pairs={{0,6},{1,4},{2,5},{3,7},{4,2},{5,0},{6,1},{7,3},{8,14},{9,12},{10,... | collective-permute-start | bytes 393224 | tf_op jit(solution)/shard_map/ppermute | solution.py:212
  148.4 12.1 %collective-permute-start.52 = (f32[8,32,128]{2,1,0:T(8,128)S(1)}, f32[8,32,128]{2,1,0:T(8,128)S(1)}, u32[]{:S(2)}, u32[]{:S(2)}) collective-permute-start(f32[8,32,128]{2,1,0:T(8,128)S(1)} %get-tuple-element.232), channel_id=1, source_target_pairs={{0,0},{1,2},{2,3},{3,1},{4,4},{5,6},{6,7},{7,5},{8,8},{9,10},{10,1... | collective-permute-start | bytes 393224 | tf_op jit(solution)/shard_map/ppermute | solution.py:212
  154.8 7.9 %collective-permute-start.53 = (f32[8,32,128]{2,1,0:T(8,128)S(1)}, f32[8,32,128]{2,1,0:T(8,128)S(1)}, u32[]{:S(2)}, u32[]{:S(2)}) collective-permute-start(f32[8,32,128]{2,1,0:T(8,128)S(1)} %get-tuple-element.224), channel_id=1, source_target_pairs={{0,2},{1,0},{2,1},{3,3},{4,6},{5,4},{6,5},{7,7},{8,10},{9,8},{10,9... | collective-permute-start | bytes 393224 | tf_op jit(solution)/shard_map/ppermute | solution.py:212
  (37 other events, 253.5 us)
